TPU v7x, 32 devices: a whole 2x2x4 slice. The times are simulated.
32 devices in a mesh: wide: 8 (over z, core), narrow: 4 (over y, x).
Axes of the slice: x: 2, y: 2, z: 4, core: 2. Of those that a mesh axis runs over, the one named last changes fastest.
Arguments:
- density: float32 [2, 1, 4096, 4096], P(None, None, 'narrow', 'wide'), may hold values from -6 to 6
- plane_wave: int32 [1], replicated, may hold values from 1 to 4
Outputs:
- potential: float32 [2, 1, 4096, 4096], P(None, None, 'narrow', 'wide')
All inputs are finite; a program needn't handle non-finite values.
Results may differ from a plain program's by a relative error of at most 0.000073.
Values sent between devices are 32-bit elements; how exact they have to be, the bound alone decides.
No kernel may reach another device: no remote copies, remote signals or barrier semaphores. Data moves between devices by JAX's collectives and lax.ppermute only.
A program may use at most 128 MiB of HBM per device.

v0:
```python
import math

import jax
import jax.numpy as jnp
from jax import lax
from jax.sharding import PartitionSpec as P

SCREEN = 1024
AMP = 2048


HIGHEST = lax.Precision.HIGHEST


def partner_2(value, axis, distance):
    mask = 2**distance
    pairs = [(source, source ^ mask) for source in range(lax.axis_size(axis))]
    return lax.ppermute(value, axis, pairs)


def apply_matrix(matrix, values, along):
    letters = "abcdefgh"[: values.ndim]
    target = letters[:along] + "z" + letters[along + 1 :]
    spec = "z" + letters[along] + "," + letters + "->" + target
    return jnp.einsum(spec, matrix, values, precision=HIGHEST)


def dft_tables(length):
    index = jnp.arange(length, dtype=jnp.int32)
    phase = index[:, None] * index[None, :] % length
    phase_angle = phase.astype(jnp.float32) * (2.0 * math.pi / length)
    return (jnp.cos(phase_angle), jnp.sin(phase_angle))


def complex_matrix(cosine, sine_table, real_part, imag_part, along, orient):
    cos_real = apply_matrix(cosine, real_part, along)
    sin_real = apply_matrix(sine_table, real_part, along)
    cos_imag = apply_matrix(cosine, imag_part, along)
    sin_imag = apply_matrix(sine_table, imag_part, along)
    return (cos_real + orient * sin_imag, cos_imag - orient * sin_real)


def rotate(real_part, imag_part, phase_angle, orient):
    cosine = jnp.cos(phase_angle)
    sine_value = jnp.sin(phase_angle)
    return (
        cosine * real_part + orient * sine_value * imag_part,
        cosine * imag_part - orient * sine_value * real_part,
    )


def direct_dft(field, along, orient):
    cosine, sine_table = dft_tables(field.shape[along + 1])
    real_part, imag_part = complex_matrix(cosine, sine_table, field[0], field[1], along, orient)
    return jnp.stack([real_part, imag_part])


def long_dft(field, along, orient):
    real_part, imag_part = (field[0], field[1])
    shape = real_part.shape
    length = shape[along]
    bit_count = length.bit_length() - 1
    first = 2 ** (bit_count // 2)
    second = length // first
    split = shape[:along] + (first, second) + shape[along + 1 :]
    real_part = real_part.reshape(split)
    imag_part = imag_part.reshape(split)
    cos_first, sin_first = dft_tables(first)
    real_part, imag_part = complex_matrix(cos_first, sin_first, real_part, imag_part, along, orient)
    outer = jnp.arange(first, dtype=jnp.int32)[:, None]
    inner = jnp.arange(second, dtype=jnp.int32)[None, :]
    phase = (outer * inner % length).astype(jnp.float32) * (2.0 * math.pi / length)
    phase = phase.reshape((first, second) + (1,) * (len(split) - along - 2))
    real_part, imag_part = rotate(real_part, imag_part, phase, orient)
    cos_second, sin_second = dft_tables(second)
    real_part, imag_part = complex_matrix(
        cos_second, sin_second, real_part, imag_part, along + 1, orient
    )
    real_part = jnp.swapaxes(real_part, along, along + 1).reshape(shape)
    imag_part = jnp.swapaxes(imag_part, along, along + 1).reshape(shape)
    return jnp.stack([real_part, imag_part])


def reversed_index(device, bit_count):
    result = jnp.int32(0)
    for level in range(bit_count):
        result = result + device // (1 << level) % 2 * (1 << bit_count - 1 - level)
    return result


def butterfly_forward(field, device, bit_count):
    for level in reversed(range(bit_count)):
        half_size = 1 << level
        partner = partner_2(field, "narrow", level)
        upper = device // half_size % 2
        phase_angle = (device % half_size).astype(jnp.float32) * (math.pi / half_size)
        summed = field + partner
        differ = partner - field
        real_part, imag_part = rotate(differ[0], differ[1], phase_angle, 1.0)
        field = jnp.where(upper == 0, summed, jnp.stack([real_part, imag_part]))
    return field


def butterfly_inverse(field, device, bit_count):
    for level in range(bit_count):
        half_size = 1 << level
        partner = partner_2(field, "narrow", level)
        upper = device // half_size % 2
        phase_angle = (device % half_size).astype(jnp.float32) * (math.pi / half_size)
        chosen = jnp.where(upper == 0, partner, field)
        kept = jnp.where(upper == 0, field, partner)
        real_part, imag_part = rotate(chosen[0], chosen[1], phase_angle, -1.0)
        turned = jnp.stack([real_part, imag_part])
        field = jnp.where(upper == 0, kept + turned, kept - turned)
    return field


def green_values(plane_wave, wave_z, total_z, total_x):
    signed_z = jnp.where(wave_z < total_z // 2, wave_z, wave_z - total_z)
    wave_x = jnp.arange(total_x, dtype=jnp.int32)
    signed_x = jnp.where(wave_x < total_x // 2, wave_x, wave_x - total_x)
    square = (
        signed_z[None, :, None] ** 2 + plane_wave[:, None, None] ** 2 + signed_x[None, None, :] ** 2
    )
    square = square.astype(jnp.float32)
    green = 1.0 / (1.0 + square / float(SCREEN * SCREEN)) + float(AMP) / (square + 1.0)
    return green * (1.0 / (total_x * total_z))


def into_pencils(field):
    return lax.all_to_all(field, "wide", split_axis=2, concat_axis=3, tiled=True)


def out_of_pencils(pencils):
    return lax.all_to_all(pencils, "wide", split_axis=3, concat_axis=2, tiled=True)


def x_filter(pencils, plane_wave, wave_local, total_z):
    pencils = long_dft(pencils, 2, 1.0)
    total_x = pencils.shape[3]
    pencils = pencils * green_values(plane_wave, wave_local, total_z, total_x)[None]
    return long_dft(pencils, 2, -1.0)


def shards(density, plane_wave):
    size_narrow = lax.axis_size("narrow")
    bit_count = size_narrow.bit_length() - 1
    device = lax.axis_index("narrow")
    size_wide = lax.axis_size("wide")
    wide_index = lax.axis_index("wide")
    z_local = density.shape[2]
    total_z = z_local * size_narrow
    field = density
    offsets = jnp.arange(z_local, dtype=jnp.int32)
    per_device = z_local // size_wide
    field = butterfly_forward(field, device, bit_count)
    low_wave = reversed_index(device, bit_count)
    phase = (offsets * low_wave % total_z).astype(jnp.float32) * (2.0 * math.pi / total_z)
    phase = phase[:, None]
    real_part, imag_part = rotate(field[0], field[1], phase, 1.0)
    field = direct_dft(jnp.stack([real_part, imag_part]), 1, 1.0)
    wave_table = low_wave + size_narrow * offsets
    pencils = into_pencils(field)
    wave_local = lax.dynamic_slice_in_dim(wave_table, wide_index * per_device, per_device)
    pencils = x_filter(pencils, plane_wave, wave_local, total_z)
    field = out_of_pencils(pencils)
    field = direct_dft(field, 1, -1.0)
    real_part, imag_part = rotate(field[0], field[1], phase, -1.0)
    field = butterfly_inverse(jnp.stack([real_part, imag_part]), device, bit_count)
    return field


def solution(mesh):
    in_specs = (P(None, None, "narrow", "wide"), P())
    out_specs = P(None, None, "narrow", "wide")
    return jax.shard_map(shards, mesh=mesh, in_specs=in_specs, out_specs=out_specs, check_vma=False)
```

profile of v0, /device:TPU:0, one launch (start us, length us, event | category | flops | bytes accessed | tf_op | source)
XLA Modules:
  0.0 952.3 jit_solution(6813250648060458960)
XLA Ops:
  0.0 5.3 copy.78
  5.3 3.0 collective-permute-start
  8.5 90.7 %collective-permute-done = f32[2,1,1024,512]{2,3,1,0:T(8,128)} collective-permute-done((f32[2,1,1024,512]{2,3,1,0:T(8,128)}, f32[2,1,1024,512]{2,3,1,0:T(8,128)}, u32[]{:S(2)}, u32[]{:S(2)}) %collective-permute-start) | collective-permute-done | bytes 4194336 | tf_op jit(solution)/shard_map/ppermute | solution.py:18
  99.2 4.4 sub.119
  104.2 1.6 copy-done.4
  105.8 5.7 maximum_select_fusion
  111.5 1.7 collective-permute-start.1
  113.3 90.3 %collective-permute-done.1 = f32[2,1,1024,512]{2,3,1,0:T(8,128)} collective-permute-done((f32[2,1,1024,512]{2,3,1,0:T(8,128)}, f32[2,1,1024,512]{2,3,1,0:T(8,128)}, u32[]{:S(2)}, u32[]{:S(2)}) %collective-permute-start.1) | collective-permute-done | bytes 4194336 | tf_op jit(solution)/shard_map/ppermute | solution.py:18
  203.6 4.4 sub.121
  208.5 5.0 maximum_select_fusion.1
  213.4 23.5 %fusion.32 = f32[512,1024]{1,0:T(8,128)S(1)} fusion(f32[2,1,1024,512]{2,3,1,0:T(8,128)S(1)} %maximum_select_fusion.1, f32[1024]{0:T(1024)S(1)} %get-tuple-element.25, f32[1024]{0:T(1024)S(1)} %get-tuple-element.26), kind=kOutput, calls=%fused_computation.69 | convolution fusion | flops 6458703872 | bytes 6299648 | tf_op jit(solution)/shard_map/zb,abc->azc/dot_general | solution.py:25
  237.0 23.7 %fusion.34 = f32[512,1024]{1,0:T(8,128)S(1)} fusion(f32[2,1,1024,512]{2,3,1,0:T(8,128)S(1)} %maximum_select_fusion.1, f32[1024]{0:T(1024)S(1)} %get-tuple-element.25, f32[1024]{0:T(1024)S(1)} %get-tuple-element.26), kind=kOutput, calls=%fused_computation.70 | convolution fusion | flops 6458703872 | bytes 6299648 | tf_op jit(solution)/shard_map/zb,abc->azc/dot_general | solution.py:25
  260.7 23.3 %subtract_bitcast_fusion.2 = f32[1,1,1024,512]{2,3,1,0:T(8,128)S(1)} fusion(f32[512,1024]{1,0:T(8,128)S(1)} %fusion.32, f32[2,1,1024,512]{2,3,1,0:T(8,128)S(1)} %maximum_select_fusion.1, f32[1024]{0:T(1024)S(1)} %get-tuple-element.25, f32[1024]{0:T(1024)S(1)} %get-tuple-element.26), kind=kOutput, calls=%fused_computation.58 | convolution fusion | flops 6459228160 | bytes 8396800 | tf_op jit(solution)/shard_map/zb,abc->azc/dot_general | solution.py:25
  284.0 23.4 %add_bitcast_fusion.2 = f32[1,1,1024,512]{2,3,1,0:T(8,128)S(1)} fusion(f32[512,1024]{1,0:T(8,128)S(1)} %fusion.34, f32[2,1,1024,512]{2,3,1,0:T(8,128)S(1)} %maximum_select_fusion.1, f32[1024]{0:T(1024)S(1)} %get-tuple-element.25, f32[1024]{0:T(1024)S(1)} %get-tuple-element.26), kind=kOutput, calls=%fused_computation.59 | convolution fusion | flops 6459228160 | bytes 8396800 | tf_op jit(solution)/shard_map/zb,abc->azc/dot_general | solution.py:25
  307.4 2.3 pad_maximum_fusion
  309.7 11.0 %copy.80 = f32[2,1,1024,512]{3,1,0,2:T(1,128)} copy(f32[2,1,1024,512]{2,3,1,0:T(8,128)} %pad_maximum_fusion) | data formatting | bytes 8388608 | tf_op jit(solution)/shard_map/stack | solution.py:55
  320.7 5.2 all-to-all-start
  327.4 3.0 add_multiply_fusion
  330.4 89.6 %all-to-all-done = f32[2,1,1024,512]{3,1,0,2:T(1,128)} async-done(((f32[2,1,1024,512]{3,1,0,2:T(1,128)}), f32[2,1,1024,512]{3,1,0,2:T(1,128)}, u32[]{:S(2)}, u32[]{:S(2)}) %all-to-all-start) | async-done | bytes 4194336 | tf_op jit(solution)/shard_map/all_to_all | solution.py:131
  420.0 3.0 copy.81
  423.0 2.8 fusion.250
  425.8 1.9 copy.84
  427.7 4.7 fusion.60
  432.4 4.6 fusion.62
  437.0 2.1 copy.82
  439.1 5.1 fusion.68
  444.3 4.5 fusion.15
  448.8 3.3 fusion.52
  452.1 3.5 fusion.54
  455.7 3.3 add_bitcast_fusion.1
  459.0 3.4 subtract_bitcast_fusion.1
  462.4 1.2 copy.94
  463.6 1.2 copy.91
  465.8 3.7 fusion.44
  469.6 3.3 fusion.46
  472.9 3.5 multiply_subtract_fusion.3
  476.4 4.7 fusion.11
  481.1 3.3 fusion.36
  484.4 3.3 fusion.38
  487.8 3.4 add_bitcast_fusion
  491.2 3.9 subtract_bitcast_fusion
  495.1 1.2 copy.105
  496.4 1.2 copy.102
  497.9 19.2 %copy.106 = f32[2,1,128,4096]{2,1,0,3:T(1,128)} copy(f32[2,1,128,4096]{2,3,1,0:T(8,128)S(1)} %pad_maximum_fusion.1) | data formatting | bytes 8388608 | tf_op jit(solution)/shard_map/stack | solution.py:81
  517.0 4.6 all-to-all-start.1
  521.6 94.0 %all-to-all-done.1 = f32[2,1,128,4096]{2,1,0,3:T(1,128)} async-done(((f32[2,1,128,4096]{2,1,0,3:T(1,128)}), f32[2,1,128,4096]{2,1,0,3:T(1,128)}, u32[]{:S(2)}, u32[]{:S(2)}) %all-to-all-start.1) | async-done | bytes 4194336 | tf_op jit(solution)/shard_map/all_to_all | solution.py:135
  615.6 2.5 copy.107
  618.1 1.7 fusion.248
  619.7 2.9 copy.108
  622.6 30.7 %fusion.22 = f32[512,1024]{1,0:T(8,128)} fusion(f32[1024,512]{1,0:T(8,128)} %bitcast.201), kind=kOutput, calls=%fused_computation.64 | convolution fusion | flops 6457131008 | bytes 4194304 | tf_op jit(solution)/shard_map/zb,abc->azc/dot_general | solution.py:25
  653.3 1.8 copy.109
  655.1 30.7 %fusion.20 = f32[512,1024]{1,0:T(8,128)S(1)} fusion(f32[1024,512]{1,0:T(8,128)} %bitcast.199), kind=kOutput, calls=%fused_computation.63 | convolution fusion | flops 6457131008 | bytes 4194304 | tf_op jit(solution)/shard_map/zb,abc->azc/dot_general | solution.py:25
  685.9 29.3 %multiply_subtract_fusion.2 = f32[512,1024]{1,0:T(8,128)S(1)} fusion(f32[512,1024]{1,0:T(8,128)S(1)} %fusion.20, f32[1024,512]{1,0:T(8,128)S(1)} %bitcast.202), kind=kOutput, calls=%fused_computation.49 | convolution fusion | flops 6458179584 | bytes 6291456 | tf_op jit(solution)/shard_map/zb,abc->azc/dot_general | solution.py:25
  715.2 29.5 %fusion.7 = (f32[1,1,1024,512]{2,3,1,0:T(8,128)S(1)}, f32[1,1,1024,512]{2,3,1,0:T(8,128)S(1)}) fusion(f32[512,1024]{1,0:T(8,128)S(1)} %multiply_subtract_fusion.2, f32[1024]{0:T(1024)S(1)} %broadcast_multiply_fusion.1, f32[1024]{0:T(1024)S(1)} %get-tuple-element.26, f32[512,1024]{1,0:T(8,128)S(1)} %copy-done.13, f32[1024,512]{1,0:T(8,128)S(1)} %bitcast.200), kind=kOutput, calls=%fused_computation.24 | convolution fusion | flops 6461325312 | bytes 10493952 | tf_op jit(solution)/shard_map/zb,abc->azc/dot_general | solution.py:25
  745.2 1.6 collective-permute-start.2
  746.7 90.6 %collective-permute-done.2 = f32[2,1,1024,512]{2,3,1,0:T(8,128)S(1)} collective-permute-done((f32[2,1,1024,512]{2,3,1,0:T(8,128)S(1)}, f32[2,1,1024,512]{2,3,1,0:T(8,128)S(1)}, u32[]{:S(2)}, u32[]{:S(2)}) %collective-permute-start.2) | collective-permute-done | bytes 4194336 | tf_op jit(solution)/shard_map/ppermute | solution.py:18
  837.4 1.1 broadcast_select_fusion
  839.9 2.8 subtract_select_fusion.1
  842.7 1.5 collective-permute-start.3
  844.2 90.0 %collective-permute-done.3 = f32[2,1,1024,512]{2,3,1,0:T(8,128)} collective-permute-done((f32[2,1,1024,512]{2,3,1,0:T(8,128)}, f32[2,1,1024,512]{2,3,1,0:T(8,128)}, u32[]{:S(2)}, u32[]{:S(2)}) %collective-permute-start.3) | collective-permute-done | bytes 4194336 | tf_op jit(solution)/shard_map/ppermute | solution.py:18
  934.2 5.1 broadcast_select_fusion.1
  940.3 1.2 copy-done.1
  942.8 4.0 subtract_select_fusion
  946.8 5.4 copy.110
  (45 shorter events, 7.3 us)
Async XLA Ops:
  5.3 93.9 %collective-permute-start = (f32[2,1,1024,512]{2,3,1,0:T(8,128)}, f32[2,1,1024,512]{2,3,1,0:T(8,128)}, u32[]{:S(2)}, u32[]{:S(2)}) collective-permute-start(f32[2,1,1024,512]{2,3,1,0:T(8,128)} %copy.78), channel_id=1, source_target_pairs={{0,2},{1,3},{2,0},{3,1},{4,6},{5,7},{6,4},{7,5},{8,10},{9,11},{10,... | collective-permute-start | bytes 12582920 | tf_op jit(solution)/shard_map/ppermute | solution.py:18
  103.6 2.2 copy-start.4
  111.5 92.1 %collective-permute-start.1 = (f32[2,1,1024,512]{2,3,1,0:T(8,128)}, f32[2,1,1024,512]{2,3,1,0:T(8,128)}, u32[]{:S(2)}, u32[]{:S(2)}) collective-permute-start(f32[2,1,1024,512]{2,3,1,0:T(8,128)} %maximum_select_fusion), channel_id=1, source_target_pairs={{0,1},{1,0},{2,3},{3,2},{4,5},{5,4},{6,7},{7,6},{8,9},{9,8},{10,11... | collective-permute-start | bytes 12582920 | tf_op jit(solution)/shard_map/ppermute | solution.py:18
  320.7 99.3 %all-to-all-start = ((f32[2,1,1024,512]{3,1,0,2:T(1,128)}), f32[2,1,1024,512]{3,1,0,2:T(1,128)}, u32[]{:S(2)}, u32[]{:S(2)}) async-start(f32[2,1,1024,512]{3,1,0,2:T(1,128)} %copy.80), calls=%async_computation | async-start | bytes 8388608 | tf_op jit(solution)/shard_map/all_to_all | solution.py:131
  439.1 5.1 copy-start.10
  463.6 1.6 copy-start.9
  517.0 98.6 %all-to-all-start.1 = ((f32[2,1,128,4096]{2,1,0,3:T(1,128)}), f32[2,1,128,4096]{2,1,0,3:T(1,128)}, u32[]{:S(2)}, u32[]{:S(2)}) async-start(f32[2,1,128,4096]{2,1,0,3:T(1,128)} %copy.106), calls=%async_computation.1 | async-start | bytes 8388608 | tf_op jit(solution)/shard_map/all_to_all | solution.py:135
  655.1 30.7 %copy-start.12 = (f32[1,1,8,128,512]{4,3,2,1,0:T(8,128)S(1)}, f32[1,1,8,128,512]{4,3,2,1,0:T(8,128)}, u32[]{:S(2)}) copy-start(f32[1,1,8,128,512]{4,3,2,1,0:T(8,128)} %copy.108) | copy-start | bytes 6291460
  685.9 29.4 %copy-start.11 = (f32[1,1,8,128,512]{4,3,2,1,0:T(8,128)S(1)}, f32[1,1,8,128,512]{4,3,2,1,0:T(8,128)}, u32[]{:S(2)}) copy-start(f32[1,1,8,128,512]{4,3,2,1,0:T(8,128)} %copy.109) | copy-start | bytes 6291460
  685.9 29.3 %copy-start.13 = (f32[512,1024]{1,0:T(8,128)S(1)}, f32[512,1024]{1,0:T(8,128)}, u32[]{:S(2)}) copy-start(f32[512,1024]{1,0:T(8,128)} %fusion.22) | copy-start | bytes 6291460
  744.7 94.3 %copy-start.2 = (f32[1,1,1024,512]{2,3,1,0:T(8,128)}, f32[1,1,1024,512]{2,3,1,0:T(8,128)S(1)}, u32[]{:S(2)}) copy-start(f32[1,1,1024,512]{2,3,1,0:T(8,128)S(1)} %get-tuple-element.10) | copy-start | bytes 6291460
  745.2 92.2 %collective-permute-start.2 = (f32[2,1,1024,512]{2,3,1,0:T(8,128)S(1)}, f32[2,1,1024,512]{2,3,1,0:T(8,128)S(1)}, u32[]{:S(2)}, u32[]{:S(2)}) collective-permute-start(f32[2,1,1024,512]{2,3,1,0:T(8,128)S(1)} %pad_maximum_fusion.2), channel_id=1, source_target_pairs={{0,1},{1,0},{2,3},{3,2},{4,5},{5,4},{6,7},{7,6},{8,9},{9,8},{10,11... | collective-permute-start | bytes 12582920 | tf_op jit(solution)/shard_map/ppermute | solution.py:18
  837.4 2.5 copy-start
  839.0 3.6 copy-start.5
  839.0 3.6 copy-start.7
  842.7 91.5 %collective-permute-start.3 = (f32[2,1,1024,512]{2,3,1,0:T(8,128)}, f32[2,1,1024,512]{2,3,1,0:T(8,128)}, u32[]{:S(2)}, u32[]{:S(2)}) collective-permute-start(f32[2,1,1024,512]{2,3,1,0:T(8,128)} %subtract_select_fusion.1), channel_id=1, source_target_pairs={{0,2},{1,3},{2,0},{3,1},{4,6},{5,7},{6,4},{7,5},{8,10},{9,11},{10,... | collective-permute-start | bytes 12582920 | tf_op jit(solution)/shard_map/ppermute | solution.py:18
  934.2 6.1 copy-start.8
  939.3 2.2 copy-start.1
  939.4 2.9 copy-start.3
  939.4 3.5 copy-start.6
where the time goes:
time: 959 us; the launch traced here: 952 us
  waiting for transfers between devices  545 us (57%)
  matrix products  276 us (29%)
  local copies, waits for them, and re-layouts  70.1 us (7%)
  other arithmetic  42.1 us (4%)
  starting transfers between devices  17.6 us (2%)
    ppermute x4, waiting for transfers between devices, partner_2(): return lax.ppermute(value, axis, pairs)  362 us
    dot_general x24, matrix products, apply_matrix(): return jnp.einsum(spec, matrix, values, precision=HIGHEST)  276 us
    all_to_all x1, waiting for transfers between devices, out_of_pencils(): lax.all_to_all(pencils, 'wide', split_axis=3, concat_axis=2, tiled=True)  94 us
    all_to_all x1, waiting for transfers between devices, into_pencils(): lax.all_to_all(field, 'wide', split_axis=2, concat_axis=3, tiled=True)  89.6 us
  transfers between devices with their start and end apart: 6, of which 6 were waited for; matrix products, arithmetic and copies ran while one was open for 0% of the time, Pallas kernels for 0%

commit v1 on v0

v1 whole, which is shorter than its diff:
```python
import functools
import math

import jax
import jax.numpy as jnp
import numpy as np
from jax import lax
from jax.experimental import pallas as pl
from jax.experimental.pallas import tpu as pltpu
from jax.sharding import PartitionSpec as P

SCREEN = 1024
AMP = 2048
LANES = 128
VMEM_LIMIT = 48 * 1024 * 1024


def split_bf16(value):
    high = np.asarray(value, np.float64).astype(np.float32).astype(jnp.bfloat16)
    low = (value - high.astype(np.float64)).astype(np.float32).astype(jnp.bfloat16)
    return high, low


def dft_matrix(length, orient, left):
    index = np.arange(length)
    angle = 2.0 * np.pi * ((index[:, None] * index[None, :]) % length) / length
    cosine, sine = np.cos(angle), orient * np.sin(angle)
    if left:
        whole = np.block([[cosine, -sine], [sine, cosine]])
    else:
        whole = np.block([[cosine, sine], [-sine, cosine]])
    high, low = split_bf16(whole)
    return np.stack([high, low])


def turn(numerator, length):
    angle = (numerator % length).astype(jnp.float32) * (2.0 * math.pi / length)
    return jnp.cos(angle), -jnp.sin(angle)


def c_add(a, b):
    return (a[0] + b[0], a[1] + b[1])


def c_sub(a, b):
    return (a[0] - b[0], a[1] - b[1])


def c_mul(a, b):
    return (a[0] * b[0] - a[1] * b[1], a[0] * b[1] + a[1] * b[0])


def c_const(a, numerator, length, orient):
    numerator = (orient * numerator) % length
    if numerator == 0:
        return a
    if 2 * numerator == length:
        return (-a[0], -a[1])
    if 4 * numerator == length:
        return (-a[1], a[0])
    if 4 * numerator == 3 * length:
        return (a[1], -a[0])
    angle = 2.0 * math.pi * numerator / length
    cosine, sine = math.cos(angle), math.sin(angle)
    if 8 * numerator % length == 0:
        root = math.sqrt(0.5)
        total, differ = (a[0] + a[1]) * root, (a[0] - a[1]) * root
        if cosine > 0 and sine > 0:
            return (differ, total)
        if cosine > 0:
            return (total, -differ)
        if sine > 0:
            return (-total, differ)
        return (-differ, -total)
    return (a[0] * cosine - a[1] * sine, a[0] * sine + a[1] * cosine)


def small_dft(values, orient):
    count = len(values)
    if count == 1:
        return values
    half = count // 2
    upper = [c_add(values[i], values[i + half]) for i in range(half)]
    lower = [
        c_const(c_sub(values[i], values[i + half]), i, count, orient) for i in range(half)
    ]
    even, odd = small_dft(upper, orient), small_dft(lower, orient)
    result = []
    for i in range(half):
        result += [even[i], odd[i]]
    return result


def dot3(high, low, value, left):
    value_high = value.astype(jnp.bfloat16)
    value_low = (value - value_high.astype(jnp.float32)).astype(jnp.bfloat16)
    dot = functools.partial(jnp.dot, preferred_element_type=jnp.float32)
    if left:
        return dot(high, value_high) + (dot(high, value_low) + dot(low, value_high))
    return dot(value_high, high) + (dot(value_low, high) + dot(value_high, low))


def z_forward_kernel(terms, parts, slots, rows, coef_ref, matrix_ref, turn_ref, *refs):
    inputs = refs[: terms * parts]
    outputs = refs[terms * parts : terms * parts + slots]
    held = refs[-1]
    per_part = slots // parts
    tile = min(rows, 8)

    def step(index, carry):
        row = pl.multiple_of(index * tile, tile)
        values = []
        for h in range(slots):
            part, inner = divmod(h, per_part)
            total = None
            for term in range(terms):
                ref = inputs[part * terms + term]
                place = pl.ds(inner * rows + row, tile)
                value = (ref[0, place, :], ref[1, place, :])
                scale = (coef_ref[h, 2 * term], coef_ref[h, 2 * term + 1])
                product = c_mul(value, scale)
                total = product if total is None else c_add(total, product)
            values.append(total)
        values = small_dft(values, 1)
        for k in range(slots):
            twiddle = (
                turn_ref[k, 0, pl.ds(row, tile), :],
                turn_ref[k, 1, pl.ds(row, tile), :],
            )
            real_part, imag_part = c_mul(values[k], twiddle)
            held[pl.ds(row, tile), k * LANES : (k + 1) * LANES] = real_part
            held[pl.ds(rows + row, tile), k * LANES : (k + 1) * LANES] = imag_part
        return carry

    lax.fori_loop(0, rows // tile, step, 0)
    result = dot3(matrix_ref[0], matrix_ref[1], held[...], True)
    for k in range(slots):
        outputs[k][0] = result[:rows, k * LANES : (k + 1) * LANES]
        outputs[k][1] = result[rows:, k * LANES : (k + 1) * LANES]


def z_forward(parts, coef, turns, slots, rows):
    terms = len(parts[0])
    flat = [array for part in parts for array in part]
    matrix = jnp.asarray(dft_matrix(rows, -1, True))
    vmem = pl.BlockSpec(memory_space=pltpu.VMEM)
    return pl.pallas_call(
        functools.partial(z_forward_kernel, terms, len(parts), slots, rows),
        out_shape=[jax.ShapeDtypeStruct((2, rows, LANES), jnp.float32)] * slots,
        in_specs=[pl.BlockSpec(memory_space=pltpu.SMEM)] + [vmem] * (2 + len(flat)),
        out_specs=[vmem] * slots,
        scratch_shapes=[pltpu.VMEM((2 * rows, slots * LANES), jnp.float32)],
        compiler_params=pltpu.CompilerParams(vmem_limit_bytes=VMEM_LIMIT),
        cost_estimate=pl.CostEstimate(
            flops=12 * rows * rows * slots * LANES, bytes_accessed=32 * rows * slots * LANES, transcendentals=0
        ),
        name="z_forward",
    )(coef, matrix, turns, *flat)


def z_inverse_kernel(parts, slots, rows, coef_ref, matrix_ref, turn_ref, *refs):
    inputs = refs[:slots]
    outputs = refs[slots : slots + parts]
    held = refs[-1]
    per_part = slots // parts
    tile = min(rows, 8)
    for k in range(slots):
        held[:rows, k * LANES : (k + 1) * LANES] = inputs[k][0]
        held[rows:, k * LANES : (k + 1) * LANES] = inputs[k][1]
    held[...] = dot3(matrix_ref[0], matrix_ref[1], held[...], True)

    def step(index, carry):
        row = pl.multiple_of(index * tile, tile)
        values = []
        for k in range(slots):
            value = (
                held[pl.ds(row, tile), k * LANES : (k + 1) * LANES],
                held[pl.ds(rows + row, tile), k * LANES : (k + 1) * LANES],
            )
            twiddle = (
                turn_ref[k, 0, pl.ds(row, tile), :],
                -turn_ref[k, 1, pl.ds(row, tile), :],
            )
            values.append(c_mul(value, twiddle))
        values = small_dft(values, -1)
        for h in range(slots):
            part, inner = divmod(h, per_part)
            real_part, imag_part = c_mul(values[h], (coef_ref[h, 0], coef_ref[h, 1]))
            outputs[part][0, pl.ds(inner * rows + row, tile), :] = real_part
            outputs[part][1, pl.ds(inner * rows + row, tile), :] = imag_part
        return carry

    lax.fori_loop(0, rows // tile, step, 0)


def z_inverse(blocks, coef, turns, parts):
    slots, rows = len(blocks), blocks[0].shape[1]
    matrix = jnp.asarray(dft_matrix(rows, 1, True))
    vmem = pl.BlockSpec(memory_space=pltpu.VMEM)
    return pl.pallas_call(
        functools.partial(z_inverse_kernel, parts, slots, rows),
        out_shape=[jax.ShapeDtypeStruct((2, slots // parts * rows, LANES), jnp.float32)] * parts,
        in_specs=[pl.BlockSpec(memory_space=pltpu.SMEM)] + [vmem] * (2 + slots),
        out_specs=[vmem] * parts,
        scratch_shapes=[pltpu.VMEM((2 * rows, slots * LANES), jnp.float32)],
        compiler_params=pltpu.CompilerParams(vmem_limit_bytes=VMEM_LIMIT),
        cost_estimate=pl.CostEstimate(
            flops=12 * rows * rows * slots * LANES, bytes_accessed=20 * rows * slots * LANES, transcendentals=0
        ),
        name="z_inverse",
    )(coef, matrix, turns, *blocks)


def x_filter_kernel(slots, chunks, rows, coef_ref, forward_ref, inverse_ref, turn_ref, green_ref, *refs):
    blocks = slots * chunks
    inputs = refs[:blocks]
    outputs = refs[blocks : 2 * blocks]
    held = refs[-1]
    tile = 8

    def before(index, carry):
        row = pl.multiple_of(index * tile, tile)
        place = pl.ds(row, tile)
        columns = []
        for c in range(chunks):
            values = [
                (inputs[c * slots + k][0, place, :], inputs[c * slots + k][1, place, :])
                for k in range(slots)
            ]
            values = small_dft(values, -1)
            columns.append(
                [
                    c_mul(values[a], (coef_ref[a * chunks + c, 0], coef_ref[a * chunks + c, 1]))
                    for a in range(slots)
                ]
            )
        for a in range(slots):
            values = small_dft([columns[c][a] for c in range(chunks)], -1)
            for b in range(chunks):
                mode = a + slots * b
                twiddle = (turn_ref[0, mode : mode + 1, :], turn_ref[1, mode : mode + 1, :])
                real_part, imag_part = c_mul(values[b], twiddle)
                held[mode, place, :LANES] = real_part
                held[mode, place, LANES:] = imag_part
        return carry

    lax.fori_loop(0, rows // tile, before, 0)

    group = max(1, min(blocks, 256 // rows))

    def middle(index, carry):
        mode = pl.multiple_of(index * group, group)
        value = held[pl.ds(mode, group)].reshape(group * rows, 2 * LANES)
        value = dot3(forward_ref[0], forward_ref[1], value, False)
        green = green_ref[pl.ds(mode, group)].reshape(group * rows, LANES)
        value = value * jnp.concatenate([green, green], axis=1)
        value = dot3(inverse_ref[0], inverse_ref[1], value, False)
        held[pl.ds(mode, group)] = value.reshape(group, rows, 2 * LANES)
        return carry

    lax.fori_loop(0, blocks // group, middle, 0)

    def after(index, carry):
        row = pl.multiple_of(index * tile, tile)
        place = pl.ds(row, tile)
        columns = []
        for a in range(slots):
            values = []
            for b in range(chunks):
                mode = a + slots * b
                twiddle = (turn_ref[0, mode : mode + 1, :], -turn_ref[1, mode : mode + 1, :])
                values.append(c_mul((held[mode, place, :LANES], held[mode, place, LANES:]), twiddle))
            columns.append(small_dft(values, 1))
        for c in range(chunks):
            values = [
                c_mul(columns[a][c], (coef_ref[a * chunks + c, 0], -coef_ref[a * chunks + c, 1]))
                for a in range(slots)
            ]
            values = small_dft(values, 1)
            for k in range(slots):
                outputs[c * slots + k][0, place, :] = values[k][0]
                outputs[c * slots + k][1, place, :] = values[k][1]
        return carry

    lax.fori_loop(0, rows // tile, after, 0)


def x_filter(blocks, coef, turns, green, slots, chunks):
    rows = blocks[0].shape[1]
    step = min(rows, 32)
    count = slots * chunks
    forward = jnp.asarray(dft_matrix(LANES, -1, False))
    inverse = jnp.asarray(dft_matrix(LANES, 1, False))
    whole = pl.BlockSpec((2, 2 * LANES, 2 * LANES), lambda i: (0, 0, 0))
    block = pl.BlockSpec((2, step, LANES), lambda i: (0, i, 0))
    return pl.pallas_call(
        functools.partial(x_filter_kernel, slots, chunks, step),
        grid=(rows // step,),
        out_shape=[jax.ShapeDtypeStruct((2, rows, LANES), jnp.float32)] * count,
        in_specs=[
            pl.BlockSpec(memory_space=pltpu.SMEM),
            whole,
            whole,
            pl.BlockSpec((2, count, LANES), lambda i: (0, 0, 0)),
            pl.BlockSpec((count, step, LANES), lambda i: (0, i, 0)),
        ]
        + [block] * count,
        out_specs=[block] * count,
        scratch_shapes=[pltpu.VMEM((count, step, 2 * LANES), jnp.float32)],
        compiler_params=pltpu.CompilerParams(vmem_limit_bytes=VMEM_LIMIT),
        cost_estimate=pl.CostEstimate(
            flops=24 * LANES * LANES * 4 * count * rows, bytes_accessed=20 * count * rows * LANES, transcendentals=0
        ),
        name="x_filter",
    )(coef, forward, inverse, turns, green, *blocks)


def finish_kernel(terms, parts, coef_ref, *refs):
    inputs = refs[: terms * parts]
    out_ref = refs[-1]
    for part in range(parts):
        rows = inputs[part * terms].shape[1]
        total = None
        for term in range(terms):
            ref = inputs[part * terms + term]
            product = c_mul(
                (ref[0], ref[1]), (coef_ref[part, 2 * term], coef_ref[part, 2 * term + 1])
            )
            total = product if total is None else c_add(total, product)
        out_ref[0, part * rows : (part + 1) * rows, :] = total[0]
        out_ref[1, part * rows : (part + 1) * rows, :] = total[1]


def finish(parts, coef, chunk, chunks, so_far):
    terms = len(parts[0])
    flat = [array for part in parts for array in part]
    rows = sum(part[0].shape[1] for part in parts)
    step = 1
    vmem = [pl.BlockSpec(array.shape, lambda i: (0, 0, 0)) for array in flat]
    extra = [] if so_far is None else [so_far]
    return pl.pallas_call(
        functools.partial(finish_kernel, terms, len(parts)),
        grid=(step,),
        out_shape=jax.ShapeDtypeStruct((2, rows, chunks * LANES), jnp.float32),
        in_specs=[pl.BlockSpec(memory_space=pltpu.SMEM)]
        + vmem
        + [pl.BlockSpec(memory_space=pl.ANY)] * len(extra),
        out_specs=pl.BlockSpec((2, rows, LANES), lambda i: (0, 0, chunk)),
        input_output_aliases={1 + len(flat): 0} if extra else {},
        compiler_params=pltpu.CompilerParams(vmem_limit_bytes=VMEM_LIMIT),
        cost_estimate=pl.CostEstimate(
            flops=20 * rows * LANES, bytes_accessed=32 * rows * LANES, transcendentals=0
        ),
        name="finish",
    )(coef, *flat, *extra)


def swap(value, axis, mask):
    pairs = [(source, source ^ mask) for source in range(lax.axis_size(axis))]
    return lax.ppermute(value, axis, pairs)


def shift(value, axis, distance):
    size = lax.axis_size(axis)
    pairs = [(source, (source + distance) % size) for source in range(size)]
    return lax.ppermute(value, axis, pairs)


def mix(array, other, first, second):
    a = c_mul((array[0], array[1]), first)
    b = c_mul((other[0], other[1]), second)
    return jnp.stack(c_add(a, b))


def quarter(target, source, orient):
    step = target * source % 4
    real_part = jnp.where(step == 0, 1.0, jnp.where(step == 2, -1.0, 0.0))
    imag_part = jnp.where(step == 1, -1.0, jnp.where(step == 3, 1.0, 0.0))
    return (real_part, imag_part * orient)


def four_way(array, device, first, orient):
    second = 3 - first
    partner = swap(array, "narrow", first)
    there = device ^ second
    sent = mix(
        array,
        partner,
        quarter(there, device, orient),
        quarter(there, device ^ first, orient),
    )
    received = swap(sent, "narrow", second)
    return [array, partner, received]


def four_way_coef(device, first, orient):
    return [
        quarter(device, device, orient),
        quarter(device, device ^ first, orient),
        (jnp.float32(1.0), jnp.float32(0.0)),
    ]


def reversed_index(device, bit_count):
    result = jnp.int32(0)
    for level in range(bit_count):
        result = result + device // (1 << level) % 2 * (1 << bit_count - 1 - level)
    return result


def rotate(field, phase_angle, orient):
    return jnp.stack(
        c_mul((field[0], field[1]), (jnp.cos(phase_angle), -orient * jnp.sin(phase_angle)))
    )


def butterfly_forward(field, device, bit_count):
    for level in reversed(range(bit_count)):
        half_size = 1 << level
        partner = swap(field, "narrow", half_size)
        upper = device // half_size % 2
        phase_angle = (device % half_size).astype(jnp.float32) * (math.pi / half_size)
        field = jnp.where(upper == 0, field + partner, rotate(partner - field, phase_angle, 1.0))
    return field


def butterfly_inverse(field, device, bit_count):
    for level in range(bit_count):
        half_size = 1 << level
        partner = swap(field, "narrow", half_size)
        upper = device // half_size % 2
        phase_angle = (device % half_size).astype(jnp.float32) * (math.pi / half_size)
        turned = rotate(jnp.where(upper == 0, partner, field), phase_angle, -1.0)
        field = jnp.where(upper == 0, field + turned, partner - turned)
    return field


def green_values(plane_wave, wave_z, modes, total_z, total_x):
    signed_z = jnp.where(wave_z < total_z // 2, wave_z, wave_z - total_z)
    wave_x = jnp.arange(modes)[:, None] + modes * jnp.arange(total_x // modes)[None, :]
    signed_x = jnp.where(wave_x < total_x // 2, wave_x, wave_x - total_x)
    square = signed_z[None, :, None] ** 2 + plane_wave**2 + signed_x[:, None, :] ** 2
    square = square.astype(jnp.float32)
    green = 1.0 / (1.0 + square / float(SCREEN * SCREEN)) + float(AMP) / (square + 1.0)
    return green * (1.0 / (total_x * total_z))


def plane(density, plane_wave):
    narrow, wide = lax.axis_size("narrow"), lax.axis_size("wide")
    bits = narrow.bit_length() - 1
    device, place = lax.axis_index("narrow"), lax.axis_index("wide")
    z_local, x_local = density.shape[1:]
    total_z, total_x = z_local * narrow, x_local * wide
    rows = z_local // wide
    chunks = x_local // LANES
    modes = wide * chunks
    four = narrow == 4
    low_wave = device if four else reversed_index(device, bits)

    slot = jnp.arange(wide, dtype=jnp.int32)
    line = jnp.arange(rows, dtype=jnp.int32)
    lane = jnp.arange(LANES, dtype=jnp.int32)
    block = (place - slot) % wide
    turns = turn(line[None, :] * (low_wave + narrow * block)[:, None], total_z)
    turns = jnp.broadcast_to(jnp.stack(turns, axis=1)[..., None], (wide, 2, rows, LANES))
    head = turn(slot * (low_wave + narrow * place), narrow * wide)
    parts = 2 if four else 1
    inner = jnp.stack([head[0], -head[1]], axis=1)
    if four:
        firsts = [1, 2]
        table = []
        for h in range(wide):
            row = []
            for coef in four_way_coef(device, firsts[h * 2 // wide], 1.0):
                row += list(c_mul(coef, (head[0][h], head[1][h])))
            table.append(jnp.stack(row))
        outer = jnp.stack(table)
        last = jnp.stack(
            [
                jnp.stack([item for pair in four_way_coef(device, first, -1.0) for item in pair])
                for first in firsts
            ]
        )
    else:
        outer = jnp.stack(head, axis=1)
        last = jnp.array([[1.0, 0.0]], jnp.float32)

    digit = jnp.arange(chunks, dtype=jnp.int32)
    x_coef = turn(slot[:, None] * (place * chunks + digit[None, :]), modes)
    x_coef = jnp.stack([value.reshape(-1) for value in x_coef], axis=1)
    mode = jnp.arange(modes, dtype=jnp.int32)
    x_turns = jnp.stack(turn(mode[:, None] * lane[None, :], total_x))
    wave_z = low_wave + narrow * (place + wide * line)
    green = green_values(plane_wave, wave_z, modes, total_z, total_x)

    half = z_local // parts
    received = []
    for c in range(chunks):
        columns = slice(c * LANES, (c + 1) * LANES)
        pieces = [density[:, p * half : (p + 1) * half, columns] for p in range(parts)]
        if four:
            pieces = [four_way(piece, device, first, 1.0) for piece, first in zip(pieces, firsts)]
        else:
            pieces = [[butterfly_forward(piece, device, bits)] for piece in pieces]
        sent = z_forward(pieces, outer, turns, wide, rows)
        received += [sent[0]] + [shift(sent[k], "wide", -k) for k in range(1, wide)]

    filtered = x_filter(received, x_coef, x_turns, green, wide, chunks)

    result = None
    for c in range(chunks):
        sent = filtered[c * wide : (c + 1) * wide]
        blocks = [sent[0]] + [shift(sent[k], "wide", k) for k in range(1, wide)]
        pieces = z_inverse(blocks, inner, turns, parts)
        if four:
            pieces = [four_way(piece, device, first, -1.0) for piece, first in zip(pieces, firsts)]
        else:
            pieces = [[butterfly_inverse(piece, device, bits)] for piece in pieces]
        result = finish(pieces, last, c, chunks, result)
    return result


def shards(density, plane_wave):
    planes = [plane(density[:, y], plane_wave[y]) for y in range(density.shape[1])]
    return jnp.stack(planes, axis=1)


def solution(mesh):
    in_specs = (P(None, None, "narrow", "wide"), P())
    out_specs = P(None, None, "narrow", "wide")
    return jax.shard_map(shards, mesh=mesh, in_specs=in_specs, out_specs=out_specs, check_vma=False)
```

time: 959 us -> 473 us (0.49)
  waiting for transfers between devices: 545 us -> 149 us
  matrix products: 276 us -> 0 us
  starting transfers between devices: 17.6 us -> 135 us
  between operations: 1.47 us -> 60.9 us
  Pallas kernels: 0 us -> 49.8 us
  other arithmetic: 42.1 us -> 21 us
  local copies, waits for them, and re-layouts: 70.1 us -> 54.9 us
    dot_general x24 -> x0, matrix products: 276 us -> none  [apply_matrix(): return jnp.einsum(spec, matrix, values, precision=HIGHEST)]
    ppermute x4 -> x88, waiting for transfers between devices: 362 us -> 149 us  [the longest x32 85.1 us: swap(): return lax.ppermute(value, axis, pairs)]
    all_to_all x2 -> x0, waiting for transfers between devices: 184 us -> none  [the longest x1 94 us: out_of_pencils(): lax.all_to_all(pencils, 'wide', split_axis=3, concat_axis=2, tiled=True)]
    ppermute x4 -> x88, starting transfers between devices: 7.76 us -> 135 us  [the longest x56 91.5 us: shift(): return lax.ppermute(value, axis, pairs)]
    pallas_call x0 -> x13, Pallas kernels: none -> 49.8 us  [the longest x1 17.8 us: x_filter(): pl.pallas_call(functools.partial(x_filter_kernel, slots, chunks, step), g...]
    unnamed x29 -> x226, local copies, waits for them, and re-layouts: 10.7 us -> 48.6 us
    another operation x2 -> x14, local copies, waits for them, and re-layouts: 30.1 us -> 1.05 us  [the longest x8 0.67 us: plane(): table.append(jnp.stack(row))]
    select_n x6 -> x0, other arithmetic: 23.7 us -> none  [the longest x2 10.7 us: butterfly_forward(): field = jnp.where(upper == 0, summed, jnp.stack([real_part, imag_part]))]
  transfers between devices with their start and end apart: 6 -> 88, of which waited for: 6 -> 29; matrix products, arithmetic and copies ran while one was open for 0% -> 5% of each run, Pallas kernels for 0% -> 6%
where the time goes in v1:
time: 473 us; the launch traced here: 471 us
  waiting for transfers between devices  149 us (32%)
  starting transfers between devices  135 us (29%)
  between operations  60.9 us (13%)
  local copies, waits for them, and re-layouts  54.9 us (12%)
  Pallas kernels  49.8 us (11%)
  other arithmetic  21 us (4%)
    ppermute x56, starting transfers between devices, shift(): return lax.ppermute(value, axis, pairs)  91.5 us
    ppermute x32, waiting for transfers between devices, swap(): return lax.ppermute(value, axis, pairs)  85.1 us
    ppermute x56, waiting for transfers between devices, shift(): return lax.ppermute(value, axis, pairs)  64.1 us
    unnamed x226, local copies, waits for them, and re-layouts  48.6 us
    ppermute x32, starting transfers between devices, swap(): return lax.ppermute(value, axis, pairs)  43.8 us
    pallas_call x1, Pallas kernels, x_filter(): pl.pallas_call(functools.partial(x_filter_kernel, slots, chunks, step), g...  17.8 us
    pallas_call x4, Pallas kernels, z_forward(): pl.pallas_call(functools.partial(z_forward_kernel, terms, len(parts), slo...  12.8 us
    pallas_call x4, Pallas kernels, finish(): pl.pallas_call(functools.partial(finish_kernel, terms, len(parts)), grid=...  11 us
  transfers between devices with their start and end apart: 88, of which 29 were waited for; matrix products, arithmetic and copies ran while one was open for 5% of the time, Pallas kernels for 6%

profile of v1, /device:TPU:0, one launch (start us, length us, event | category | flops | bytes accessed | tf_op | source)
XLA Modules:
  0.0 471.0 jit_solution(10544006880765919772)
XLA Ops:
  0.0 3.5 fusion.34
  3.6 3.0 collective-permute-start.35
  8.7 1.9 collective-permute-start.13
  12.2 7.5 %collective-permute-done.35.refs_4_ = f32[2,512,128]{2,1,0:T(8,128)} collective-permute-done((f32[2,512,128]{2,1,0:T(8,128)}, f32[2,512,128]{2,1,0:T(8,128)}, u32[]{:S(2)}, u32[]{:S(2)}) %collective-permute-start.35) | collective-permute-done | bytes 524320 | tf_op jit(solution)/shard_map/ppermute | solution.py:360
  19.7 2.0 collective-permute-start.11
  23.0 7.8 %collective-permute-done.24.refs_4_ = f32[2,512,128]{2,1,0:T(8,128)} collective-permute-done((f32[2,512,128]{2,1,0:T(8,128)S(1)}, f32[2,512,128]{2,1,0:T(8,128)}, u32[]{:S(2)}, u32[]{:S(2)}) %collective-permute-start.24) | collective-permute-done | bytes 524320 | tf_op jit(solution)/shard_map/ppermute | solution.py:360
  30.9 2.1 collective-permute-start.2
  39.7 2.4 collective-permute-done.13.refs_4_
  42.1 2.1 collective-permute-start.34
  47.1 6.2 %collective-permute-done.2.refs_4_ = f32[2,512,128]{2,1,0:T(8,128)S(1)} collective-permute-done((f32[2,512,128]{2,1,0:T(8,128)S(1)}, f32[2,512,128]{2,1,0:T(8,128)S(1)}, u32[]{:S(2)}, u32[]{:S(2)}) %collective-permute-start.2) | collective-permute-done | bytes 524320 | tf_op jit(solution)/shard_map/ppermute | solution.py:360
  53.3 2.1 collective-permute-start.23
  59.7 6.9 %collective-permute-done.36.refs_5_ = f32[2,512,128]{2,1,0:T(8,128)S(1)} collective-permute-done((f32[2,512,128]{2,1,0:T(8,128)S(1)}, f32[2,512,128]{2,1,0:T(8,128)S(1)}, u32[]{:S(2)}, u32[]{:S(2)}) %collective-permute-start.36) | collective-permute-done | bytes 524320 | tf_op jit(solution)/shard_map/ppermute | solution.py:360
  68.4 1.9 collective-permute-start.3
  70.3 7.5 %collective-permute-done.25.refs_5_ = f32[2,512,128]{2,1,0:T(8,128)S(1)} collective-permute-done((f32[2,512,128]{2,1,0:T(8,128)S(1)}, f32[2,512,128]{2,1,0:T(8,128)S(1)}, u32[]{:S(2)}, u32[]{:S(2)}) %collective-permute-start.25) | collective-permute-done | bytes 524320 | tf_op jit(solution)/shard_map/ppermute | solution.py:360
  141.8 3.0 z_forward.7
  146.2 3.4 collective-permute-start.38
  149.7 3.5 z_forward.6
  153.3 2.8 collective-permute-start.40
  156.9 9.4 %collective-permute-start.26 = (f32[2,128,128]{2,1,0:T(8,128)S(1)}, f32[2,128,128]{2,1,0:T(8,128)S(1)}, u32[]{:S(2)}, u32[]{:S(2)}) collective-permute-start(f32[2,128,128]{2,1,0:T(8,128)S(1)} %get-tuple-element.94), channel_id=1, source_target_pairs={{0,28},{4,0},{8,4},{12,8},{16,12},{20,16},{24,20},{28,24},{1,29},{... | collective-permute-start | bytes 393224 | tf_op jit(solution)/shard_map/ppermute | solution.py:366
  166.3 2.1 add_multiply_fusion.green_ref
  168.4 3.1 collective-permute-done.40.refs_28_
  171.5 2.3 collective-permute-done.41.refs_29_
  173.8 9.0 %collective-permute-start.29 = (f32[2,128,128]{2,1,0:T(8,128)}, f32[2,128,128]{2,1,0:T(8,128)}, u32[]{:S(2)}, u32[]{:S(2)}) collective-permute-start(f32[2,128,128]{2,1,0:T(8,128)} %get-tuple-element.97), channel_id=1, source_target_pairs={{0,16},{4,20},{8,24},{12,28},{16,0},{20,4},{24,8},{28,12},{1,17},{... | collective-permute-start | bytes 393224 | tf_op jit(solution)/shard_map/ppermute | solution.py:366
  185.6 2.9 z_forward.5
  189.2 3.0 collective-permute-start.15
  192.1 3.5 collective-permute-done.29.refs_20_
  195.8 3.7 collective-permute-start.18
  199.5 3.3 z_forward.4
  204.6 3.1 collective-permute-start.10
  207.7 10.0 %collective-permute-done.18.refs_12_ = f32[2,128,128]{2,1,0:T(8,128)S(1)} collective-permute-done((f32[2,128,128]{2,1,0:T(8,128)S(1)}, f32[2,128,128]{2,1,0:T(8,128)S(1)}, u32[]{:S(2)}, u32[]{:S(2)}) %collective-permute-start.18) | collective-permute-done | bytes 131104 | tf_op jit(solution)/shard_map/ppermute | solution.py:366
  217.8 2.3 collective-permute-done.19.refs_13_
  224.0 3.5 collective-permute-done.5.refs_2_
  227.6 12.0 %collective-permute-done.7.refs_4_ = f32[2,128,128]{2,1,0:T(8,128)S(1)} collective-permute-done((f32[2,128,128]{2,1,0:T(8,128)}, f32[2,128,128]{2,1,0:T(8,128)S(1)}, u32[]{:S(2)}, u32[]{:S(2)}) %collective-permute-start.7) | collective-permute-done | bytes 131104 | tf_op jit(solution)/shard_map/ppermute | solution.py:366
  246.1 17.8 %x_filter.1 = (f32[2,128,128]{2,1,0:T(8,128)S(1)}, f32[2,128,128]{2,1,0:T(8,128)S(1)}, f32[2,128,128]{2,1,0:T(8,128)S(1)}, f32[2,128,128]{2,1,0:T(8,128)S(1)}, f...) custom-call(f32[32,2]{1,0:T(8,128)S(1)} %copy.31.coef_ref, ...), custom_call_target="tpu_custom_call" | custom-call | flops 6442450944 | bytes 10485760 | tf_op jit(solution)/shard_map/x_filter/pallas_call | solution.py:296
  271.5 2.4 collective-permute-start.80
  273.9 3.0 collective-permute-done.77.refs_1_
  279.0 9.6 %collective-permute-done.79.refs_3_ = f32[2,128,128]{2,1,0:T(8,128)S(1)} collective-permute-done((f32[2,128,128]{2,1,0:T(8,128)S(1)}, f32[2,128,128]{2,1,0:T(8,128)S(1)}, u32[]{:S(2)}, u32[]{:S(2)}) %collective-permute-start.79) | collective-permute-done | bytes 131104 | tf_op jit(solution)/shard_map/ppermute | solution.py:366
  288.7 3.7 collective-permute-start.67
  293.1 2.3 collective-permute-start.68
  296.0 3.3 collective-permute-start.69
  300.0 6.0 %collective-permute-start.70 = (f32[2,128,128]{2,1,0:T(8,128)S(1)}, f32[2,128,128]{2,1,0:T(8,128)S(1)}, u32[]{:S(2)}, u32[]{:S(2)}) collective-permute-start(f32[2,128,128]{2,1,0:T(8,128)S(1)} %get-tuple-element.134), channel_id=1, source_target_pairs={{0,20},{4,24},{8,28},{12,0},{16,4},{20,8},{24,12},{28,16},{1,21},{... | collective-permute-start | bytes 393224 | tf_op jit(solution)/shard_map/ppermute | solution.py:366
  306.0 3.1 collective-permute-start.71
  310.9 5.8 %collective-permute-start.57 = (f32[2,128,128]{2,1,0:T(8,128)}, f32[2,128,128]{2,1,0:T(8,128)S(1)}, u32[]{:S(2)}, u32[]{:S(2)}) collective-permute-start(f32[2,128,128]{2,1,0:T(8,128)} %copy-done.93), channel_id=1, source_target_pairs={{0,12},{4,16},{8,20},{12,24},{16,28},{20,0},{24,4},{28,8},{1,13},{... | collective-permute-start | bytes 393224 | tf_op jit(solution)/shard_map/ppermute | solution.py:366
  319.4 2.5 z_inverse.7
  324.8 4.9 %collective-permute-start.58 = (f32[2,128,128]{2,1,0:T(8,128)S(1)}, f32[2,128,128]{2,1,0:T(8,128)S(1)}, u32[]{:S(2)}, u32[]{:S(2)}) collective-permute-start(f32[2,128,128]{2,1,0:T(8,128)S(1)} %copy-done.92), channel_id=1, source_target_pairs={{0,16},{4,20},{8,24},{12,28},{16,0},{20,4},{24,8},{28,12},{1,17},{... | collective-permute-start | bytes 393224 | tf_op jit(solution)/shard_map/ppermute | solution.py:366
  330.4 1.8 collective-permute-start.60
  332.9 4.8 %collective-permute-done.58.refs_4_ = f32[2,128,128]{2,1,0:T(8,128)S(1)} collective-permute-done((f32[2,128,128]{2,1,0:T(8,128)S(1)}, f32[2,128,128]{2,1,0:T(8,128)S(1)}, u32[]{:S(2)}, u32[]{:S(2)}) %collective-permute-start.58) | collective-permute-done | bytes 131104 | tf_op jit(solution)/shard_map/ppermute | solution.py:366
  339.0 5.8 %collective-permute-start.45 = (f32[2,128,128]{2,1,0:T(8,128)S(1)}, f32[2,128,128]{2,1,0:T(8,128)S(1)}, u32[]{:S(2)}, u32[]{:S(2)}) collective-permute-start(f32[2,128,128]{2,1,0:T(8,128)S(1)} %copy-done.82), channel_id=1, source_target_pairs={{0,8},{4,12},{8,16},{12,20},{16,24},{20,28},{24,0},{28,4},{1,9},{5... | collective-permute-start | bytes 393224 | tf_op jit(solution)/shard_map/ppermute | solution.py:366
  345.5 2.4 collective-permute-start.46
  349.7 2.0 collective-permute-start.48
  352.3 2.0 collective-permute-start.49
  354.3 6.7 %collective-permute-done.46.refs_3_ = f32[2,128,128]{2,1,0:T(8,128)S(1)} collective-permute-done((f32[2,128,128]{2,1,0:T(8,128)S(1)}, f32[2,128,128]{2,1,0:T(8,128)S(1)}, u32[]{:S(2)}, u32[]{:S(2)}) %collective-permute-start.46) | collective-permute-done | bytes 131104 | tf_op jit(solution)/shard_map/ppermute | solution.py:366
  373.7 1.8 z_inverse.5
  381.8 2.2 z_inverse.4
  392.0 9.6 %collective-permute-done.73.refs_1_ = f32[2,512,128]{2,1,0:T(8,128)S(1)} collective-permute-done((f32[2,512,128]{2,1,0:T(8,128)S(1)}, f32[2,512,128]{2,1,0:T(8,128)S(1)}, u32[]{:S(2)}, u32[]{:S(2)}) %collective-permute-start.73) | collective-permute-done | bytes 524320 | tf_op jit(solution)/shard_map/ppermute | solution.py:360
  405.8 7.0 %collective-permute-done.62.refs_1_ = f32[2,512,128]{2,1,0:T(8,128)S(1)} collective-permute-done((f32[2,512,128]{2,1,0:T(8,128)S(1)}, f32[2,512,128]{2,1,0:T(8,128)S(1)}, u32[]{:S(2)}, u32[]{:S(2)}) %collective-permute-start.62) | collective-permute-done | bytes 524320 | tf_op jit(solution)/shard_map/ppermute | solution.py:360
  418.6 5.4 %collective-permute-done.51.refs_1_ = f32[2,512,128]{2,1,0:T(8,128)S(1)} collective-permute-done((f32[2,512,128]{2,1,0:T(8,128)S(1)}, f32[2,512,128]{2,1,0:T(8,128)S(1)}, u32[]{:S(2)}, u32[]{:S(2)}) %collective-permute-start.51) | collective-permute-done | bytes 524320 | tf_op jit(solution)/shard_map/ppermute | solution.py:360
  425.7 9.6 %collective-permute-done.87.refs_5_ = f32[2,512,128]{2,1,0:T(8,128)S(1)} collective-permute-done((f32[2,512,128]{2,1,0:T(8,128)S(1)}, f32[2,512,128]{2,1,0:T(8,128)S(1)}, u32[]{:S(2)}, u32[]{:S(2)}) %collective-permute-start.87) | collective-permute-done | bytes 524320 | tf_op jit(solution)/shard_map/ppermute | solution.py:360
  439.9 6.7 %collective-permute-done.76.refs_5_ = f32[2,512,128]{2,1,0:T(8,128)S(1)} collective-permute-done((f32[2,512,128]{2,1,0:T(8,128)S(1)}, f32[2,512,128]{2,1,0:T(8,128)S(1)}, u32[]{:S(2)}, u32[]{:S(2)}) %collective-permute-start.76) | collective-permute-done | bytes 524320 | tf_op jit(solution)/shard_map/ppermute | solution.py:360
  453.2 2.9 finish.4.refs_6_
  456.0 2.8 finish.5.refs_6_
  458.8 2.7 finish.6.refs_6_
  461.6 6.8 %collective-permute-done.54.refs_5_ = f32[2,512,128]{2,1,0:T(8,128)} collective-permute-done((f32[2,512,128]{2,1,0:T(8,128)}, f32[2,512,128]{2,1,0:T(8,128)}, u32[]{:S(2)}, u32[]{:S(2)}) %collective-permute-start.54) | collective-permute-done | bytes 524320 | tf_op jit(solution)/shard_map/ppermute | solution.py:360
  468.4 2.6 finish.7
  (420 shorter events, 117.4 us)
Async XLA Ops:
  3.6 16.1 %collective-permute-start.35 = (f32[2,512,128]{2,1,0:T(8,128)}, f32[2,512,128]{2,1,0:T(8,128)}, u32[]{:S(2)}, u32[]{:S(2)}) collective-permute-start(f32[2,512,128]{2,1,0:T(8,128)} %get-tuple-element.167.refs_3_), channel_id=1, source_target_pairs={{0,2},{1,3},{2,0},{3,1},{4,6},{5,7},{6,4},{7,5},{8,10},{9,11},{10,... | collective-permute-start | bytes 1572872 | tf_op jit(solution)/shard_map/ppermute | solution.py:360
  6.6 27.7 %collective-permute-start.33 = (f32[2,512,128]{2,1,0:T(8,128)}, f32[2,512,128]{2,1,0:T(8,128)}, u32[]{:S(2)}, u32[]{:S(2)}) collective-permute-start(f32[2,512,128]{2,1,0:T(8,128)} %get-tuple-element.168.refs_0_), channel_id=1, source_target_pairs={{0,1},{1,0},{2,3},{3,2},{4,5},{5,4},{6,7},{7,6},{8,9},{9,8},{10,11... | collective-permute-start | bytes 1572872 | tf_op jit(solution)/shard_map/ppermute | solution.py:360
  8.1 22.8 %collective-permute-start.24 = (f32[2,512,128]{2,1,0:T(8,128)S(1)}, f32[2,512,128]{2,1,0:T(8,128)}, u32[]{:S(2)}, u32[]{:S(2)}) collective-permute-start(f32[2,512,128]{2,1,0:T(8,128)S(1)} %get-tuple-element.169.refs_3_), channel_id=1, source_target_pairs={{0,2},{1,3},{2,0},{3,1},{4,6},{5,7},{6,4},{7,5},{8,10},{9,11},{10,... | collective-permute-start | bytes 1572872 | tf_op jit(solution)/shard_map/ppermute | solution.py:360
  8.6 28.5 %collective-permute-start.22 = (f32[2,512,128]{2,1,0:T(8,128)S(1)}, f32[2,512,128]{2,1,0:T(8,128)}, u32[]{:S(2)}, u32[]{:S(2)}) collective-permute-start(f32[2,512,128]{2,1,0:T(8,128)S(1)} %get-tuple-element.170.refs_0_), channel_id=1, source_target_pairs={{0,1},{1,0},{2,3},{3,2},{4,5},{5,4},{6,7},{7,6},{8,9},{9,8},{10,11... | collective-permute-start | bytes 1572872 | tf_op jit(solution)/shard_map/ppermute | solution.py:360
  8.7 33.4 %collective-permute-start.13 = (f32[2,512,128]{2,1,0:T(8,128)S(1)}, f32[2,512,128]{2,1,0:T(8,128)}, u32[]{:S(2)}, u32[]{:S(2)}) collective-permute-start(f32[2,512,128]{2,1,0:T(8,128)S(1)} %get-tuple-element.171.refs_3_), channel_id=1, source_target_pairs={{0,2},{1,3},{2,0},{3,1},{4,6},{5,7},{6,4},{7,5},{8,10},{9,11},{10,... | collective-permute-start | bytes 1572872 | tf_op jit(solution)/shard_map/ppermute | solution.py:360
  19.7 25.7 %collective-permute-start.11 = (f32[2,512,128]{2,1,0:T(8,128)S(1)}, f32[2,512,128]{2,1,0:T(8,128)S(1)}, u32[]{:S(2)}, u32[]{:S(2)}) collective-permute-start(f32[2,512,128]{2,1,0:T(8,128)S(1)} %get-tuple-element.172.refs_0_), channel_id=1, source_target_pairs={{0,1},{1,0},{2,3},{3,2},{4,5},{5,4},{6,7},{7,6},{8,9},{9,8},{10,11... | collective-permute-start | bytes 1572872 | tf_op jit(solution)/shard_map/ppermute | solution.py:360
  30.9 22.4 %collective-permute-start.2 = (f32[2,512,128]{2,1,0:T(8,128)S(1)}, f32[2,512,128]{2,1,0:T(8,128)S(1)}, u32[]{:S(2)}, u32[]{:S(2)}) collective-permute-start(f32[2,512,128]{2,1,0:T(8,128)S(1)} %get-tuple-element.173.refs_3_), channel_id=1, source_target_pairs={{0,2},{1,3},{2,0},{3,1},{4,6},{5,7},{6,4},{7,5},{8,10},{9,11},{10,... | collective-permute-start | bytes 1572872 | tf_op jit(solution)/shard_map/ppermute | solution.py:360
  34.3 23.7 %collective-permute-start = (f32[2,512,128]{2,1,0:T(8,128)S(1)}, f32[2,512,128]{2,1,0:T(8,128)S(1)}, u32[]{:S(2)}, u32[]{:S(2)}) collective-permute-start(f32[2,512,128]{2,1,0:T(8,128)S(1)} %get-tuple-element.174.refs_0_), channel_id=1, source_target_pairs={{0,1},{1,0},{2,3},{3,2},{4,5},{5,4},{6,7},{7,6},{8,9},{9,8},{10,11... | collective-permute-start | bytes 1572872 | tf_op jit(solution)/shard_map/ppermute | solution.py:360
  37.0 29.5 %collective-permute-start.36 = (f32[2,512,128]{2,1,0:T(8,128)S(1)}, f32[2,512,128]{2,1,0:T(8,128)S(1)}, u32[]{:S(2)}, u32[]{:S(2)}) collective-permute-start(f32[2,512,128]{2,1,0:T(8,128)S(1)} %pad_maximum_fusion.7), channel_id=1, source_target_pairs={{0,1},{1,0},{2,3},{3,2},{4,5},{5,4},{6,7},{7,6},{8,9},{9,8},{10,11... | collective-permute-start | bytes 1572872 | tf_op jit(solution)/shard_map/ppermute | solution.py:360
  42.1 25.5 %collective-permute-start.34 = (f32[2,512,128]{2,1,0:T(8,128)S(1)}, f32[2,512,128]{2,1,0:T(8,128)S(1)}, u32[]{:S(2)}, u32[]{:S(2)}) collective-permute-start(f32[2,512,128]{2,1,0:T(8,128)S(1)} %pad_maximum_fusion.6), channel_id=1, source_target_pairs={{0,2},{1,3},{2,0},{3,1},{4,6},{5,7},{6,4},{7,5},{8,10},{9,11},{10,... | collective-permute-start | bytes 1572872 | tf_op jit(solution)/shard_map/ppermute | solution.py:360
  45.4 32.4 %collective-permute-start.25 = (f32[2,512,128]{2,1,0:T(8,128)S(1)}, f32[2,512,128]{2,1,0:T(8,128)S(1)}, u32[]{:S(2)}, u32[]{:S(2)}) collective-permute-start(f32[2,512,128]{2,1,0:T(8,128)S(1)} %pad_maximum_fusion.5), channel_id=1, source_target_pairs={{0,1},{1,0},{2,3},{3,2},{4,5},{5,4},{6,7},{7,6},{8,9},{9,8},{10,11... | collective-permute-start | bytes 1572872 | tf_op jit(solution)/shard_map/ppermute | solution.py:360
  53.3 92.3 %collective-permute-start.23 = (f32[2,512,128]{2,1,0:T(8,128)}, f32[2,512,128]{2,1,0:T(8,128)}, u32[]{:S(2)}, u32[]{:S(2)}) collective-permute-start(f32[2,512,128]{2,1,0:T(8,128)} %pad_maximum_fusion.4), channel_id=1, source_target_pairs={{0,2},{1,3},{2,0},{3,1},{4,6},{5,7},{6,4},{7,5},{8,10},{9,11},{10,... | collective-permute-start | bytes 1572872 | tf_op jit(solution)/shard_map/ppermute | solution.py:360
  58.0 88.3 %collective-permute-start.14 = (f32[2,512,128]{2,1,0:T(8,128)}, f32[2,512,128]{2,1,0:T(8,128)}, u32[]{:S(2)}, u32[]{:S(2)}) collective-permute-start(f32[2,512,128]{2,1,0:T(8,128)} %pad_maximum_fusion.3), channel_id=1, source_target_pairs={{0,1},{1,0},{2,3},{3,2},{4,5},{5,4},{6,7},{7,6},{8,9},{9,8},{10,11... | collective-permute-start | bytes 1572872 | tf_op jit(solution)/shard_map/ppermute | solution.py:360
  66.6 83.1 %collective-permute-start.12 = (f32[2,512,128]{2,1,0:T(8,128)}, f32[2,512,128]{2,1,0:T(8,128)}, u32[]{:S(2)}, u32[]{:S(2)}) collective-permute-start(f32[2,512,128]{2,1,0:T(8,128)} %pad_maximum_fusion.2), channel_id=1, source_target_pairs={{0,2},{1,3},{2,0},{3,1},{4,6},{5,7},{6,4},{7,5},{8,10},{9,11},{10,... | collective-permute-start | bytes 1572872 | tf_op jit(solution)/shard_map/ppermute | solution.py:360
  68.4 84.8 %collective-permute-start.3 = (f32[2,512,128]{2,1,0:T(8,128)}, f32[2,512,128]{2,1,0:T(8,128)}, u32[]{:S(2)}, u32[]{:S(2)}) collective-permute-start(f32[2,512,128]{2,1,0:T(8,128)} %pad_maximum_fusion.1), channel_id=1, source_target_pairs={{0,1},{1,0},{2,3},{3,2},{4,5},{5,4},{6,7},{7,6},{8,9},{9,8},{10,11... | collective-permute-start | bytes 1572872 | tf_op jit(solution)/shard_map/ppermute | solution.py:360
  78.6 77.4 %collective-permute-start.1 = (f32[2,512,128]{2,1,0:T(8,128)}, f32[2,512,128]{2,1,0:T(8,128)}, u32[]{:S(2)}, u32[]{:S(2)}) collective-permute-start(f32[2,512,128]{2,1,0:T(8,128)} %pad_maximum_fusion), channel_id=1, source_target_pairs={{0,2},{1,3},{2,0},{3,1},{4,6},{5,7},{6,4},{7,5},{8,10},{9,11},{10,... | collective-permute-start | bytes 1572872 | tf_op jit(solution)/shard_map/ppermute | solution.py:360
  153.3 18.2 %collective-permute-start.40 = (f32[2,128,128]{2,1,0:T(8,128)S(1)}, f32[2,128,128]{2,1,0:T(8,128)S(1)}, u32[]{:S(2)}, u32[]{:S(2)}) collective-permute-start(f32[2,128,128]{2,1,0:T(8,128)S(1)} %get-tuple-element.105), channel_id=1, source_target_pairs={{0,16},{4,20},{8,24},{12,28},{16,0},{20,4},{24,8},{28,12},{1,17},{... | collective-permute-start | bytes 393224 | tf_op jit(solution)/shard_map/ppermute | solution.py:366
  156.0 17.8 %collective-permute-start.41 = (f32[2,128,128]{2,1,0:T(8,128)S(1)}, f32[2,128,128]{2,1,0:T(8,128)S(1)}, u32[]{:S(2)}, u32[]{:S(2)}) collective-permute-start(f32[2,128,128]{2,1,0:T(8,128)S(1)} %get-tuple-element.106), channel_id=1, source_target_pairs={{0,12},{4,16},{8,20},{12,24},{16,28},{20,0},{24,4},{28,8},{1,13},{... | collective-permute-start | bytes 393224 | tf_op jit(solution)/shard_map/ppermute | solution.py:366
  156.0 17.7 %collective-permute-start.42 = (f32[2,128,128]{2,1,0:T(8,128)S(1)}, f32[2,128,128]{2,1,0:T(8,128)S(1)}, u32[]{:S(2)}, u32[]{:S(2)}) collective-permute-start(f32[2,128,128]{2,1,0:T(8,128)S(1)} %get-tuple-element.107), channel_id=1, source_target_pairs={{0,8},{4,12},{8,16},{12,20},{16,24},{20,28},{24,0},{28,4},{1,9},{5... | collective-permute-start | bytes 393224 | tf_op jit(solution)/shard_map/ppermute | solution.py:366
  156.7 26.0 %collective-permute-start.43 = (f32[2,128,128]{2,1,0:T(8,128)S(1)}, f32[2,128,128]{2,1,0:T(8,128)S(1)}, u32[]{:S(2)}, u32[]{:S(2)}) collective-permute-start(f32[2,128,128]{2,1,0:T(8,128)S(1)} %get-tuple-element.108), channel_id=1, source_target_pairs={{0,4},{4,8},{8,12},{12,16},{16,20},{20,24},{24,28},{28,0},{1,5},{5... | collective-permute-start | bytes 393224 | tf_op jit(solution)/shard_map/ppermute | solution.py:366
  156.9 25.9 %collective-permute-start.26 = (f32[2,128,128]{2,1,0:T(8,128)S(1)}, f32[2,128,128]{2,1,0:T(8,128)S(1)}, u32[]{:S(2)}, u32[]{:S(2)}) collective-permute-start(f32[2,128,128]{2,1,0:T(8,128)S(1)} %get-tuple-element.94), channel_id=1, source_target_pairs={{0,28},{4,0},{8,4},{12,8},{16,12},{20,16},{24,20},{28,24},{1,29},{... | collective-permute-start | bytes 393224 | tf_op jit(solution)/shard_map/ppermute | solution.py:366
  171.5 17.0 %collective-permute-start.27 = (f32[2,128,128]{2,1,0:T(8,128)}, f32[2,128,128]{2,1,0:T(8,128)}, u32[]{:S(2)}, u32[]{:S(2)}) collective-permute-start(f32[2,128,128]{2,1,0:T(8,128)} %get-tuple-element.95), channel_id=1, source_target_pairs={{0,24},{4,28},{8,0},{12,4},{16,8},{20,12},{24,16},{28,20},{1,25},{... | collective-permute-start | bytes 393224 | tf_op jit(solution)/shard_map/ppermute | solution.py:366
  173.8 15.4 %collective-permute-start.28 = (f32[2,128,128]{2,1,0:T(8,128)S(1)}, f32[2,128,128]{2,1,0:T(8,128)}, u32[]{:S(2)}, u32[]{:S(2)}) collective-permute-start(f32[2,128,128]{2,1,0:T(8,128)S(1)} %get-tuple-element.96), channel_id=1, source_target_pairs={{0,20},{4,24},{8,28},{12,0},{16,4},{20,8},{24,12},{28,16},{1,21},{... | collective-permute-start | bytes 393224 | tf_op jit(solution)/shard_map/ppermute | solution.py:366
  173.8 21.8 %collective-permute-start.29 = (f32[2,128,128]{2,1,0:T(8,128)}, f32[2,128,128]{2,1,0:T(8,128)}, u32[]{:S(2)}, u32[]{:S(2)}) collective-permute-start(f32[2,128,128]{2,1,0:T(8,128)} %get-tuple-element.97), channel_id=1, source_target_pairs={{0,16},{4,20},{8,24},{12,28},{16,0},{20,4},{24,8},{28,12},{1,17},{... | collective-permute-start | bytes 393224 | tf_op jit(solution)/shard_map/ppermute | solution.py:366
  195.8 21.9 %collective-permute-start.18 = (f32[2,128,128]{2,1,0:T(8,128)S(1)}, f32[2,128,128]{2,1,0:T(8,128)S(1)}, u32[]{:S(2)}, u32[]{:S(2)}) collective-permute-start(f32[2,128,128]{2,1,0:T(8,128)S(1)} %get-tuple-element.89), channel_id=1, source_target_pairs={{0,16},{4,20},{8,24},{12,28},{16,0},{20,4},{24,8},{28,12},{1,17},{... | collective-permute-start | bytes 393224 | tf_op jit(solution)/shard_map/ppermute | solution.py:366
  203.5 16.5 %collective-permute-start.19 = (f32[2,128,128]{2,1,0:T(8,128)S(1)}, f32[2,128,128]{2,1,0:T(8,128)S(1)}, u32[]{:S(2)}, u32[]{:S(2)}) collective-permute-start(f32[2,128,128]{2,1,0:T(8,128)S(1)} %get-tuple-element.90), channel_id=1, source_target_pairs={{0,12},{4,16},{8,20},{12,24},{16,28},{20,0},{24,4},{28,8},{1,13},{... | collective-permute-start | bytes 393224 | tf_op jit(solution)/shard_map/ppermute | solution.py:366
  203.5 16.5 %collective-permute-start.20 = (f32[2,128,128]{2,1,0:T(8,128)S(1)}, f32[2,128,128]{2,1,0:T(8,128)S(1)}, u32[]{:S(2)}, u32[]{:S(2)}) collective-permute-start(f32[2,128,128]{2,1,0:T(8,128)S(1)} %get-tuple-element.91), channel_id=1, source_target_pairs={{0,8},{4,12},{8,16},{12,20},{16,24},{20,28},{24,0},{28,4},{1,9},{5... | collective-permute-start | bytes 393224 | tf_op jit(solution)/shard_map/ppermute | solution.py:366
  203.6 16.5 %collective-permute-start.21 = (f32[2,128,128]{2,1,0:T(8,128)S(1)}, f32[2,128,128]{2,1,0:T(8,128)S(1)}, u32[]{:S(2)}, u32[]{:S(2)}) collective-permute-start(f32[2,128,128]{2,1,0:T(8,128)S(1)} %get-tuple-element.92), channel_id=1, source_target_pairs={{0,4},{4,8},{8,12},{12,16},{16,20},{20,24},{24,28},{28,0},{1,5},{5... | collective-permute-start | bytes 393224 | tf_op jit(solution)/shard_map/ppermute | solution.py:366
  204.6 16.7 %collective-permute-start.10 = (f32[2,128,128]{2,1,0:T(8,128)S(1)}, f32[2,128,128]{2,1,0:T(8,128)S(1)}, u32[]{:S(2)}, u32[]{:S(2)}) collective-permute-start(f32[2,128,128]{2,1,0:T(8,128)S(1)} %get-tuple-element.84), channel_id=1, source_target_pairs={{0,4},{4,8},{8,12},{12,16},{16,20},{20,24},{24,28},{28,0},{1,5},{5... | collective-permute-start | bytes 393224 | tf_op jit(solution)/shard_map/ppermute | solution.py:366
  220.1 19.4 %collective-permute-start.7 = (f32[2,128,128]{2,1,0:T(8,128)}, f32[2,128,128]{2,1,0:T(8,128)S(1)}, u32[]{:S(2)}, u32[]{:S(2)}) collective-permute-start(f32[2,128,128]{2,1,0:T(8,128)} %get-tuple-element.81), channel_id=1, source_target_pairs={{0,16},{4,20},{8,24},{12,28},{16,0},{20,4},{24,8},{28,12},{1,17},{... | collective-permute-start | bytes 393224 | tf_op jit(solution)/shard_map/ppermute | solution.py:366
  221.2 19.9 %collective-permute-start.8 = (f32[2,128,128]{2,1,0:T(8,128)S(1)}, f32[2,128,128]{2,1,0:T(8,128)S(1)}, u32[]{:S(2)}, u32[]{:S(2)}) collective-permute-start(f32[2,128,128]{2,1,0:T(8,128)S(1)} %get-tuple-element.82), channel_id=1, source_target_pairs={{0,12},{4,16},{8,20},{12,24},{16,28},{20,0},{24,4},{28,8},{1,13},{... | collective-permute-start | bytes 393224 | tf_op jit(solution)/shard_map/ppermute | solution.py:366
  222.6 19.2 %collective-permute-start.9 = (f32[2,128,128]{2,1,0:T(8,128)S(1)}, f32[2,128,128]{2,1,0:T(8,128)S(1)}, u32[]{:S(2)}, u32[]{:S(2)}) collective-permute-start(f32[2,128,128]{2,1,0:T(8,128)S(1)} %get-tuple-element.83), channel_id=1, source_target_pairs={{0,8},{4,12},{8,16},{12,20},{16,24},{20,28},{24,0},{28,4},{1,9},{5... | collective-permute-start | bytes 393224 | tf_op jit(solution)/shard_map/ppermute | solution.py:366
  269.8 18.8 %collective-permute-start.79 = (f32[2,128,128]{2,1,0:T(8,128)S(1)}, f32[2,128,128]{2,1,0:T(8,128)S(1)}, u32[]{:S(2)}, u32[]{:S(2)}) collective-permute-start(f32[2,128,128]{2,1,0:T(8,128)S(1)} %get-tuple-element.142), channel_id=1, source_target_pairs={{0,12},{4,16},{8,20},{12,24},{16,28},{20,0},{24,4},{28,8},{1,13},{... | collective-permute-start | bytes 393224 | tf_op jit(solution)/shard_map/ppermute | solution.py:366
  271.5 17.3 %collective-permute-start.80 = (f32[2,128,128]{2,1,0:T(8,128)S(1)}, f32[2,128,128]{2,1,0:T(8,128)S(1)}, u32[]{:S(2)}, u32[]{:S(2)}) collective-permute-start(f32[2,128,128]{2,1,0:T(8,128)S(1)} %get-tuple-element.143), channel_id=1, source_target_pairs={{0,16},{4,20},{8,24},{12,28},{16,0},{20,4},{24,8},{28,12},{1,17},{... | collective-permute-start | bytes 393224 | tf_op jit(solution)/shard_map/ppermute | solution.py:366
  273.9 18.5 %collective-permute-start.81 = (f32[2,128,128]{2,1,0:T(8,128)S(1)}, f32[2,128,128]{2,1,0:T(8,128)S(1)}, u32[]{:S(2)}, u32[]{:S(2)}) collective-permute-start(f32[2,128,128]{2,1,0:T(8,128)S(1)} %get-tuple-element.144), channel_id=1, source_target_pairs={{0,20},{4,24},{8,28},{12,0},{16,4},{20,8},{24,12},{28,16},{1,21},{... | collective-permute-start | bytes 393224 | tf_op jit(solution)/shard_map/ppermute | solution.py:366
  276.9 18.5 %collective-permute-start.82 = (f32[2,128,128]{2,1,0:T(8,128)S(1)}, f32[2,128,128]{2,1,0:T(8,128)S(1)}, u32[]{:S(2)}, u32[]{:S(2)}) collective-permute-start(f32[2,128,128]{2,1,0:T(8,128)S(1)} %get-tuple-element.145), channel_id=1, source_target_pairs={{0,24},{4,28},{8,0},{12,4},{16,8},{20,12},{24,16},{28,20},{1,25},{... | collective-permute-start | bytes 393224 | tf_op jit(solution)/shard_map/ppermute | solution.py:366
  278.1 21.3 %collective-permute-start.83 = (f32[2,128,128]{2,1,0:T(8,128)S(1)}, f32[2,128,128]{2,1,0:T(8,128)S(1)}, u32[]{:S(2)}, u32[]{:S(2)}) collective-permute-start(f32[2,128,128]{2,1,0:T(8,128)S(1)} %get-tuple-element.146), channel_id=1, source_target_pairs={{0,28},{4,0},{8,4},{12,8},{16,12},{20,16},{24,20},{28,24},{1,29},{... | collective-permute-start | bytes 393224 | tf_op jit(solution)/shard_map/ppermute | solution.py:366
  288.6 17.5 %collective-permute-start.66 = (f32[2,128,128]{2,1,0:T(8,128)S(1)}, f32[2,128,128]{2,1,0:T(8,128)S(1)}, u32[]{:S(2)}, u32[]{:S(2)}) collective-permute-start(f32[2,128,128]{2,1,0:T(8,128)S(1)} %get-tuple-element.130), channel_id=1, source_target_pairs={{0,4},{4,8},{8,12},{12,16},{16,20},{20,24},{24,28},{28,0},{1,5},{5... | collective-permute-start | bytes 393224 | tf_op jit(solution)/shard_map/ppermute | solution.py:366
  288.7 20.4 %collective-permute-start.67 = (f32[2,128,128]{2,1,0:T(8,128)S(1)}, f32[2,128,128]{2,1,0:T(8,128)S(1)}, u32[]{:S(2)}, u32[]{:S(2)}) collective-permute-start(f32[2,128,128]{2,1,0:T(8,128)S(1)} %get-tuple-element.131), channel_id=1, source_target_pairs={{0,8},{4,12},{8,16},{12,20},{16,24},{20,28},{24,0},{28,4},{1,9},{5... | collective-permute-start | bytes 393224 | tf_op jit(solution)/shard_map/ppermute | solution.py:366
  293.1 16.1 %collective-permute-start.68 = (f32[2,128,128]{2,1,0:T(8,128)S(1)}, f32[2,128,128]{2,1,0:T(8,128)S(1)}, u32[]{:S(2)}, u32[]{:S(2)}) collective-permute-start(f32[2,128,128]{2,1,0:T(8,128)S(1)} %get-tuple-element.132), channel_id=1, source_target_pairs={{0,12},{4,16},{8,20},{12,24},{16,28},{20,0},{24,4},{28,8},{1,13},{... | collective-permute-start | bytes 393224 | tf_op jit(solution)/shard_map/ppermute | solution.py:366
  306.0 15.9 %collective-permute-start.71 = (f32[2,128,128]{2,1,0:T(8,128)}, f32[2,128,128]{2,1,0:T(8,128)S(1)}, u32[]{:S(2)}, u32[]{:S(2)}) collective-permute-start(f32[2,128,128]{2,1,0:T(8,128)} %get-tuple-element.135), channel_id=1, source_target_pairs={{0,24},{4,28},{8,0},{12,4},{16,8},{20,12},{24,16},{28,20},{1,25},{... | collective-permute-start | bytes 393224 | tf_op jit(solution)/shard_map/ppermute | solution.py:366
  309.2 20.5 %collective-permute-start.55 = (f32[2,128,128]{2,1,0:T(8,128)}, f32[2,128,128]{2,1,0:T(8,128)S(1)}, u32[]{:S(2)}, u32[]{:S(2)}) collective-permute-start(f32[2,128,128]{2,1,0:T(8,128)} %get-tuple-element.120), channel_id=1, source_target_pairs={{0,4},{4,8},{8,12},{12,16},{16,20},{20,24},{24,28},{28,0},{1,5},{5... | collective-permute-start | bytes 393224 | tf_op jit(solution)/shard_map/ppermute | solution.py:366
  309.7 20.1 %collective-permute-start.56 = (f32[2,128,128]{2,1,0:T(8,128)}, f32[2,128,128]{2,1,0:T(8,128)S(1)}, u32[]{:S(2)}, u32[]{:S(2)}) collective-permute-start(f32[2,128,128]{2,1,0:T(8,128)} %get-tuple-element.121), channel_id=1, source_target_pairs={{0,8},{4,12},{8,16},{12,20},{16,24},{20,28},{24,0},{28,4},{1,9},{5... | collective-permute-start | bytes 393224 | tf_op jit(solution)/shard_map/ppermute | solution.py:366
  310.9 21.3 %collective-permute-start.57 = (f32[2,128,128]{2,1,0:T(8,128)}, f32[2,128,128]{2,1,0:T(8,128)S(1)}, u32[]{:S(2)}, u32[]{:S(2)}) collective-permute-start(f32[2,128,128]{2,1,0:T(8,128)} %copy-done.93), channel_id=1, source_target_pairs={{0,12},{4,16},{8,20},{12,24},{16,28},{20,0},{24,4},{28,8},{1,13},{... | collective-permute-start | bytes 393224 | tf_op jit(solution)/shard_map/ppermute | solution.py:366
  322.6 61.4 %collective-permute-start.86 = (f32[2,512,128]{2,1,0:T(8,128)}, f32[2,512,128]{2,1,0:T(8,128)}, u32[]{:S(2)}, u32[]{:S(2)}) collective-permute-start(f32[2,512,128]{2,1,0:T(8,128)} %get-tuple-element.148.refs_3_), channel_id=1, source_target_pairs={{0,2},{1,3},{2,0},{3,1},{4,6},{5,7},{6,4},{7,5},{8,10},{9,11},{10,... | collective-permute-start | bytes 1572872 | tf_op jit(solution)/shard_map/ppermute | solution.py:360
  345.5 15.5 %collective-permute-start.46 = (f32[2,128,128]{2,1,0:T(8,128)S(1)}, f32[2,128,128]{2,1,0:T(8,128)S(1)}, u32[]{:S(2)}, u32[]{:S(2)}) collective-permute-start(f32[2,128,128]{2,1,0:T(8,128)S(1)} %copy-done.80), channel_id=1, source_target_pairs={{0,12},{4,16},{8,20},{12,24},{16,28},{20,0},{24,4},{28,8},{1,13},{... | collective-permute-start | bytes 393224 | tf_op jit(solution)/shard_map/ppermute | solution.py:366
  348.6 16.6 %collective-permute-start.47 = (f32[2,128,128]{2,1,0:T(8,128)S(1)}, f32[2,128,128]{2,1,0:T(8,128)S(1)}, u32[]{:S(2)}, u32[]{:S(2)}) collective-permute-start(f32[2,128,128]{2,1,0:T(8,128)S(1)} %copy-done.78), channel_id=1, source_target_pairs={{0,16},{4,20},{8,24},{12,28},{16,0},{20,4},{24,8},{28,12},{1,17},{... | collective-permute-start | bytes 393224 | tf_op jit(solution)/shard_map/ppermute | solution.py:366
  349.7 25.8 %collective-permute-start.48 = (f32[2,128,128]{2,1,0:T(8,128)}, f32[2,128,128]{2,1,0:T(8,128)}, u32[]{:S(2)}, u32[]{:S(2)}) collective-permute-start(f32[2,128,128]{2,1,0:T(8,128)} %get-tuple-element.114), channel_id=1, source_target_pairs={{0,20},{4,24},{8,28},{12,0},{16,4},{20,8},{24,12},{28,16},{1,21},{... | collective-permute-start | bytes 393224 | tf_op jit(solution)/shard_map/ppermute | solution.py:366
  352.3 24.8 %collective-permute-start.49 = (f32[2,128,128]{2,1,0:T(8,128)}, f32[2,128,128]{2,1,0:T(8,128)}, u32[]{:S(2)}, u32[]{:S(2)}) collective-permute-start(f32[2,128,128]{2,1,0:T(8,128)} %get-tuple-element.115), channel_id=1, source_target_pairs={{0,24},{4,28},{8,0},{12,4},{16,8},{20,12},{24,16},{28,20},{1,25},{... | collective-permute-start | bytes 393224 | tf_op jit(solution)/shard_map/ppermute | solution.py:366
  361.6 16.0 %collective-permute-start.50 = (f32[2,128,128]{2,1,0:T(8,128)}, f32[2,128,128]{2,1,0:T(8,128)}, u32[]{:S(2)}, u32[]{:S(2)}) collective-permute-start(f32[2,128,128]{2,1,0:T(8,128)} %get-tuple-element.116), channel_id=1, source_target_pairs={{0,28},{4,0},{8,4},{12,8},{16,12},{20,16},{24,20},{28,24},{1,29},{... | collective-permute-start | bytes 393224 | tf_op jit(solution)/shard_map/ppermute | solution.py:366
  365.9 21.0 %collective-permute-start.75 = (f32[2,512,128]{2,1,0:T(8,128)S(1)}, f32[2,512,128]{2,1,0:T(8,128)}, u32[]{:S(2)}, u32[]{:S(2)}) collective-permute-start(f32[2,512,128]{2,1,0:T(8,128)S(1)} %get-tuple-element.138.refs_3_), channel_id=1, source_target_pairs={{0,2},{1,3},{2,0},{3,1},{4,6},{5,7},{6,4},{7,5},{8,10},{9,11},{10,... | collective-permute-start | bytes 1572872 | tf_op jit(solution)/shard_map/ppermute | solution.py:360
  377.1 24.5 %collective-permute-start.73 = (f32[2,512,128]{2,1,0:T(8,128)S(1)}, f32[2,512,128]{2,1,0:T(8,128)S(1)}, u32[]{:S(2)}, u32[]{:S(2)}) collective-permute-start(f32[2,512,128]{2,1,0:T(8,128)S(1)} %get-tuple-element.137.refs_0_), channel_id=1, source_target_pairs={{0,1},{1,0},{2,3},{3,2},{4,5},{5,4},{6,7},{7,6},{8,9},{9,8},{10,11... | collective-permute-start | bytes 1572872 | tf_op jit(solution)/shard_map/ppermute | solution.py:360
  377.6 26.6 %collective-permute-start.64 = (f32[2,512,128]{2,1,0:T(8,128)S(1)}, f32[2,512,128]{2,1,0:T(8,128)S(1)}, u32[]{:S(2)}, u32[]{:S(2)}) collective-permute-start(f32[2,512,128]{2,1,0:T(8,128)S(1)} %get-tuple-element.128.refs_3_), channel_id=1, source_target_pairs={{0,2},{1,3},{2,0},{3,1},{4,6},{5,7},{6,4},{7,5},{8,10},{9,11},{10,... | collective-permute-start | bytes 1572872 | tf_op jit(solution)/shard_map/ppermute | solution.py:360
  384.0 28.8 %collective-permute-start.62 = (f32[2,512,128]{2,1,0:T(8,128)S(1)}, f32[2,512,128]{2,1,0:T(8,128)S(1)}, u32[]{:S(2)}, u32[]{:S(2)}) collective-permute-start(f32[2,512,128]{2,1,0:T(8,128)S(1)} %get-tuple-element.127.refs_0_), channel_id=1, source_target_pairs={{0,1},{1,0},{2,3},{3,2},{4,5},{5,4},{6,7},{7,6},{8,9},{9,8},{10,11... | collective-permute-start | bytes 1572872 | tf_op jit(solution)/shard_map/ppermute | solution.py:360
  386.9 27.5 %collective-permute-start.53 = (f32[2,512,128]{2,1,0:T(8,128)S(1)}, f32[2,512,128]{2,1,0:T(8,128)S(1)}, u32[]{:S(2)}, u32[]{:S(2)}) collective-permute-start(f32[2,512,128]{2,1,0:T(8,128)S(1)} %get-tuple-element.118.refs_3_), channel_id=1, source_target_pairs={{0,2},{1,3},{2,0},{3,1},{4,6},{5,7},{6,4},{7,5},{8,10},{9,11},{10,... | collective-permute-start | bytes 1572872 | tf_op jit(solution)/shard_map/ppermute | solution.py:360
  390.3 33.7 %collective-permute-start.51 = (f32[2,512,128]{2,1,0:T(8,128)S(1)}, f32[2,512,128]{2,1,0:T(8,128)S(1)}, u32[]{:S(2)}, u32[]{:S(2)}) collective-permute-start(f32[2,512,128]{2,1,0:T(8,128)S(1)} %get-tuple-element.117.refs_0_), channel_id=1, source_target_pairs={{0,1},{1,0},{2,3},{3,2},{4,5},{5,4},{6,7},{7,6},{8,9},{9,8},{10,11... | collective-permute-start | bytes 1572872 | tf_op jit(solution)/shard_map/ppermute | solution.py:360
  401.6 33.7 %collective-permute-start.87 = (f32[2,512,128]{2,1,0:T(8,128)S(1)}, f32[2,512,128]{2,1,0:T(8,128)S(1)}, u32[]{:S(2)}, u32[]{:S(2)}) collective-permute-start(f32[2,512,128]{2,1,0:T(8,128)S(1)} %pad_maximum_fusion.15), channel_id=1, source_target_pairs={{0,1},{1,0},{2,3},{3,2},{4,5},{5,4},{6,7},{7,6},{8,9},{9,8},{10,11... | collective-permute-start | bytes 1572872 | tf_op jit(solution)/shard_map/ppermute | solution.py:360
  404.2 33.4 %collective-permute-start.85 = (f32[2,512,128]{2,1,0:T(8,128)S(1)}, f32[2,512,128]{2,1,0:T(8,128)S(1)}, u32[]{:S(2)}, u32[]{:S(2)}) collective-permute-start(f32[2,512,128]{2,1,0:T(8,128)S(1)} %pad_maximum_fusion.14), channel_id=1, source_target_pairs={{0,2},{1,3},{2,0},{3,1},{4,6},{5,7},{6,4},{7,5},{8,10},{9,11},{10,... | collective-permute-start | bytes 1572872 | tf_op jit(solution)/shard_map/ppermute | solution.py:360
  412.8 33.7 %collective-permute-start.76 = (f32[2,512,128]{2,1,0:T(8,128)S(1)}, f32[2,512,128]{2,1,0:T(8,128)S(1)}, u32[]{:S(2)}, u32[]{:S(2)}) collective-permute-start(f32[2,512,128]{2,1,0:T(8,128)S(1)} %pad_maximum_fusion.13), channel_id=1, source_target_pairs={{0,1},{1,0},{2,3},{3,2},{4,5},{5,4},{6,7},{7,6},{8,9},{9,8},{10,11... | collective-permute-start | bytes 1572872 | tf_op jit(solution)/shard_map/ppermute | solution.py:360
  414.4 41.6 %collective-permute-start.74 = (f32[2,512,128]{2,1,0:T(8,128)}, f32[2,512,128]{2,1,0:T(8,128)}, u32[]{:S(2)}, u32[]{:S(2)}) collective-permute-start(f32[2,512,128]{2,1,0:T(8,128)} %pad_maximum_fusion.12), channel_id=1, source_target_pairs={{0,2},{1,3},{2,0},{3,1},{4,6},{5,7},{6,4},{7,5},{8,10},{9,11},{10,... | collective-permute-start | bytes 1572872 | tf_op jit(solution)/shard_map/ppermute | solution.py:360
  424.0 34.8 %collective-permute-start.65 = (f32[2,512,128]{2,1,0:T(8,128)}, f32[2,512,128]{2,1,0:T(8,128)}, u32[]{:S(2)}, u32[]{:S(2)}) collective-permute-start(f32[2,512,128]{2,1,0:T(8,128)} %pad_maximum_fusion.11), channel_id=1, source_target_pairs={{0,1},{1,0},{2,3},{3,2},{4,5},{5,4},{6,7},{7,6},{8,9},{9,8},{10,11... | collective-permute-start | bytes 1572872 | tf_op jit(solution)/shard_map/ppermute | solution.py:360
  435.3 23.6 %collective-permute-start.63 = (f32[2,512,128]{2,1,0:T(8,128)}, f32[2,512,128]{2,1,0:T(8,128)}, u32[]{:S(2)}, u32[]{:S(2)}) collective-permute-start(f32[2,512,128]{2,1,0:T(8,128)} %pad_maximum_fusion.10), channel_id=1, source_target_pairs={{0,2},{1,3},{2,0},{3,1},{4,6},{5,7},{6,4},{7,5},{8,10},{9,11},{10,... | collective-permute-start | bytes 1572872 | tf_op jit(solution)/shard_map/ppermute | solution.py:360
  438.4 30.0 %collective-permute-start.54 = (f32[2,512,128]{2,1,0:T(8,128)}, f32[2,512,128]{2,1,0:T(8,128)}, u32[]{:S(2)}, u32[]{:S(2)}) collective-permute-start(f32[2,512,128]{2,1,0:T(8,128)} %pad_maximum_fusion.9), channel_id=1, source_target_pairs={{0,1},{1,0},{2,3},{3,2},{4,5},{5,4},{6,7},{7,6},{8,9},{9,8},{10,11... | collective-permute-start | bytes 1572872 | tf_op jit(solution)/shard_map/ppermute | solution.py:360
  447.3 21.1 %collective-permute-start.52 = (f32[2,512,128]{2,1,0:T(8,128)}, f32[2,512,128]{2,1,0:T(8,128)}, u32[]{:S(2)}, u32[]{:S(2)}) collective-permute-start(f32[2,512,128]{2,1,0:T(8,128)} %pad_maximum_fusion.8), channel_id=1, source_target_pairs={{0,2},{1,3},{2,0},{3,1},{4,6},{5,7},{6,4},{7,5},{8,10},{9,11},{10,... | collective-permute-start | bytes 1572872 | tf_op jit(solution)/shard_map/ppermute | solution.py:360
  (137 other events, 1347.7 us)

commit v2 on v1

v2 whole, which is shorter than its diff:
```python
import functools
import math

import jax
import jax.numpy as jnp
import numpy as np
from jax import lax
from jax.experimental import pallas as pl
from jax.experimental.pallas import tpu as pltpu
from jax.sharding import PartitionSpec as P

SCREEN = 1024
AMP = 2048
LANES = 128
MIX_WEIGHT = 480
VMEM_LIMIT = 48 * 1024 * 1024
FIRSTS = (1, 2)


def split_bf16(value):
    high = np.asarray(value, np.float64).astype(np.float32).astype(jnp.bfloat16)
    low = (value - high.astype(np.float64)).astype(np.float32).astype(jnp.bfloat16)
    return high, low


def dft_matrix(length, orient, left):
    index = np.arange(length)
    angle = 2.0 * np.pi * ((index[:, None] * index[None, :]) % length) / length
    cosine, sine = np.cos(angle), orient * np.sin(angle)
    if left:
        whole = np.block([[cosine, -sine], [sine, cosine]])
    else:
        whole = np.block([[cosine, sine], [-sine, cosine]])
    high, low = split_bf16(whole)
    return np.stack([high, low])


def turn(numerator, length):
    angle = (np.asarray(numerator) % length) * (2.0 * np.pi / length)
    return np.stack([np.cos(angle), -np.sin(angle)], axis=-1).astype(np.float32)


def c_add(a, b):
    return (a[0] + b[0], a[1] + b[1])


def c_sub(a, b):
    return (a[0] - b[0], a[1] - b[1])


def c_mul(a, b):
    return (a[0] * b[0] - a[1] * b[1], a[0] * b[1] + a[1] * b[0])


def c_const(a, numerator, length, orient):
    numerator = (orient * numerator) % length
    if numerator == 0:
        return a
    if 2 * numerator == length:
        return (-a[0], -a[1])
    if 4 * numerator == length:
        return (-a[1], a[0])
    if 4 * numerator == 3 * length:
        return (a[1], -a[0])
    angle = 2.0 * math.pi * numerator / length
    cosine, sine = math.cos(angle), math.sin(angle)
    if 8 * numerator % length == 0:
        root = math.sqrt(0.5)
        total, differ = (a[0] + a[1]) * root, (a[0] - a[1]) * root
        if cosine > 0 and sine > 0:
            return (differ, total)
        if cosine > 0:
            return (total, -differ)
        if sine > 0:
            return (-total, differ)
        return (-differ, -total)
    return (a[0] * cosine - a[1] * sine, a[0] * sine + a[1] * cosine)


def small_dft(values, orient):
    count = len(values)
    if count == 1:
        return values
    half = count // 2
    upper = [c_add(values[i], values[i + half]) for i in range(half)]
    lower = [
        c_const(c_sub(values[i], values[i + half]), i, count, orient) for i in range(half)
    ]
    even, odd = small_dft(upper, orient), small_dft(lower, orient)
    result = []
    for i in range(half):
        result += [even[i], odd[i]]
    return result


def dot3(high, low, value, left):
    value_high = value.astype(jnp.bfloat16)
    value_low = (value - value_high.astype(jnp.float32)).astype(jnp.bfloat16)
    dot = functools.partial(jnp.dot, preferred_element_type=jnp.float32)
    if left:
        return dot(high, value_high) + (dot(high, value_low) + dot(low, value_high))
    return dot(value_high, high) + (dot(value_low, high) + dot(value_high, low))


def whole_spec(shape):
    return pl.BlockSpec(shape, lambda *_: (0,) * len(shape))


def params():
    return pltpu.CompilerParams(vmem_limit_bytes=VMEM_LIMIT)


def combine(inputs, coef_ref, row, place):
    total = None
    for term, ref in enumerate(inputs):
        value = (ref[0, place, :], ref[1, place, :])
        product = c_mul(value, (coef_ref[row, 2 * term], coef_ref[row, 2 * term + 1]))
        total = product if total is None else c_add(total, product)
    return total


def z_forward_kernel(terms, parts, slots, rows, coef_ref, matrix_ref, turn_ref, *refs):
    inputs = refs[: terms * parts]
    out_ref, held = refs[-2:]
    per_part = slots // parts
    tile = min(rows, 8)

    def step(index, carry):
        row = pl.multiple_of(index * tile, tile)
        values = []
        for h in range(slots):
            part, inner = divmod(h, per_part)
            place = pl.ds(inner * rows + row, tile)
            values.append(combine(inputs[part * terms : (part + 1) * terms], coef_ref, h, place))
        values = small_dft(values, -1)
        for k in range(slots):
            twiddle = (
                turn_ref[k, 0, pl.ds(row, tile), :],
                turn_ref[k, 1, pl.ds(row, tile), :],
            )
            real_part, imag_part = c_mul(values[k], twiddle)
            held[pl.ds(row, tile), k * LANES : (k + 1) * LANES] = real_part
            held[pl.ds(rows + row, tile), k * LANES : (k + 1) * LANES] = imag_part
        return carry

    lax.fori_loop(0, rows // tile, step, 0)
    result = dot3(matrix_ref[0], matrix_ref[1], held[...], True)
    for k in range(slots):
        out_ref[k, 0] = result[:rows, k * LANES : (k + 1) * LANES]
        out_ref[k, 1] = result[rows:, k * LANES : (k + 1) * LANES]


def z_forward(parts, coef, turns, slots, rows):
    terms = len(parts[0])
    flat = [pair for part in parts for pair in part]
    matrix = jnp.asarray(dft_matrix(rows, -1, True))
    shape = (slots, 2, rows, LANES)
    return pl.pallas_call(
        functools.partial(z_forward_kernel, terms, len(parts), slots, rows),
        grid=(1,),
        out_shape=jax.ShapeDtypeStruct(shape, jnp.float32),
        in_specs=[
            pl.BlockSpec(memory_space=pltpu.SMEM),
            whole_spec(matrix.shape),
            whole_spec(turns.shape),
        ]
        + [spec for _, spec in flat],
        out_specs=whole_spec(shape),
        scratch_shapes=[pltpu.VMEM((2 * rows, slots * LANES), jnp.float32)],
        compiler_params=params(),
        cost_estimate=pl.CostEstimate(
            flops=700 * rows * rows * slots * LANES,
            bytes_accessed=32 * rows * slots * LANES,
            transcendentals=0,
        ),
        name="z_forward",
    )(coef, matrix, turns, *[array for array, _ in flat])


def z_inverse_kernel(parts, slots, rows, coef_ref, matrix_ref, turn_ref, in_ref, *refs):
    outputs, held = refs[:parts], refs[parts]
    per_part = slots // parts
    tile = min(rows, 8)
    for k in range(slots):
        held[:rows, k * LANES : (k + 1) * LANES] = in_ref[k, 0]
        held[rows:, k * LANES : (k + 1) * LANES] = in_ref[k, 1]
    held[...] = dot3(matrix_ref[0], matrix_ref[1], held[...], True)

    def step(index, carry):
        row = pl.multiple_of(index * tile, tile)
        values = []
        for k in range(slots):
            value = (
                held[pl.ds(row, tile), k * LANES : (k + 1) * LANES],
                held[pl.ds(rows + row, tile), k * LANES : (k + 1) * LANES],
            )
            twiddle = (
                turn_ref[k, 0, pl.ds(row, tile), :],
                -turn_ref[k, 1, pl.ds(row, tile), :],
            )
            values.append(c_mul(value, twiddle))
        values = small_dft(values, 1)
        for h in range(slots):
            part, inner = divmod(h, per_part)
            real_part, imag_part = c_mul(values[h], (coef_ref[h, 0], coef_ref[h, 1]))
            outputs[part][0, pl.ds(inner * rows + row, tile), :] = real_part
            outputs[part][1, pl.ds(inner * rows + row, tile), :] = imag_part
        return carry

    lax.fori_loop(0, rows // tile, step, 0)


def z_inverse(blocks, coef, turns, parts):
    slots, _, rows, _ = blocks.shape
    matrix = jnp.asarray(dft_matrix(rows, 1, True))
    shape = (2, slots // parts * rows, LANES)
    return pl.pallas_call(
        functools.partial(z_inverse_kernel, parts, slots, rows),
        grid=(1,),
        out_shape=[jax.ShapeDtypeStruct(shape, jnp.float32)] * parts,
        in_specs=[
            pl.BlockSpec(memory_space=pltpu.SMEM),
            whole_spec(matrix.shape),
            whole_spec(turns.shape),
            whole_spec(blocks.shape),
        ],
        out_specs=[whole_spec(shape)] * parts,
        scratch_shapes=[pltpu.VMEM((2 * rows, slots * LANES), jnp.float32)],
        compiler_params=params(),
        cost_estimate=pl.CostEstimate(
            flops=700 * rows * rows * slots * LANES,
            bytes_accessed=20 * rows * slots * LANES,
            transcendentals=0,
        ),
        name="z_inverse",
    )(coef, matrix, turns, blocks)


def x_filter_kernel(slots, chunks, rows, forward_ref, inverse_ref, turn_ref, green_ref, *refs):
    inputs = refs[:chunks]
    outputs = refs[chunks : 2 * chunks]
    held = refs[-1]
    tile = 8
    modes = slots * chunks

    def before(index, carry):
        row = pl.multiple_of(index * tile, tile)
        place = pl.ds(row, tile)
        columns = []
        for c in range(chunks):
            values = [
                (inputs[c][k, 0, place, :], inputs[c][k, 1, place, :]) for k in range(slots)
            ]
            values = small_dft(values, -1)
            columns.append([c_const(values[a], a * c, modes, -1) for a in range(slots)])
        for a in range(slots):
            values = small_dft([columns[c][a] for c in range(chunks)], -1)
            for b in range(chunks):
                mode = a + slots * b
                twiddle = (turn_ref[0, mode : mode + 1, :], turn_ref[1, mode : mode + 1, :])
                real_part, imag_part = c_mul(values[b], twiddle)
                held[mode, place, :LANES] = real_part
                held[mode, place, LANES:] = imag_part
        return carry

    lax.fori_loop(0, rows // tile, before, 0)

    group = max(1, min(modes, 256 // rows))

    def middle(index, carry):
        mode = pl.multiple_of(index * group, group)
        value = held[pl.ds(mode, group)].reshape(group * rows, 2 * LANES)
        value = dot3(forward_ref[0], forward_ref[1], value, False)
        green = green_ref[pl.ds(mode, group)].reshape(group * rows, LANES)
        value = value * jnp.concatenate([green, green], axis=1)
        value = dot3(inverse_ref[0], inverse_ref[1], value, False)
        held[pl.ds(mode, group)] = value.reshape(group, rows, 2 * LANES)
        return carry

    lax.fori_loop(0, modes // group, middle, 0)

    def after(index, carry):
        row = pl.multiple_of(index * tile, tile)
        place = pl.ds(row, tile)
        columns = []
        for a in range(slots):
            values = []
            for b in range(chunks):
                mode = a + slots * b
                twiddle = (turn_ref[0, mode : mode + 1, :], -turn_ref[1, mode : mode + 1, :])
                values.append(c_mul((held[mode, place, :LANES], held[mode, place, LANES:]), twiddle))
            columns.append(small_dft(values, 1))
        for c in range(chunks):
            values = [c_const(columns[a][c], a * c, modes, 1) for a in range(slots)]
            values = small_dft(values, 1)
            for k in range(slots):
                outputs[c][k, 0, place, :] = values[k][0]
                outputs[c][k, 1, place, :] = values[k][1]
        return carry

    lax.fori_loop(0, rows // tile, after, 0)


def x_filter(blocks, turns, green):
    chunks = len(blocks)
    slots, _, rows, _ = blocks[0].shape
    step = min(rows, 32)
    modes = slots * chunks
    forward = jnp.asarray(dft_matrix(LANES, -1, False))
    inverse = jnp.asarray(dft_matrix(LANES, 1, False))
    block = pl.BlockSpec((slots, 2, step, LANES), lambda i: (0, 0, i, 0))
    return pl.pallas_call(
        functools.partial(x_filter_kernel, slots, chunks, step),
        grid=(rows // step,),
        out_shape=[jax.ShapeDtypeStruct(blocks[0].shape, jnp.float32)] * chunks,
        in_specs=[
            whole_spec(forward.shape),
            whole_spec(inverse.shape),
            whole_spec(turns.shape),
            pl.BlockSpec((modes, step, LANES), lambda i: (0, i, 0)),
        ]
        + [block] * chunks,
        out_specs=[block] * chunks,
        scratch_shapes=[pltpu.VMEM((modes, step, 2 * LANES), jnp.float32)],
        compiler_params=params(),
        cost_estimate=pl.CostEstimate(
            flops=96 * LANES * LANES * modes * rows,
            bytes_accessed=20 * modes * rows * LANES,
            transcendentals=0,
        ),
        name="x_filter",
    )(forward, inverse, turns, green, *blocks)


def mix_kernel(terms, parts, coef_ref, *refs):
    for part in range(parts):
        out_ref = refs[terms * parts + part]
        inputs = refs[part * terms : (part + 1) * terms]
        total = combine(inputs, coef_ref, part, slice(None))
        out_ref[0], out_ref[1] = total


def mix(parts, coef, rows):
    terms = len(parts[0])
    flat = [pair for part in parts for pair in part]
    steps = 4 if rows % 32 == 0 else 1
    return pl.pallas_call(
        functools.partial(mix_kernel, terms, len(parts)),
        grid=(steps,),
        out_shape=[jax.ShapeDtypeStruct((2, rows, LANES), jnp.float32)] * len(parts),
        in_specs=[pl.BlockSpec(memory_space=pltpu.SMEM)] + [make(steps) for _, make in flat],
        out_specs=[pl.BlockSpec((2, rows // steps, LANES), lambda i: (0, i, 0))] * len(parts),
        compiler_params=params(),
        cost_estimate=pl.CostEstimate(
            flops=20 * rows * LANES * len(parts),
            bytes_accessed=MIX_WEIGHT * rows * LANES * len(parts),
            transcendentals=0,
        ),
        name="mix",
    )(coef, *[array for array, _ in flat])


def finish_kernel(terms, parts, coef_ref, *refs):
    out_ref = refs[-1]
    for part in range(parts):
        inputs = refs[part * terms : (part + 1) * terms]
        total = combine(inputs, coef_ref, part, slice(None))
        out_ref[0, part], out_ref[1, part] = total


def finish(parts, coef, chunk, chunks, so_far):
    terms = len(parts[0])
    flat = [array for part in parts for array in part]
    rows = parts[0][0].shape[1]
    steps = 4 if rows % 32 == 0 else 1
    extra = [] if so_far is None else [so_far]
    return pl.pallas_call(
        functools.partial(finish_kernel, terms, len(parts)),
        grid=(steps,),
        out_shape=jax.ShapeDtypeStruct((2, len(parts), rows, chunks * LANES), jnp.float32),
        in_specs=[pl.BlockSpec(memory_space=pltpu.SMEM)]
        + [pl.BlockSpec((2, rows // steps, LANES), lambda i: (0, i, 0))] * len(flat)
        + [pl.BlockSpec(memory_space=pl.ANY)] * len(extra),
        out_specs=pl.BlockSpec((2, len(parts), rows // steps, LANES), lambda i: (0, 0, i, chunk)),
        input_output_aliases={1 + len(flat): 0} if extra else {},
        compiler_params=params(),
        cost_estimate=pl.CostEstimate(
            flops=20 * rows * LANES * len(parts),
            bytes_accessed=32 * rows * LANES * len(parts),
            transcendentals=0,
        ),
        name="finish",
    )(coef, *flat, *extra)


def after(value, *others):
    return lax.optimization_barrier((value, others))[0]


def swap(value, axis, mask):
    pairs = [(source, source ^ mask) for source in range(lax.axis_size(axis))]
    return lax.ppermute(value, axis, pairs)


def trade(blocks):
    return lax.all_to_all(blocks, "wide", 0, 0, tiled=True)


def narrow_terms(orient, length):
    give, keep = [], []
    for device in range(4):
        for first in FIRSTS:
            there = device ^ (3 - first)
            unit = orient * (length // 4)
            give.append([there * device * unit, there * (device ^ first) * unit])
            keep.append([device * device * unit, device * (device ^ first) * unit, 0])
    shape = (4, len(FIRSTS), -1)
    return np.array(give).reshape(shape), np.array(keep).reshape(shape)


def pick(table, index):
    return lax.dynamic_index_in_dim(jnp.asarray(table), index, 0, keepdims=False)


def reversed_index(device, bit_count):
    result = jnp.int32(0)
    for level in range(bit_count):
        result = result + device // (1 << level) % 2 * (1 << bit_count - 1 - level)
    return result


def rotate(field, phase_angle, orient):
    return jnp.stack(
        c_mul((field[0], field[1]), (jnp.cos(phase_angle), -orient * jnp.sin(phase_angle)))
    )


def butterfly_forward(field, device, bit_count):
    for level in reversed(range(bit_count)):
        half_size = 1 << level
        partner = swap(field, "narrow", half_size)
        upper = device // half_size % 2
        phase_angle = (device % half_size).astype(jnp.float32) * (math.pi / half_size)
        field = jnp.where(upper == 0, field + partner, rotate(partner - field, phase_angle, 1.0))
    return field


def butterfly_inverse(field, device, bit_count):
    for level in range(bit_count):
        half_size = 1 << level
        partner = swap(field, "narrow", half_size)
        upper = device // half_size % 2
        phase_angle = (device % half_size).astype(jnp.float32) * (math.pi / half_size)
        turned = rotate(jnp.where(upper == 0, partner, field), phase_angle, -1.0)
        field = jnp.where(upper == 0, field + turned, partner - turned)
    return field


def green_values(plane_wave, wave_z, modes, total_z, total_x):
    signed_z = jnp.where(wave_z < total_z // 2, wave_z, wave_z - total_z)
    wave_x = jnp.arange(modes)[:, None] + modes * jnp.arange(total_x // modes)[None, :]
    signed_x = jnp.where(wave_x < total_x // 2, wave_x, wave_x - total_x)
    square = signed_z[None, :, None] ** 2 + plane_wave**2 + signed_x[:, None, :] ** 2
    square = square.astype(jnp.float32)
    green = 1.0 / (1.0 + square / float(SCREEN * SCREEN)) + float(AMP) / (square + 1.0)
    return green * (1.0 / (total_x * total_z))


def plane(density, plane_wave):
    narrow, wide = lax.axis_size("narrow"), lax.axis_size("wide")
    bits = narrow.bit_length() - 1
    device, place = lax.axis_index("narrow"), lax.axis_index("wide")
    z_local, x_local = density.shape[1:]
    total_z, total_x = z_local * narrow, x_local * wide
    rows = z_local // wide
    chunks = x_local // LANES
    modes = wide * chunks
    four = narrow == 4
    low_wave = device if four else reversed_index(device, bits)
    parts = 2 if four else 1
    half = z_local // parts

    waves = [d if four else int(format(d, "b").zfill(bits)[::-1], 2) for d in range(narrow)]
    waves = np.array(waves)
    block = waves[:, None] + narrow * np.arange(wide)
    turns = turn(np.arange(rows) * block[..., None], total_z)
    turns = pick(np.moveaxis(turns, 3, 2), device)
    turns = jnp.broadcast_to(turns[..., None], (wide, 2, rows, LANES))
    head = np.arange(wide) * waves[:, None]
    inner = pick(turn(-head, narrow * wide), device)
    if four:
        give, keep = narrow_terms(1, narrow * wide)
        outer = np.repeat(keep, wide // 2, axis=1) + head[..., None]
        outer = pick(turn(outer, narrow * wide).reshape(narrow, wide, 6), device)
        give = pick(turn(give, narrow * wide).reshape(narrow, 2, 4), device)
        give_back, keep = narrow_terms(-1, narrow * wide)
        give_back = pick(turn(give_back, narrow * wide).reshape(narrow, 2, 4), device)
        last = pick(turn(keep, narrow * wide).reshape(narrow, 2, 6), device)
    else:
        outer = pick(turn(head, narrow * wide), device)
        last = jnp.array([[1.0, 0.0]], jnp.float32)
    x_turns = turn(np.arange(modes)[:, None] * np.arange(LANES)[None, :], total_x)
    x_turns = jnp.asarray(np.moveaxis(x_turns, 2, 0))
    line = jnp.arange(rows, dtype=jnp.int32)
    wave_z = low_wave + narrow * (place + wide * line)
    green = green_values(plane_wave, wave_z, modes, total_z, total_x)

    def part_spec(part, chunk):
        def make(steps):
            first = part * steps
            return pl.BlockSpec((2, half // steps, LANES), lambda i: (0, first + i, chunk))

        return make

    def own_spec(steps):
        return pl.BlockSpec((2, half // steps, LANES), lambda i: (0, i, 0))

    def cut(c, source):
        columns = slice(c * LANES, (c + 1) * LANES)
        return [source[:, p * half : (p + 1) * half, columns] for p in range(parts)]

    def first_swap(pieces):
        return [swap(piece, "narrow", first) for piece, first in zip(pieces, FIRSTS)]

    def second_swap(pieces):
        return [swap(piece, "narrow", 3 - first) for piece, first in zip(pieces, FIRSTS)]

    arrived, pieces = [], [cut(0, density)]
    rest = after(density, pieces[0])
    pieces += [cut(c, rest) for c in range(1, chunks)]
    partner = received = sent = None
    for c in range(chunks):
        if four:
            if c == 0:
                partner = first_swap(pieces[0])
            else:
                partner = first_swap(after(pieces[c], received))
            ready = after(partner, sent) if c else partner
            mixed = mix(
                [[(density, part_spec(p, c)), (ready[p], own_spec)] for p in range(parts)], give, half
            )
            received = second_swap(mixed)
            terms = [
                [
                    (density, part_spec(p, c)(1)),
                    (partner[p], own_spec(1)),
                    (received[p], own_spec(1)),
                ]
                for p in range(parts)
            ]
        else:
            terms = [[(butterfly_forward(piece, device, bits), own_spec(1))] for piece in pieces[c]]
        sent = z_forward(terms, outer, turns, wide, rows)
        arrived.append(trade(sent))

    filtered = x_filter(arrived, x_turns, green)

    result, done = None, []
    for c in range(chunks):
        blocks = after(filtered[c], done[c - 2]) if four and c >= 2 else filtered[c]
        pieces = z_inverse(trade(blocks), inner, turns, parts)
        if four:
            partner = first_swap(pieces)
            ready = after(partner, received) if c else partner
            mixed = mix(
                [[(pieces[p], own_spec), (ready[p], own_spec)] for p in range(parts)], give_back, half
            )
            done.append(mixed)
            received = second_swap(mixed)
            pieces = [[pieces[p], partner[p], received[p]] for p in range(parts)]
        else:
            pieces = [[butterfly_inverse(piece, device, bits)] for piece in pieces]
        result = finish(pieces, last, c, chunks, result)
    return result.reshape(density.shape)


def shards(density, plane_wave):
    planes = [plane(density[:, y], plane_wave[y]) for y in range(density.shape[1])]
    return jnp.stack(planes, axis=1)


def solution(mesh):
    in_specs = (P(None, None, "narrow", "wide"), P())
    out_specs = P(None, None, "narrow", "wide")
    return jax.shard_map(shards, mesh=mesh, in_specs=in_specs, out_specs=out_specs, check_vma=False)
```

time: 473 us -> 356 us (0.75)
  starting transfers between devices: 135 us -> 63.1 us
  between operations: 60.9 us -> 1.06 us
  local copies, waits for them, and re-layouts: 54.9 us -> 23.8 us
  blocking collectives: 0 us -> 29 us
  waiting for transfers between devices: 149 us -> 169 us
  other arithmetic: 21 us -> 2.1 us
  Pallas kernels: 49.8 us -> 66.3 us
    ppermute x56 -> x0, starting transfers between devices: 91.5 us -> none  [shift(): return lax.ppermute(value, axis, pairs)]
    ppermute x56 -> x0, waiting for transfers between devices: 64.1 us -> none  [shift(): return lax.ppermute(value, axis, pairs)]
    ppermute x32, waiting for transfers between devices: 85.1 us -> 132 us  [swap(): return lax.ppermute(value, axis, pairs)]
    all_to_all x0 -> x7, waiting for transfers between devices: none -> 37 us  [trade(): return lax.all_to_all(blocks, 'wide', 0, 0, tiled=True)]
    unnamed x226 -> x84, local copies, waits for them, and re-layouts: 48.6 us -> 16.3 us
    all_to_all x0 -> x7, starting transfers between devices: none -> 29.4 us  [trade(): return lax.all_to_all(blocks, 'wide', 0, 0, tiled=True)]
    all_to_all x0 -> x1, blocking collectives: none -> 29 us  [trade(): return lax.all_to_all(blocks, 'wide', 0, 0, tiled=True)]
    pallas_call x4 -> x12, Pallas kernels: 8.23 us -> 23.6 us  [the longest x8 16 us: mix(): pl.pallas_call(functools.partial(mix_kernel, terms, len(parts)), grid=(st...]
  transfers between devices with their start and end apart: 88 -> 39, of which waited for: 29 -> 34; matrix products, arithmetic and copies ran while one was open for 5% -> 2% of each run, Pallas kernels for 6% -> 12%
where the time goes in v2:
time: 356 us; the launch traced here: 355 us
  waiting for transfers between devices  169 us (47%)
  Pallas kernels  66.3 us (19%)
  starting transfers between devices  63.1 us (18%)
  blocking collectives  29 us (8%)
  local copies, waits for them, and re-layouts  23.8 us (7%)
    ppermute x32, waiting for transfers between devices, swap(): return lax.ppermute(value, axis, pairs)  132 us
    all_to_all x7, waiting for transfers between devices, trade(): return lax.all_to_all(blocks, 'wide', 0, 0, tiled=True)  37 us
    ppermute x32, starting transfers between devices, swap(): return lax.ppermute(value, axis, pairs)  33.6 us
    all_to_all x7, starting transfers between devices, trade(): return lax.all_to_all(blocks, 'wide', 0, 0, tiled=True)  29.4 us
    all_to_all x1, blocking collectives, trade(): return lax.all_to_all(blocks, 'wide', 0, 0, tiled=True)  29 us
    pallas_call x1, Pallas kernels, x_filter(): pl.pallas_call(functools.partial(x_filter_kernel, slots, chunks, step), g...  16.3 us
    unnamed x84, local copies, waits for them, and re-layouts  16.3 us
    pallas_call x8, Pallas kernels, mix(): pl.pallas_call(functools.partial(mix_kernel, terms, len(parts)), grid=(st...  16 us
  transfers between devices with their start and end apart: 39, of which 34 were waited for; matrix products, arithmetic and copies ran while one was open for 2% of the time, Pallas kernels for 12%

profile of v2, /device:TPU:0, one launch (start us, length us, event | category | flops | bytes accessed | tf_op | source)
XLA Modules:
  0.0 354.7 jit_solution(285201880847749841)
XLA Ops:
  0.0 1.3 fusion.8
  1.3 3.0 collective-permute-start
  4.3 1.5 collective-permute-start.1
  6.5 9.7 %collective-permute-done.refs_1_ = f32[2,512,128]{2,1,0:T(8,128)S(1)} collective-permute-done((f32[2,512,128]{2,1,0:T(8,128)S(1)}, f32[2,512,128]{2,1,0:T(8,128)S(1)}, u32[]{:S(2)}, u32[]{:S(2)}) %collective-permute-start) | collective-permute-done | bytes 524320 | tf_op jit(solution)/shard_map/ppermute | solution.py:402
  16.2 1.5 collective-permute-done.1.refs_3_.refs_4_
  17.7 2.7 mix.8
  20.4 1.6 collective-permute-start.2
  23.9 1.7 fusion.7
  25.7 7.3 %collective-permute-done.2.refs_2_ = f32[2,512,128]{2,1,0:T(8,128)S(1)} collective-permute-done((f32[2,512,128]{2,1,0:T(8,128)S(1)}, f32[2,512,128]{2,1,0:T(8,128)S(1)}, u32[]{:S(2)}, u32[]{:S(2)}) %collective-permute-start.2) | collective-permute-done | bytes 524320 | tf_op jit(solution)/shard_map/ppermute | solution.py:402
  33.0 1.2 collective-permute-done.3.refs_5_
  35.8 4.0 %z_forward.4 = f32[8,2,128,128]{3,2,1,0:T(8,128)} custom-call(f32[8,6]{1,0:T(8,128)S(1)} %dynamic-slice_bitcast_fusion.1.coef_ref, bf16[2,256,256]{2,1,0:T(8,128)(2,1)S(1)} %copy-done.38, f32[8,2,128,128]{3,2,1,0:T(8,128)S(1)} %broadcast_in_dim.5.turn_ref, f32[2,1024,512]{2,1,0:T(8,128)} %bitcast.20, f32[2,512,128]{2,1,0:T(8,128)S(1)} %collective-permute-done.refs_1_, ...), custom_call_target="tpu_custom_call" | custom-call | flops 11744051200 | bytes 4194304 | tf_op jit(solution)/shard_map/z_forward/pallas_call | solution.py:158
  39.8 4.8 %all-to-all-start = ((f32[8,2,128,128]{3,2,1,0:T(8,128)}), f32[8,2,128,128]{3,2,1,0:T(8,128)S(1)}, u32[]{:S(2)}, u32[]{:S(2)}) async-start(f32[8,2,128,128]{3,2,1,0:T(8,128)} %z_forward.4), calls=%async_computation | async-start | bytes 2097152 | tf_op jit(solution)/shard_map/all_to_all | solution.py:406
  46.1 2.6 mix.9
  50.7 11.1 %collective-permute-done.6.refs_2_ = f32[2,512,128]{2,1,0:T(8,128)S(1)} collective-permute-done((f32[2,512,128]{2,1,0:T(8,128)S(1)}, f32[2,512,128]{2,1,0:T(8,128)S(1)}, u32[]{:S(2)}, u32[]{:S(2)}) %collective-permute-start.6) | collective-permute-done | bytes 524320 | tf_op jit(solution)/shard_map/ppermute | solution.py:402
  63.0 1.4 collective-permute-start.8
  67.0 3.7 %z_forward.5 = f32[8,2,128,128]{3,2,1,0:T(8,128)} custom-call(f32[8,6]{1,0:T(8,128)S(1)} %dynamic-slice_bitcast_fusion.1.coef_ref, bf16[2,256,256]{2,1,0:T(8,128)(2,1)S(1)} %copy-done.38, f32[8,2,128,128]{3,2,1,0:T(8,128)S(1)} %broadcast_in_dim.5.turn_ref, f32[2,1024,512]{2,1,0:T(8,128)} %bitcast.24, f32[2,512,128]{2,1,0:T(8,128)S(1)} %copy-done.24, ...), custom_call_target="tpu_custom_call" | custom-call | flops 11744051200 | bytes 4194304 | tf_op jit(solution)/shard_map/z_forward/pallas_call | solution.py:158
  71.2 4.2 %all-to-all-start.1 = ((f32[8,2,128,128]{3,2,1,0:T(8,128)}), f32[8,2,128,128]{3,2,1,0:T(8,128)}, u32[]{:S(2)}, u32[]{:S(2)}) async-start(f32[8,2,128,128]{3,2,1,0:T(8,128)} %z_forward.5), calls=%async_computation.1 | async-start | bytes 2097152 | tf_op jit(solution)/shard_map/all_to_all | solution.py:406
  75.8 1.5 collective-permute-done.9.refs_3_.refs_4_
  77.2 2.4 mix.10
  80.9 11.4 %collective-permute-done.10.refs_2_ = f32[2,512,128]{2,1,0:T(8,128)S(1)} collective-permute-done((f32[2,512,128]{2,1,0:T(8,128)S(1)}, f32[2,512,128]{2,1,0:T(8,128)S(1)}, u32[]{:S(2)}, u32[]{:S(2)}) %collective-permute-start.10) | collective-permute-done | bytes 524320 | tf_op jit(solution)/shard_map/ppermute | solution.py:402
  93.5 1.3 collective-permute-start.12
  95.3 3.6 %z_forward.6 = f32[8,2,128,128]{3,2,1,0:T(8,128)} custom-call(f32[8,6]{1,0:T(8,128)S(1)} %dynamic-slice_bitcast_fusion.1.coef_ref, bf16[2,256,256]{2,1,0:T(8,128)(2,1)S(1)} %copy-done.38, f32[8,2,128,128]{3,2,1,0:T(8,128)S(1)} %broadcast_in_dim.5.turn_ref, f32[2,1024,512]{2,1,0:T(8,128)} %bitcast.28, f32[2,512,128]{2,1,0:T(8,128)S(1)} %collective-permute-done.8.refs_1_, ...), custom_call_target="tpu_custom_call" | custom-call | flops 11744051200 | bytes 4194304 | tf_op jit(solution)/shard_map/z_forward/pallas_call | solution.py:158
  98.9 3.2 all-to-all-done.1.refs_1_
  102.1 4.3 %all-to-all-start.2 = ((f32[8,2,128,128]{3,2,1,0:T(8,128)}), f32[8,2,128,128]{3,2,1,0:T(8,128)}, u32[]{:S(2)}, u32[]{:S(2)}) async-start(f32[8,2,128,128]{3,2,1,0:T(8,128)} %z_forward.6), calls=%async_computation.2 | async-start | bytes 2097152 | tf_op jit(solution)/shard_map/all_to_all | solution.py:406
  106.5 1.5 collective-permute-done.13.refs_3_.refs_4_
  108.0 2.6 mix.11
  112.0 11.3 %collective-permute-done.14.refs_2_ = f32[2,512,128]{2,1,0:T(8,128)S(1)} collective-permute-done((f32[2,512,128]{2,1,0:T(8,128)S(1)}, f32[2,512,128]{2,1,0:T(8,128)S(1)}, u32[]{:S(2)}, u32[]{:S(2)}) %collective-permute-start.14) | collective-permute-done | bytes 524320 | tf_op jit(solution)/shard_map/ppermute | solution.py:402
  124.6 3.9 %z_forward.7 = f32[8,2,128,128]{3,2,1,0:T(8,128)} custom-call(f32[8,6]{1,0:T(8,128)S(1)} %dynamic-slice_bitcast_fusion.1.coef_ref, bf16[2,256,256]{2,1,0:T(8,128)(2,1)S(1)} %copy-done.38, f32[8,2,128,128]{3,2,1,0:T(8,128)S(1)} %broadcast_in_dim.5.turn_ref, f32[2,1024,512]{2,1,0:T(8,128)} %bitcast.32, f32[2,512,128]{2,1,0:T(8,128)} %collective-permute-done.12.refs_1_, ...), custom_call_target="tpu_custom_call" | custom-call | flops 11744051200 | bytes 4194304 | tf_op jit(solution)/shard_map/z_forward/pallas_call | solution.py:158
  128.5 4.5 %all-to-all-done.2.refs_2_ = f32[8,2,128,128]{3,2,1,0:T(8,128)} async-done(((f32[8,2,128,128]{3,2,1,0:T(8,128)}), f32[8,2,128,128]{3,2,1,0:T(8,128)}, u32[]{:S(2)}, u32[]{:S(2)}) %all-to-all-start.2) | async-done | bytes 1048608 | tf_op jit(solution)/shard_map/all_to_all | solution.py:406
  133.0 4.3 %all-to-all-start.3 = ((f32[8,2,128,128]{3,2,1,0:T(8,128)}), f32[8,2,128,128]{3,2,1,0:T(8,128)}, u32[]{:S(2)}, u32[]{:S(2)}) async-start(f32[8,2,128,128]{3,2,1,0:T(8,128)} %z_forward.7), calls=%async_computation.3 | async-start | bytes 2097152 | tf_op jit(solution)/shard_map/all_to_all | solution.py:406
  137.9 2.1 add_multiply_fusion.green_ref
  140.0 23.8 %all-to-all-done.3.refs_3_ = f32[8,2,128,128]{3,2,1,0:T(8,128)} async-done(((f32[8,2,128,128]{3,2,1,0:T(8,128)}), f32[8,2,128,128]{3,2,1,0:T(8,128)}, u32[]{:S(2)}, u32[]{:S(2)}) %all-to-all-start.3) | async-done | bytes 1048608 | tf_op jit(solution)/shard_map/all_to_all | solution.py:406
  163.8 16.3 %x_filter.1 = (f32[8,2,128,128]{3,2,1,0:T(8,128)S(1)}, f32[8,2,128,128]{3,2,1,0:T(8,128)}, f32[8,2,128,128]{3,2,1,0:T(8,128)}, f32[8,2,128,128]{3,2,1,0:T(8,128)}) custom-call(bf16[2,256,256]{2,1,0:T(8,128)(2,1)S(1)} %copy-done.37, bf16[2,256,256]{2,1,0:T(8,128)(2,1)S(1)} %copy-done.39, f32[2,32,128]{2,1,0:T(8,128)S(1)} %copy-done.40, ...), custom_call_target="tpu_custom_call" | custom-call | flops 6442450944 | bytes 10485760 | tf_op jit(solution)/shard_map/x_filter/pallas_call | solution.py:312
  180.2 29.0 %all_to_all.40.in_ref = f32[8,2,128,128]{3,2,1,0:T(8,128)S(1)} all-to-all(f32[8,2,128,128]{3,2,1,0:T(8,128)S(1)} %get-tuple-element.79), channel_id=1, replica_groups=mesh['wide'=8,'narrow'=4] {'wide'}, dimensions={0} | all-to-all | bytes 2097152 | tf_op jit(solution)/shard_map/all_to_all | solution.py:406
  209.2 3.6 %all-to-all-start.4 = ((f32[8,2,128,128]{3,2,1,0:T(8,128)}), f32[8,2,128,128]{3,2,1,0:T(8,128)S(1)}, u32[]{:S(2)}, u32[]{:S(2)}) async-start(f32[8,2,128,128]{3,2,1,0:T(8,128)} %get-tuple-element.76), calls=%async_computation.4 | async-start | bytes 2097152 | tf_op jit(solution)/shard_map/all_to_all | solution.py:406
  213.5 1.7 z_inverse.5
  215.3 1.4 collective-permute-start.18
  216.6 1.5 collective-permute-start.19
  218.8 10.7 %collective-permute-done.18.refs_1_ = f32[2,512,128]{2,1,0:T(8,128)S(1)} collective-permute-done((f32[2,512,128]{2,1,0:T(8,128)S(1)}, f32[2,512,128]{2,1,0:T(8,128)S(1)}, u32[]{:S(2)}, u32[]{:S(2)}) %collective-permute-start.18) | collective-permute-done | bytes 524320 | tf_op jit(solution)/shard_map/ppermute | solution.py:402
  234.3 5.0 %all-to-all-done.4.in_ref = f32[8,2,128,128]{3,2,1,0:T(8,128)S(1)} async-done(((f32[8,2,128,128]{3,2,1,0:T(8,128)}), f32[8,2,128,128]{3,2,1,0:T(8,128)S(1)}, u32[]{:S(2)}, u32[]{:S(2)}) %all-to-all-start.4) | async-done | bytes 1048608 | tf_op jit(solution)/shard_map/all_to_all | solution.py:406
  240.2 3.6 %all-to-all-start.7 = ((f32[8,2,128,128]{3,2,1,0:T(8,128)}), f32[8,2,128,128]{3,2,1,0:T(8,128)S(1)}, u32[]{:S(2)}, u32[]{:S(2)}) async-start(f32[8,2,128,128]{3,2,1,0:T(8,128)} %get-tuple-element.92), calls=%async_computation.7 | async-start | bytes 2097152 | tf_op jit(solution)/shard_map/all_to_all | solution.py:406
  245.0 1.7 z_inverse.4
  246.8 1.4 collective-permute-start.16
  248.2 1.5 collective-permute-start.17
  250.9 10.7 %collective-permute-done.16.refs_1_ = f32[2,512,128]{2,1,0:T(8,128)S(1)} collective-permute-done((f32[2,512,128]{2,1,0:T(8,128)S(1)}, f32[2,512,128]{2,1,0:T(8,128)S(1)}, u32[]{:S(2)}, u32[]{:S(2)}) %collective-permute-start.16) | collective-permute-done | bytes 524320 | tf_op jit(solution)/shard_map/ppermute | solution.py:402
  261.6 1.4 collective-permute-done.17.refs_3_.refs_4_
  262.9 10.4 %collective-permute-done.20.refs_2_ = f32[2,512,128]{2,1,0:T(8,128)S(1)} collective-permute-done((f32[2,512,128]{2,1,0:T(8,128)S(1)}, f32[2,512,128]{2,1,0:T(8,128)S(1)}, u32[]{:S(2)}, u32[]{:S(2)}) %collective-permute-start.20) | collective-permute-done | bytes 524320 | tf_op jit(solution)/shard_map/ppermute | solution.py:402
  277.8 4.7 %all-to-all-start.6 = ((f32[8,2,128,128]{3,2,1,0:T(8,128)}), f32[8,2,128,128]{3,2,1,0:T(8,128)}, u32[]{:S(2)}, u32[]{:S(2)}) async-start(f32[8,2,128,128]{3,2,1,0:T(8,128)} %get-tuple-element.88), calls=%async_computation.6 | async-start | bytes 2097152 | tf_op jit(solution)/shard_map/all_to_all | solution.py:406
  282.5 1.5 collective-permute-start.26
  287.2 1.7 z_inverse.7
  288.9 1.4 collective-permute-start.24
  290.8 6.6 %collective-permute-done.26.refs_2_ = f32[2,512,128]{2,1,0:T(8,128)S(1)} collective-permute-done((f32[2,512,128]{2,1,0:T(8,128)}, f32[2,512,128]{2,1,0:T(8,128)S(1)}, u32[]{:S(2)}, u32[]{:S(2)}) %collective-permute-start.26) | collective-permute-done | bytes 524320 | tf_op jit(solution)/shard_map/ppermute | solution.py:402
  299.8 9.7 %collective-permute-done.24.refs_1_ = f32[2,512,128]{2,1,0:T(8,128)S(1)} collective-permute-done((f32[2,512,128]{2,1,0:T(8,128)S(1)}, f32[2,512,128]{2,1,0:T(8,128)S(1)}, u32[]{:S(2)}, u32[]{:S(2)}) %collective-permute-start.24) | collective-permute-done | bytes 524320 | tf_op jit(solution)/shard_map/ppermute | solution.py:402
  309.5 2.3 mix.14
  315.1 2.4 z_inverse.6
  317.6 1.4 collective-permute-start.22
  319.0 1.5 collective-permute-start.23
  320.5 7.3 %collective-permute-done.28.refs_2_ = f32[2,512,128]{2,1,0:T(8,128)} collective-permute-done((f32[2,512,128]{2,1,0:T(8,128)}, f32[2,512,128]{2,1,0:T(8,128)}, u32[]{:S(2)}, u32[]{:S(2)}) %collective-permute-start.28) | collective-permute-done | bytes 524320 | tf_op jit(solution)/shard_map/ppermute | solution.py:402
  328.4 9.4 %collective-permute-done.22.refs_1_ = f32[2,512,128]{2,1,0:T(8,128)S(1)} collective-permute-done((f32[2,512,128]{2,1,0:T(8,128)S(1)}, f32[2,512,128]{2,1,0:T(8,128)S(1)}, u32[]{:S(2)}, u32[]{:S(2)}) %collective-permute-start.22) | collective-permute-done | bytes 524320 | tf_op jit(solution)/shard_map/ppermute | solution.py:402
  338.9 1.5 collective-permute-start.30
  341.8 2.5 finish.4.refs_6_
  344.4 2.5 finish.5.refs_6_
  346.8 3.7 %finish.6.refs_6_ = f32[2,2,512,512]{3,2,1,0:T(8,128)} custom-call(f32[2,6]{1,0:T(2,128)S(1)} %fusion.1.coef_ref, f32[2,512,128]{2,1,0:T(8,128)S(1)} %get-tuple-element.93.refs_0_, f32[2,512,128]{2,1,0:T(8,128)S(1)} %copy-done.1, f32[2,512,128]{2,1,0:T(8,128)} %collective-permute-done.28.refs_2_, ...), custom_call_target="tpu_custom_call", output_to_operand_aliasing={{}: (7, {})} | custom-call | flops 2621440 | bytes 4194304 | tf_op jit(solution)/shard_map/finish/pallas_call | solution.py:377
  352.3 2.5 finish.7
  (134 shorter events, 46.1 us)
Async XLA Ops:
  1.3 14.9 %collective-permute-start = (f32[2,512,128]{2,1,0:T(8,128)S(1)}, f32[2,512,128]{2,1,0:T(8,128)S(1)}, u32[]{:S(2)}, u32[]{:S(2)}) collective-permute-start(f32[2,512,128]{2,1,0:T(8,128)S(1)} %get-tuple-element.110), channel_id=1, source_target_pairs={{0,1},{1,0},{2,3},{3,2},{4,5},{5,4},{6,7},{7,6},{8,9},{9,8},{10,11... | collective-permute-start | bytes 1572872 | tf_op jit(solution)/shard_map/ppermute | solution.py:402
  4.3 13.4 %collective-permute-start.1 = (f32[2,512,128]{2,1,0:T(8,128)S(1)}, f32[2,512,128]{2,1,0:T(8,128)S(1)}, u32[]{:S(2)}, u32[]{:S(2)}) collective-permute-start(f32[2,512,128]{2,1,0:T(8,128)S(1)} %get-tuple-element.109), channel_id=1, source_target_pairs={{0,2},{1,3},{2,0},{3,1},{4,6},{5,7},{6,4},{7,5},{8,10},{9,11},{10,... | collective-permute-start | bytes 1572872 | tf_op jit(solution)/shard_map/ppermute | solution.py:402
  17.7 6.3 %copy-start.41 = (f32[2,1,1024,512]{3,2,1,0:T(8,128)S(1)}, f32[2,1,1024,512]{3,2,1,0:T(8,128)}, u32[]{:S(2)}) copy-start(f32[2,1,1024,512]{3,2,1,0:T(8,128)} %param.19) | copy-start | bytes 12582916
  20.4 12.5 %collective-permute-start.2 = (f32[2,512,128]{2,1,0:T(8,128)S(1)}, f32[2,512,128]{2,1,0:T(8,128)S(1)}, u32[]{:S(2)}, u32[]{:S(2)}) collective-permute-start(f32[2,512,128]{2,1,0:T(8,128)S(1)} %get-tuple-element.54), channel_id=1, source_target_pairs={{0,2},{1,3},{2,0},{3,1},{4,6},{5,7},{6,4},{7,5},{8,10},{9,11},{10,... | collective-permute-start | bytes 1572872 | tf_op jit(solution)/shard_map/ppermute | solution.py:402
  22.0 12.2 %collective-permute-start.3 = (f32[2,512,128]{2,1,0:T(8,128)S(1)}, f32[2,512,128]{2,1,0:T(8,128)S(1)}, u32[]{:S(2)}, u32[]{:S(2)}) collective-permute-start(f32[2,512,128]{2,1,0:T(8,128)S(1)} %get-tuple-element.55), channel_id=1, source_target_pairs={{0,1},{1,0},{2,3},{3,2},{4,5},{5,4},{6,7},{7,6},{8,9},{9,8},{10,11... | collective-permute-start | bytes 1572872 | tf_op jit(solution)/shard_map/ppermute | solution.py:402
  23.9 11.8 %copy-start.38 = (bf16[2,256,256]{2,1,0:T(8,128)(2,1)S(1)}, bf16[2,256,256]{2,1,0:T(8,128)(2,1)}, u32[]{:S(2)}) copy-start(bf16[2,256,256]{2,1,0:T(8,128)(2,1)} %constant.80.clone.matrix_ref.inverse_ref) | copy-start | bytes 786436
  34.2 11.5 %collective-permute-start.4 = (f32[2,512,128]{2,1,0:T(8,128)}, f32[2,512,128]{2,1,0:T(8,128)S(1)}, u32[]{:S(2)}, u32[]{:S(2)}) collective-permute-start(f32[2,512,128]{2,1,0:T(8,128)} %get-tuple-element.57), channel_id=1, source_target_pairs={{0,1},{1,0},{2,3},{3,2},{4,5},{5,4},{6,7},{7,6},{8,9},{9,8},{10,11... | collective-permute-start | bytes 1572872 | tf_op jit(solution)/shard_map/ppermute | solution.py:402
  34.8 11.3 %collective-permute-start.5 = (f32[2,512,128]{2,1,0:T(8,128)}, f32[2,512,128]{2,1,0:T(8,128)S(1)}, u32[]{:S(2)}, u32[]{:S(2)}) collective-permute-start(f32[2,512,128]{2,1,0:T(8,128)} %get-tuple-element.58), channel_id=1, source_target_pairs={{0,2},{1,3},{2,0},{3,1},{4,6},{5,7},{6,4},{7,5},{8,10},{9,11},{10,... | collective-permute-start | bytes 1572872 | tf_op jit(solution)/shard_map/ppermute | solution.py:402
  35.7 208.0 %copy-start.12 = (f32[8,2,128,128]{3,2,1,0:T(8,128)}, f32[8,2,128,128]{3,2,1,0:T(8,128)S(1)}, u32[]{:S(2)}) copy-start(f32[8,2,128,128]{3,2,1,0:T(8,128)S(1)} %broadcast_in_dim.5.turn_ref) | copy-start | bytes 3145732
  39.8 31.4 %all-to-all-start = ((f32[8,2,128,128]{3,2,1,0:T(8,128)}), f32[8,2,128,128]{3,2,1,0:T(8,128)S(1)}, u32[]{:S(2)}, u32[]{:S(2)}) async-start(f32[8,2,128,128]{3,2,1,0:T(8,128)} %z_forward.4), calls=%async_computation | async-start | bytes 2097152 | tf_op jit(solution)/shard_map/all_to_all | solution.py:406
  45.7 3.0 copy-start.23
  46.1 2.6 copy-start.25
  48.7 13.1 %collective-permute-start.6 = (f32[2,512,128]{2,1,0:T(8,128)S(1)}, f32[2,512,128]{2,1,0:T(8,128)S(1)}, u32[]{:S(2)}, u32[]{:S(2)}) collective-permute-start(f32[2,512,128]{2,1,0:T(8,128)S(1)} %get-tuple-element.61), channel_id=1, source_target_pairs={{0,2},{1,3},{2,0},{3,1},{4,6},{5,7},{6,4},{7,5},{8,10},{9,11},{10,... | collective-permute-start | bytes 1572872 | tf_op jit(solution)/shard_map/ppermute | solution.py:402
  49.6 13.4 %collective-permute-start.7 = (f32[2,512,128]{2,1,0:T(8,128)S(1)}, f32[2,512,128]{2,1,0:T(8,128)S(1)}, u32[]{:S(2)}, u32[]{:S(2)}) collective-permute-start(f32[2,512,128]{2,1,0:T(8,128)S(1)} %get-tuple-element.62), channel_id=1, source_target_pairs={{0,1},{1,0},{2,3},{3,2},{4,5},{5,4},{6,7},{7,6},{8,9},{9,8},{10,11... | collective-permute-start | bytes 1572872 | tf_op jit(solution)/shard_map/ppermute | solution.py:402
  63.0 12.8 %collective-permute-start.8 = (f32[2,512,128]{2,1,0:T(8,128)}, f32[2,512,128]{2,1,0:T(8,128)S(1)}, u32[]{:S(2)}, u32[]{:S(2)}) collective-permute-start(f32[2,512,128]{2,1,0:T(8,128)} %get-tuple-element.63), channel_id=1, source_target_pairs={{0,1},{1,0},{2,3},{3,2},{4,5},{5,4},{6,7},{7,6},{8,9},{9,8},{10,11... | collective-permute-start | bytes 1572872 | tf_op jit(solution)/shard_map/ppermute | solution.py:402
  64.4 12.8 %collective-permute-start.9 = (f32[2,512,128]{2,1,0:T(8,128)}, f32[2,512,128]{2,1,0:T(8,128)S(1)}, u32[]{:S(2)}, u32[]{:S(2)}) collective-permute-start(f32[2,512,128]{2,1,0:T(8,128)} %get-tuple-element.64), channel_id=1, source_target_pairs={{0,2},{1,3},{2,0},{3,1},{4,6},{5,7},{6,4},{7,5},{8,10},{9,11},{10,... | collective-permute-start | bytes 1572872 | tf_op jit(solution)/shard_map/ppermute | solution.py:402
  71.2 30.9 %all-to-all-start.1 = ((f32[8,2,128,128]{3,2,1,0:T(8,128)}), f32[8,2,128,128]{3,2,1,0:T(8,128)}, u32[]{:S(2)}, u32[]{:S(2)}) async-start(f32[8,2,128,128]{3,2,1,0:T(8,128)} %z_forward.5), calls=%async_computation.1 | async-start | bytes 2097152 | tf_op jit(solution)/shard_map/all_to_all | solution.py:406
  79.6 12.6 %collective-permute-start.10 = (f32[2,512,128]{2,1,0:T(8,128)S(1)}, f32[2,512,128]{2,1,0:T(8,128)S(1)}, u32[]{:S(2)}, u32[]{:S(2)}) collective-permute-start(f32[2,512,128]{2,1,0:T(8,128)S(1)} %get-tuple-element.67), channel_id=1, source_target_pairs={{0,2},{1,3},{2,0},{3,1},{4,6},{5,7},{6,4},{7,5},{8,10},{9,11},{10,... | collective-permute-start | bytes 1572872 | tf_op jit(solution)/shard_map/ppermute | solution.py:402
  80.3 13.2 %collective-permute-start.11 = (f32[2,512,128]{2,1,0:T(8,128)S(1)}, f32[2,512,128]{2,1,0:T(8,128)S(1)}, u32[]{:S(2)}, u32[]{:S(2)}) collective-permute-start(f32[2,512,128]{2,1,0:T(8,128)S(1)} %get-tuple-element.68), channel_id=1, source_target_pairs={{0,1},{1,0},{2,3},{3,2},{4,5},{5,4},{6,7},{7,6},{8,9},{9,8},{10,11... | collective-permute-start | bytes 1572872 | tf_op jit(solution)/shard_map/ppermute | solution.py:402
  93.5 13.0 %collective-permute-start.12 = (f32[2,512,128]{2,1,0:T(8,128)}, f32[2,512,128]{2,1,0:T(8,128)}, u32[]{:S(2)}, u32[]{:S(2)}) collective-permute-start(f32[2,512,128]{2,1,0:T(8,128)} %get-tuple-element.69), channel_id=1, source_target_pairs={{0,1},{1,0},{2,3},{3,2},{4,5},{5,4},{6,7},{7,6},{8,9},{9,8},{10,11... | collective-permute-start | bytes 1572872 | tf_op jit(solution)/shard_map/ppermute | solution.py:402
  94.8 13.2 %collective-permute-start.13 = (f32[2,512,128]{2,1,0:T(8,128)}, f32[2,512,128]{2,1,0:T(8,128)}, u32[]{:S(2)}, u32[]{:S(2)}) collective-permute-start(f32[2,512,128]{2,1,0:T(8,128)} %get-tuple-element.70), channel_id=1, source_target_pairs={{0,2},{1,3},{2,0},{3,1},{4,6},{5,7},{6,4},{7,5},{8,10},{9,11},{10,... | collective-permute-start | bytes 1572872 | tf_op jit(solution)/shard_map/ppermute | solution.py:402
  102.1 30.9 %all-to-all-start.2 = ((f32[8,2,128,128]{3,2,1,0:T(8,128)}), f32[8,2,128,128]{3,2,1,0:T(8,128)}, u32[]{:S(2)}, u32[]{:S(2)}) async-start(f32[8,2,128,128]{3,2,1,0:T(8,128)} %z_forward.6), calls=%async_computation.2 | async-start | bytes 2097152 | tf_op jit(solution)/shard_map/all_to_all | solution.py:406
  110.6 12.7 %collective-permute-start.14 = (f32[2,512,128]{2,1,0:T(8,128)S(1)}, f32[2,512,128]{2,1,0:T(8,128)S(1)}, u32[]{:S(2)}, u32[]{:S(2)}) collective-permute-start(f32[2,512,128]{2,1,0:T(8,128)S(1)} %get-tuple-element.73), channel_id=1, source_target_pairs={{0,2},{1,3},{2,0},{3,1},{4,6},{5,7},{6,4},{7,5},{8,10},{9,11},{10,... | collective-permute-start | bytes 1572872 | tf_op jit(solution)/shard_map/ppermute | solution.py:402
  111.3 13.3 %collective-permute-start.15 = (f32[2,512,128]{2,1,0:T(8,128)S(1)}, f32[2,512,128]{2,1,0:T(8,128)S(1)}, u32[]{:S(2)}, u32[]{:S(2)}) collective-permute-start(f32[2,512,128]{2,1,0:T(8,128)S(1)} %get-tuple-element.74), channel_id=1, source_target_pairs={{0,1},{1,0},{2,3},{3,2},{4,5},{5,4},{6,7},{7,6},{8,9},{9,8},{10,11... | collective-permute-start | bytes 1572872 | tf_op jit(solution)/shard_map/ppermute | solution.py:402
  128.5 35.3 %copy-start.37 = (bf16[2,256,256]{2,1,0:T(8,128)(2,1)S(1)}, bf16[2,256,256]{2,1,0:T(8,128)(2,1)}, u32[]{:S(2)}) copy-start(bf16[2,256,256]{2,1,0:T(8,128)(2,1)} %constant.81.clone.forward_ref.matrix_ref) | copy-start | bytes 786436
  128.5 35.3 %copy-start.39 = (bf16[2,256,256]{2,1,0:T(8,128)(2,1)S(1)}, bf16[2,256,256]{2,1,0:T(8,128)(2,1)}, u32[]{:S(2)}) copy-start(bf16[2,256,256]{2,1,0:T(8,128)(2,1)} %constant.80.clone.matrix_ref.inverse_ref) | copy-start | bytes 786436
  128.5 35.3 %copy-start.40 = (f32[2,32,128]{2,1,0:T(8,128)S(1)}, f32[2,32,128]{2,1,0:T(8,128)}, u32[]{:S(2)}) copy-start(f32[2,32,128]{2,1,0:T(8,128)} %constant.79.clone.turn_ref) | copy-start | bytes 98308
  133.0 30.9 %all-to-all-start.3 = ((f32[8,2,128,128]{3,2,1,0:T(8,128)}), f32[8,2,128,128]{3,2,1,0:T(8,128)}, u32[]{:S(2)}, u32[]{:S(2)}) async-start(f32[8,2,128,128]{3,2,1,0:T(8,128)} %z_forward.7), calls=%async_computation.3 | async-start | bytes 2097152 | tf_op jit(solution)/shard_map/all_to_all | solution.py:406
  209.2 30.1 %all-to-all-start.4 = ((f32[8,2,128,128]{3,2,1,0:T(8,128)}), f32[8,2,128,128]{3,2,1,0:T(8,128)S(1)}, u32[]{:S(2)}, u32[]{:S(2)}) async-start(f32[8,2,128,128]{3,2,1,0:T(8,128)} %get-tuple-element.76), calls=%async_computation.4 | async-start | bytes 2097152 | tf_op jit(solution)/shard_map/all_to_all | solution.py:406
  215.2 16.5 %copy-start.6 = (f32[2,512,128]{2,1,0:T(8,128)}, f32[2,512,128]{2,1,0:T(8,128)S(1)}, u32[]{:S(2)}) copy-start(f32[2,512,128]{2,1,0:T(8,128)S(1)} %get-tuple-element.81.refs_2_.refs_3_) | copy-start | bytes 1572868
  215.3 14.3 %collective-permute-start.18 = (f32[2,512,128]{2,1,0:T(8,128)S(1)}, f32[2,512,128]{2,1,0:T(8,128)S(1)}, u32[]{:S(2)}, u32[]{:S(2)}) collective-permute-start(f32[2,512,128]{2,1,0:T(8,128)S(1)} %get-tuple-element.80.refs_0_), channel_id=1, source_target_pairs={{0,1},{1,0},{2,3},{3,2},{4,5},{5,4},{6,7},{7,6},{8,9},{9,8},{10,11... | collective-permute-start | bytes 1572872 | tf_op jit(solution)/shard_map/ppermute | solution.py:402
  216.6 14.0 %collective-permute-start.19 = (f32[2,512,128]{2,1,0:T(8,128)S(1)}, f32[2,512,128]{2,1,0:T(8,128)S(1)}, u32[]{:S(2)}, u32[]{:S(2)}) collective-permute-start(f32[2,512,128]{2,1,0:T(8,128)S(1)} %get-tuple-element.81.refs_2_.refs_3_), channel_id=1, source_target_pairs={{0,2},{1,3},{2,0},{3,1},{4,6},{5,7},{6,4},{7,5},{8,10},{9,11},{10,... | collective-permute-start | bytes 1572872 | tf_op jit(solution)/shard_map/ppermute | solution.py:402
  229.6 4.7 %copy-start.8 = (f32[2,512,128]{2,1,0:T(8,128)}, f32[2,512,128]{2,1,0:T(8,128)S(1)}, u32[]{:S(2)}) copy-start(f32[2,512,128]{2,1,0:T(8,128)S(1)} %collective-permute-done.18.refs_1_) | copy-start | bytes 1572868
  230.6 3.6 %copy-start.10 = (f32[2,512,128]{2,1,0:T(8,128)}, f32[2,512,128]{2,1,0:T(8,128)S(1)}, u32[]{:S(2)}) copy-start(f32[2,512,128]{2,1,0:T(8,128)S(1)} %collective-permute-done.19.refs_3_.refs_4_) | copy-start | bytes 1572868
  240.2 37.6 %all-to-all-start.7 = ((f32[8,2,128,128]{3,2,1,0:T(8,128)}), f32[8,2,128,128]{3,2,1,0:T(8,128)S(1)}, u32[]{:S(2)}, u32[]{:S(2)}) async-start(f32[8,2,128,128]{3,2,1,0:T(8,128)} %get-tuple-element.92), calls=%async_computation.7 | async-start | bytes 2097152 | tf_op jit(solution)/shard_map/all_to_all | solution.py:406
  245.0 4.7 %copy-start.34 = (f32[2,512,128]{2,1,0:T(8,128)S(1)}, f32[2,512,128]{2,1,0:T(8,128)}, u32[]{:S(2)}) copy-start(f32[2,512,128]{2,1,0:T(8,128)} %copy-done.33) | copy-start | bytes 1572868
  245.0 5.2 %copy-start.32 = (f32[2,512,128]{2,1,0:T(8,128)S(1)}, f32[2,512,128]{2,1,0:T(8,128)}, u32[]{:S(2)}) copy-start(f32[2,512,128]{2,1,0:T(8,128)} %copy-done.31) | copy-start | bytes 1572868
  246.8 14.8 %collective-permute-start.16 = (f32[2,512,128]{2,1,0:T(8,128)S(1)}, f32[2,512,128]{2,1,0:T(8,128)S(1)}, u32[]{:S(2)}, u32[]{:S(2)}) collective-permute-start(f32[2,512,128]{2,1,0:T(8,128)S(1)} %get-tuple-element.77.refs_0_), channel_id=1, source_target_pairs={{0,1},{1,0},{2,3},{3,2},{4,5},{5,4},{6,7},{7,6},{8,9},{9,8},{10,11... | collective-permute-start | bytes 1572872 | tf_op jit(solution)/shard_map/ppermute | solution.py:402
  248.2 14.8 %collective-permute-start.17 = (f32[2,512,128]{2,1,0:T(8,128)S(1)}, f32[2,512,128]{2,1,0:T(8,128)S(1)}, u32[]{:S(2)}, u32[]{:S(2)}) collective-permute-start(f32[2,512,128]{2,1,0:T(8,128)S(1)} %get-tuple-element.78.refs_2_.refs_3_), channel_id=1, source_target_pairs={{0,2},{1,3},{2,0},{3,1},{4,6},{5,7},{6,4},{7,5},{8,10},{9,11},{10,... | collective-permute-start | bytes 1572872 | tf_op jit(solution)/shard_map/ppermute | solution.py:402
  249.7 23.7 %collective-permute-start.20 = (f32[2,512,128]{2,1,0:T(8,128)S(1)}, f32[2,512,128]{2,1,0:T(8,128)S(1)}, u32[]{:S(2)}, u32[]{:S(2)}) collective-permute-start(f32[2,512,128]{2,1,0:T(8,128)S(1)} %copy-done.34), channel_id=1, source_target_pairs={{0,2},{1,3},{2,0},{3,1},{4,6},{5,7},{6,4},{7,5},{8,10},{9,11},{10,... | collective-permute-start | bytes 1572872 | tf_op jit(solution)/shard_map/ppermute | solution.py:402
  250.2 24.0 %collective-permute-start.21 = (f32[2,512,128]{2,1,0:T(8,128)S(1)}, f32[2,512,128]{2,1,0:T(8,128)S(1)}, u32[]{:S(2)}, u32[]{:S(2)}) collective-permute-start(f32[2,512,128]{2,1,0:T(8,128)S(1)} %copy-done.32), channel_id=1, source_target_pairs={{0,1},{1,0},{2,3},{3,2},{4,5},{5,4},{6,7},{7,6},{8,9},{9,8},{10,11... | collective-permute-start | bytes 1572872 | tf_op jit(solution)/shard_map/ppermute | solution.py:402
  277.8 6.3 %copy-start.15 = (f32[8,2,128,128]{3,2,1,0:T(8,128)}, f32[8,2,128,128]{3,2,1,0:T(8,128)S(1)}, u32[]{:S(2)}) copy-start(f32[8,2,128,128]{3,2,1,0:T(8,128)S(1)} %all-to-all-done.7.in_ref) | copy-start | bytes 3145732
  277.8 36.1 %all-to-all-start.6 = ((f32[8,2,128,128]{3,2,1,0:T(8,128)}), f32[8,2,128,128]{3,2,1,0:T(8,128)}, u32[]{:S(2)}, u32[]{:S(2)}) async-start(f32[8,2,128,128]{3,2,1,0:T(8,128)} %get-tuple-element.88), calls=%async_computation.6 | async-start | bytes 2097152 | tf_op jit(solution)/shard_map/all_to_all | solution.py:406
  282.5 14.9 %collective-permute-start.26 = (f32[2,512,128]{2,1,0:T(8,128)}, f32[2,512,128]{2,1,0:T(8,128)S(1)}, u32[]{:S(2)}, u32[]{:S(2)}) collective-permute-start(f32[2,512,128]{2,1,0:T(8,128)} %copy-done.36), channel_id=1, source_target_pairs={{0,2},{1,3},{2,0},{3,1},{4,6},{5,7},{6,4},{7,5},{8,10},{9,11},{10,... | collective-permute-start | bytes 1572872 | tf_op jit(solution)/shard_map/ppermute | solution.py:402
  284.0 15.0 %collective-permute-start.27 = (f32[2,512,128]{2,1,0:T(8,128)}, f32[2,512,128]{2,1,0:T(8,128)S(1)}, u32[]{:S(2)}, u32[]{:S(2)}) collective-permute-start(f32[2,512,128]{2,1,0:T(8,128)} %copy-done.35), channel_id=1, source_target_pairs={{0,1},{1,0},{2,3},{3,2},{4,5},{5,4},{6,7},{7,6},{8,9},{9,8},{10,11... | collective-permute-start | bytes 1572872 | tf_op jit(solution)/shard_map/ppermute | solution.py:402
  288.9 20.6 %collective-permute-start.24 = (f32[2,512,128]{2,1,0:T(8,128)S(1)}, f32[2,512,128]{2,1,0:T(8,128)S(1)}, u32[]{:S(2)}, u32[]{:S(2)}) collective-permute-start(f32[2,512,128]{2,1,0:T(8,128)S(1)} %get-tuple-element.93.refs_0_), channel_id=1, source_target_pairs={{0,1},{1,0},{2,3},{3,2},{4,5},{5,4},{6,7},{7,6},{8,9},{9,8},{10,11... | collective-permute-start | bytes 1572872 | tf_op jit(solution)/shard_map/ppermute | solution.py:402
  290.3 19.2 %collective-permute-start.25 = (f32[2,512,128]{2,1,0:T(8,128)S(1)}, f32[2,512,128]{2,1,0:T(8,128)S(1)}, u32[]{:S(2)}, u32[]{:S(2)}) collective-permute-start(f32[2,512,128]{2,1,0:T(8,128)S(1)} %get-tuple-element.94.refs_2_.refs_3_), channel_id=1, source_target_pairs={{0,2},{1,3},{2,0},{3,1},{4,6},{5,7},{6,4},{7,5},{8,10},{9,11},{10,... | collective-permute-start | bytes 1572872 | tf_op jit(solution)/shard_map/ppermute | solution.py:402
  309.5 2.3 copy-start.2
  312.7 15.2 %collective-permute-start.28 = (f32[2,512,128]{2,1,0:T(8,128)}, f32[2,512,128]{2,1,0:T(8,128)}, u32[]{:S(2)}, u32[]{:S(2)}) collective-permute-start(f32[2,512,128]{2,1,0:T(8,128)} %get-tuple-element.97), channel_id=1, source_target_pairs={{0,2},{1,3},{2,0},{3,1},{4,6},{5,7},{6,4},{7,5},{8,10},{9,11},{10,... | collective-permute-start | bytes 1572872 | tf_op jit(solution)/shard_map/ppermute | solution.py:402
  313.2 15.2 %collective-permute-start.29 = (f32[2,512,128]{2,1,0:T(8,128)}, f32[2,512,128]{2,1,0:T(8,128)}, u32[]{:S(2)}, u32[]{:S(2)}) collective-permute-start(f32[2,512,128]{2,1,0:T(8,128)} %get-tuple-element.98), channel_id=1, source_target_pairs={{0,1},{1,0},{2,3},{3,2},{4,5},{5,4},{6,7},{7,6},{8,9},{9,8},{10,11... | collective-permute-start | bytes 1572872 | tf_op jit(solution)/shard_map/ppermute | solution.py:402
  315.1 26.7 %copy-start.28 = (f32[2,512,128]{2,1,0:T(8,128)S(1)}, f32[2,512,128]{2,1,0:T(8,128)}, u32[]{:S(2)}) copy-start(f32[2,512,128]{2,1,0:T(8,128)} %copy-done.27) | copy-start | bytes 1572868
  315.1 26.7 %copy-start.30 = (f32[2,512,128]{2,1,0:T(8,128)S(1)}, f32[2,512,128]{2,1,0:T(8,128)}, u32[]{:S(2)}) copy-start(f32[2,512,128]{2,1,0:T(8,128)} %copy-done.29) | copy-start | bytes 1572868
  317.6 24.2 %copy-start.5 = (f32[2,512,128]{2,1,0:T(8,128)S(1)}, f32[2,512,128]{2,1,0:T(8,128)}, u32[]{:S(2)}) copy-start(f32[2,512,128]{2,1,0:T(8,128)} %copy-done.4) | copy-start | bytes 1572868
  317.6 24.2 %copy-start.7 = (f32[2,512,128]{2,1,0:T(8,128)S(1)}, f32[2,512,128]{2,1,0:T(8,128)}, u32[]{:S(2)}) copy-start(f32[2,512,128]{2,1,0:T(8,128)} %copy-done.6) | copy-start | bytes 1572868
  317.6 24.2 %copy-start.9 = (f32[2,512,128]{2,1,0:T(8,128)S(1)}, f32[2,512,128]{2,1,0:T(8,128)}, u32[]{:S(2)}) copy-start(f32[2,512,128]{2,1,0:T(8,128)} %copy-done.8) | copy-start | bytes 1572868
  317.6 24.2 %copy-start.11 = (f32[2,512,128]{2,1,0:T(8,128)S(1)}, f32[2,512,128]{2,1,0:T(8,128)}, u32[]{:S(2)}) copy-start(f32[2,512,128]{2,1,0:T(8,128)} %copy-done.10) | copy-start | bytes 1572868
  317.6 20.2 %collective-permute-start.22 = (f32[2,512,128]{2,1,0:T(8,128)S(1)}, f32[2,512,128]{2,1,0:T(8,128)S(1)}, u32[]{:S(2)}, u32[]{:S(2)}) collective-permute-start(f32[2,512,128]{2,1,0:T(8,128)S(1)} %get-tuple-element.89.refs_0_), channel_id=1, source_target_pairs={{0,1},{1,0},{2,3},{3,2},{4,5},{5,4},{6,7},{7,6},{8,9},{9,8},{10,11... | collective-permute-start | bytes 1572872 | tf_op jit(solution)/shard_map/ppermute | solution.py:402
  319.0 18.8 %collective-permute-start.23 = (f32[2,512,128]{2,1,0:T(8,128)S(1)}, f32[2,512,128]{2,1,0:T(8,128)S(1)}, u32[]{:S(2)}, u32[]{:S(2)}) collective-permute-start(f32[2,512,128]{2,1,0:T(8,128)S(1)} %get-tuple-element.90.refs_2_.refs_3_), channel_id=1, source_target_pairs={{0,2},{1,3},{2,0},{3,1},{4,6},{5,7},{6,4},{7,5},{8,10},{9,11},{10,... | collective-permute-start | bytes 1572872 | tf_op jit(solution)/shard_map/ppermute | solution.py:402
  338.9 12.3 %collective-permute-start.30 = (f32[2,512,128]{2,1,0:T(8,128)S(1)}, f32[2,512,128]{2,1,0:T(8,128)S(1)}, u32[]{:S(2)}, u32[]{:S(2)}) collective-permute-start(f32[2,512,128]{2,1,0:T(8,128)S(1)} %get-tuple-element.101), channel_id=1, source_target_pairs={{0,2},{1,3},{2,0},{3,1},{4,6},{5,7},{6,4},{7,5},{8,10},{9,11},{10,... | collective-permute-start | bytes 1572872 | tf_op jit(solution)/shard_map/ppermute | solution.py:402
  340.4 11.9 %collective-permute-start.31 = (f32[2,512,128]{2,1,0:T(8,128)S(1)}, f32[2,512,128]{2,1,0:T(8,128)S(1)}, u32[]{:S(2)}, u32[]{:S(2)}) collective-permute-start(f32[2,512,128]{2,1,0:T(8,128)S(1)} %get-tuple-element.102), channel_id=1, source_target_pairs={{0,1},{1,0},{2,3},{3,2},{4,5},{5,4},{6,7},{7,6},{8,9},{9,8},{10,11... | collective-permute-start | bytes 1572872 | tf_op jit(solution)/shard_map/ppermute | solution.py:402
  341.8 2.5 copy-start.20
  341.8 2.5 copy-start.22
  344.3 2.5 copy-start.1
  344.3 2.5 copy-start.3
  (17 other events, 16.2 us)

commit v3 on v2

--- a/solution.py
+++ b/solution.py
@@ -13,6 +13,9 @@
 AMP = 2048
 LANES = 128
 MIX_WEIGHT = 480
+LINE_WEIGHT = 3000
+MIDDLE_UNROLL = 4
+PLAN = ((0, 1), (2, 3))
 VMEM_LIMIT = 48 * 1024 * 1024
 FIRSTS = (1, 2)
 
@@ -456,14 +459,463 @@
     return field
 
 
+def green_of(plane_wave, wave_z, signed_x, total_z, total_x):
+    signed_z = jnp.where(wave_z < total_z // 2, wave_z, wave_z - total_z)
+    square = (signed_z**2 + plane_wave**2 + signed_x**2).astype(jnp.float32)
+    green = 1.0 / (1.0 + square / float(SCREEN * SCREEN)) + float(AMP) / (square + 1.0)
+    return green * (1.0 / (total_x * total_z))
+
+
 def green_values(plane_wave, wave_z, modes, total_z, total_x):
-    signed_z = jnp.where(wave_z < total_z // 2, wave_z, wave_z - total_z)
     wave_x = jnp.arange(modes)[:, None] + modes * jnp.arange(total_x // modes)[None, :]
     signed_x = jnp.where(wave_x < total_x // 2, wave_x, wave_x - total_x)
-    square = signed_z[None, :, None] ** 2 + plane_wave**2 + signed_x[:, None, :] ** 2
-    square = square.astype(jnp.float32)
-    green = 1.0 / (1.0 + square / float(SCREEN * SCREEN)) + float(AMP) / (square + 1.0)
-    return green * (1.0 / (total_x * total_z))
+    return green_of(plane_wave, wave_z[None, :, None], signed_x[:, None, :], total_z, total_x)
+
+
+GROUPS = 4
+WIDTH = LANES // GROUPS
+
+
+def fits(narrow, wide, z_local, x_local):
+    rows = z_local // GROUPS
+    return (
+        narrow == GROUPS
+        and x_local == GROUPS * LANES
+        and z_local % GROUPS == 0
+        and rows % (8 * narrow * wide) == 0
+        and rows == 8 * narrow * wide
+    )
+
+
+def swap_lanes(tiles):
+    lane = lax.broadcasted_iota(jnp.int32, tiles[0].shape, len(tiles[0].shape) - 1)
+    axis = len(tiles[0].shape) - 1
+    low = lane % (2 * WIDTH) < WIDTH
+    left = lane < 2 * WIDTH
+    first = [None] * 4
+    for a in range(2):
+        one, two = tiles[a], tiles[a + 2]
+        first[a] = jnp.where(left, one, pltpu.roll(two, 2 * WIDTH, axis))
+        first[a + 2] = jnp.where(left, pltpu.roll(one, 2 * WIDTH, axis), two)
+    second = [None] * 4
+    for b in (0, 2):
+        one, two = first[b], first[b + 1]
+        second[b] = jnp.where(low, one, pltpu.roll(two, WIDTH, axis))
+        second[b + 1] = jnp.where(low, pltpu.roll(one, LANES - WIDTH, axis), two)
+    return second
+
+
+def pick_lanes(tiles, which):
+    axis = len(tiles[0].shape) - 1
+    group = lax.broadcasted_iota(jnp.int32, tiles[0].shape, axis) // WIDTH
+    result = None
+    for g, tile in enumerate(tiles):
+        distance = (g - which) * WIDTH % LANES
+        moved = pltpu.roll(tile, distance, axis) if distance else tile
+        result = moved if result is None else jnp.where(group == g, moved, result)
+    return result
+
+
+def cut_kernel(which, place_ref, in_ref, *out_refs):
+    for k in range(GROUPS):
+        lanes = pl.ds(pl.multiple_of(place_ref[k] * LANES, LANES), LANES)
+        for part in range(2):
+            tiles = [in_ref[part, g, :, lanes] for g in range(GROUPS)]
+            if len(which) == 1:
+                out_refs[k][0, part] = pick_lanes(tiles, which[0])
+            else:
+                tiles = swap_lanes(tiles)
+                for index, q in enumerate(which):
+                    out_refs[k][index, part] = tiles[q]
+
+
+def cut_columns(density, places, which):
+    rows, columns = density.shape[2:]
+    step = min(rows, 128)
+    block = pl.BlockSpec((len(which), 2, step, LANES), lambda i: (0, 0, i, 0))
+    shape = jax.ShapeDtypeStruct((len(which), 2, rows, LANES), jnp.float32)
+    return pl.pallas_call(
+        functools.partial(cut_kernel, which),
+        grid=(rows // step,),
+        out_shape=[shape] * GROUPS,
+        in_specs=[
+            pl.BlockSpec(memory_space=pltpu.SMEM),
+            pl.BlockSpec((2, GROUPS, step, columns), lambda i: (0, 0, i, 0)),
+        ],
+        out_specs=[block] * GROUPS,
+        compiler_params=params(),
+        cost_estimate=pl.CostEstimate(
+            flops=8 * rows * columns * len(which),
+            bytes_accessed=40 * rows * columns,
+            transcendentals=0,
+        ),
+        name="cut",
+    )(places, density)
+
+
+def place_kernel(chunks, order, place_ref, *refs):
+    inputs, out_ref = refs[:-1], refs[-1]
+    for k in range(GROUPS):
+        lanes = pl.ds(pl.multiple_of(place_ref[k] * LANES, LANES), LANES)
+        for part in range(2):
+            tiles = [inputs[c * GROUPS + k][index, part] for c, index in order]
+            tiles = swap_lanes(tiles)
+            for g in range(GROUPS):
+                out_ref[part, g, :, lanes] = tiles[g]
+
+
+def place_columns(chunks, plan, places):
+    rows = chunks[0][0].shape[2]
+    step = min(rows, 128)
+    where = {q: (c, index) for c, which in enumerate(plan) for index, q in enumerate(which)}
+    order = [where[q] for q in range(GROUPS)]
+    specs, operands = [], []
+    for which, chunk in zip(plan, chunks):
+        specs += [pl.BlockSpec((len(which), 2, step, LANES), lambda i: (0, 0, i, 0))] * GROUPS
+        operands += list(chunk)
+    shape = (2, GROUPS, rows, GROUPS * LANES)
+    return pl.pallas_call(
+        functools.partial(place_kernel, len(plan), order),
+        grid=(rows // step,),
+        out_shape=jax.ShapeDtypeStruct(shape, jnp.float32),
+        in_specs=[pl.BlockSpec(memory_space=pltpu.SMEM)] + specs,
+        out_specs=pl.BlockSpec((2, GROUPS, step, GROUPS * LANES), lambda i: (0, 0, i, 0)),
+        compiler_params=params(),
+        cost_estimate=pl.CostEstimate(
+            flops=64 * rows * LANES, bytes_accessed=128 * rows * LANES, transcendentals=0
+        ),
+        name="place",
+    )(places, *operands)
+
+
+def lines_forward_kernel(rows, slot_ref, mix_ref, high_ref, low_ref, head_ref, turn_ref, *refs):
+    inputs, out_ref, first, second = refs[:4], refs[4], refs[5], refs[6]
+    tile = 8
+
+    def step(index, carry):
+        place = pl.ds(pl.multiple_of(index * tile, tile), tile)
+        x = [(ref[0, 0, place, :], ref[0, 1, place, :]) for ref in inputs]
+        even = [c_add(x[0], x[2]), c_add(x[1], x[3])]
+        odd = [c_sub(x[0], x[2]), c_sub(x[1], x[3])]
+        turned = (odd[1][1], -odd[1][0])
+        values = [
+            c_add(even[0], even[1]),
+            c_sub(even[0], even[1]),
+            c_add(odd[0], turned),
+            c_sub(odd[0], turned),
+        ]
+        for k in range(4):
+            twiddle = (head_ref[k, 0, place, :], head_ref[k, 1, place, :])
+            real_part, imag_part = c_mul(values[k], twiddle)
+            first[slot_ref[k], place, :LANES] = real_part
+            first[slot_ref[k], place, LANES:] = imag_part
+        return carry
+
+    lax.fori_loop(0, rows // tile, step, 0)
+    dot = functools.partial(jnp.dot, preferred_element_type=jnp.float32)
+    for k in range(4):
+        value = first[k]
+        high = value.astype(jnp.bfloat16)
+        low = (value - high.astype(jnp.float32)).astype(jnp.bfloat16)
+        value = dot(high, mix_ref[...]) + dot(low, mix_ref[...])
+        real_part, imag_part = c_mul(
+            (value[:, :LANES], value[:, LANES:]), (turn_ref[0], turn_ref[1])
+        )
+        second[:rows, k * LANES : (k + 1) * LANES] = real_part
+        second[rows:, k * LANES : (k + 1) * LANES] = imag_part
+    for side in range(2):
+        lanes = slice(2 * side * LANES, 2 * (side + 1) * LANES)
+        value = dot3(high_ref[...], low_ref[...], second[:, lanes], True)
+        for k in range(2):
+            for part in range(2):
+                piece = value[part * rows : (part + 1) * rows, k * LANES : (k + 1) * LANES]
+                out_ref[:, 0, part, 2 * side + k] = piece.reshape(rows // tile, tile, LANES)
+
+
+def line_specs(rows, tables):
+    return [pl.BlockSpec(memory_space=pltpu.SMEM)] + [whole_spec(table.shape) for table in tables]
+
+
+def lines_forward(pieces, slots, head, orient_tables):
+    count, _, rows, _ = pieces[0].shape
+    mixing, matrix, turns = orient_tables
+    tables = [mixing, matrix[0], matrix[1], head, turns]
+    places = rows // 8
+    return pl.pallas_call(
+        functools.partial(lines_forward_kernel, rows),
+        grid=(count,),
+        out_shape=jax.ShapeDtypeStruct((places, count, 2, 4, 8, LANES), jnp.float32),
+        in_specs=line_specs(rows, tables)
+        + [pl.BlockSpec((1, 2, rows, LANES), lambda i: (i, 0, 0, 0))] * 4,
+        out_specs=pl.BlockSpec((places, 1, 2, 4, 8, LANES), lambda i: (0, i, 0, 0, 0, 0)),
+        scratch_shapes=[
+            pltpu.VMEM((4, rows, 2 * LANES), jnp.float32),
+            pltpu.VMEM((2 * rows, 4 * LANES), jnp.float32),
+        ],
+        compiler_params=params(),
+        cost_estimate=pl.CostEstimate(
+            flops=LINE_WEIGHT * rows * rows * LANES * count,
+            bytes_accessed=64 * rows * LANES * count,
+            transcendentals=0,
+        ),
+        name="lines_forward",
+    )(slots, *tables, *pieces)
+
+
+def lines_inverse_kernel(rows, slot_ref, mix_ref, high_ref, low_ref, head_ref, turn_ref, in_ref, *refs):
+    outputs, first, second = refs[:4], refs[4], refs[5]
+    tile = 8
+    for k in range(4):
+        for part in range(2):
+            piece = in_ref[:, 0, part, k].reshape(rows, LANES)
+            second[part * rows : (part + 1) * rows, k * LANES : (k + 1) * LANES] = piece
+    dot = functools.partial(jnp.dot, preferred_element_type=jnp.float32)
+    for side in range(2):
+        lanes = slice(2 * side * LANES, 2 * (side + 1) * LANES)
+        second[:, lanes] = dot3(high_ref[...], low_ref[...], second[:, lanes], True)
+    for k in range(4):
+        lanes = slice(k * LANES, (k + 1) * LANES)
+        real_part, imag_part = c_mul(
+            (second[:rows, lanes], second[rows:, lanes]), (turn_ref[0], -turn_ref[1])
+        )
+        value = jnp.concatenate([real_part, imag_part], axis=1)
+        high = value.astype(jnp.bfloat16)
+        low = (value - high.astype(jnp.float32)).astype(jnp.bfloat16)
+        first[k] = dot(high, mix_ref[...]) + dot(low, mix_ref[...])
+
+    def step(index, carry):
+        place = pl.ds(pl.multiple_of(index * tile, tile), tile)
+        values = []
+        for k in range(4):
+            value = (first[slot_ref[k], place, :LANES], first[slot_ref[k], place, LANES:])
+            values.append(c_mul(value, (head_ref[k, 0, place, :], -head_ref[k, 1, place, :])))
+        even = [c_add(values[0], values[1]), c_sub(values[0], values[1])]
+        differ = c_sub(values[2], values[3])
+        odd = [c_add(values[2], values[3]), (-differ[1], differ[0])]
+        for k in range(2):
+            for side, value in enumerate((c_add(even[k], odd[k]), c_sub(even[k], odd[k]))):
+                outputs[k + 2 * side][0, 0, place, :] = value[0]
+                outputs[k + 2 * side][0, 1, place, :] = value[1]
+        return carry
+
+    lax.fori_loop(0, rows // tile, step, 0)
+
+
+def lines_inverse(blocks, slots, head, orient_tables):
+    places, count = blocks.shape[:2]
+    rows = places * 8
+    mixing, matrix, turns = orient_tables
+    tables = [mixing, matrix[0], matrix[1], head, turns]
+    return pl.pallas_call(
+        functools.partial(lines_inverse_kernel, rows),
+        grid=(count,),
+        out_shape=[jax.ShapeDtypeStruct((count, 2, rows, LANES), jnp.float32)] * 4,
+        in_specs=line_specs(rows, tables)
+        + [pl.BlockSpec((places, 1, 2, 4, 8, LANES), lambda i: (0, i, 0, 0, 0, 0))],
+        out_specs=[pl.BlockSpec((1, 2, rows, LANES), lambda i: (i, 0, 0, 0))] * 4,
+        scratch_shapes=[
+            pltpu.VMEM((4, rows, 2 * LANES), jnp.float32),
+            pltpu.VMEM((2 * rows, 4 * LANES), jnp.float32),
+        ],
+        compiler_params=params(),
+        cost_estimate=pl.CostEstimate(
+            flops=LINE_WEIGHT * rows * rows * LANES * count,
+            bytes_accessed=64 * rows * LANES * count,
+            transcendentals=0,
+        ),
+        name="lines_inverse",
+    )(slots, *tables, blocks)
+
+
+def row_filter_kernel(plan, slots, forward_ref, inverse_ref, turn_ref, green_ref, *refs):
+    inputs, outputs = refs[: len(plan)], refs[len(plan) : 2 * len(plan)]
+    x, held = refs[-2:]
+    chunks = 4
+    inner = slots * chunks
+    modes = inner * GROUPS
+    rows = 8
+    where = {q: (c, index) for c, which in enumerate(plan) for index, q in enumerate(which)}
+
+    for q in range(GROUPS):
+        c, index = where[q]
+        columns = []
+        for n in range(chunks):
+            values = [
+                (inputs[c][n * slots + k, index, 0, 0], inputs[c][n * slots + k, index, 1, 0])
+                for k in range(slots)
+            ]
+            values = small_dft(values, -1)
+            columns.append([c_const(values[a], a * n, inner, -1) for a in range(slots)])
+        for a in range(slots):
+            values = small_dft([columns[n][a] for n in range(chunks)], -1)
+            for b in range(chunks):
+                mode = a + slots * b
+                x[q, mode, 0], x[q, mode, 1] = c_const(values[b], q * mode, modes, -1)
+
+    def before(mode, carry):
+        values = [(x[q, mode, 0], x[q, mode, 1]) for q in range(GROUPS)]
+        values = small_dft(values, -1)
+        for e in range(GROUPS):
+            where_to = mode + inner * e
+            twiddle = (turn_ref[0, pl.ds(where_to, 1), :], turn_ref[1, pl.ds(where_to, 1), :])
+            held[where_to, :, :LANES], held[where_to, :, LANES:] = c_mul(values[e], twiddle)
+        return carry
+
+    lax.fori_loop(0, inner, before, 0, unroll=8)
+
+    group = 256 // rows
+
+    def middle(index, carry):
+        mode = pl.multiple_of(index * group, group)
+        value = held[pl.ds(mode, group)].reshape(group * rows, 2 * LANES)
+        value = dot3(forward_ref[0], forward_ref[1], value, False)
+        green = green_ref[pl.ds(mode, group)].reshape(group * rows, LANES)
+        value = value * jnp.concatenate([green, green], axis=1)
+        value = dot3(inverse_ref[0], inverse_ref[1], value, False)
+        held[pl.ds(mode, group)] = value.reshape(group, rows, 2 * LANES)
+        return carry
+
+    lax.fori_loop(0, modes // group, middle, 0, unroll=MIDDLE_UNROLL)
+
+    def after_(mode, carry):
+        values = []
+        for e in range(GROUPS):
+            where_from = mode + inner * e
+            twiddle = (turn_ref[0, pl.ds(where_from, 1), :], -turn_ref[1, pl.ds(where_from, 1), :])
+            values.append(c_mul((held[where_from, :, :LANES], held[where_from, :, LANES:]), twiddle))
+        values = small_dft(values, 1)
+        for q in range(GROUPS):
+            x[q, mode, 0], x[q, mode, 1] = values[q]
+        return carry
+
+    lax.fori_loop(0, inner, after_, 0, unroll=8)
+
+    for q in range(GROUPS):
+        c, index = where[q]
+        columns = []
+        for a in range(slots):
+            values = []
+            for b in range(chunks):
+                mode = a + slots * b
+                values.append(c_const((x[q, mode, 0], x[q, mode, 1]), q * mode, modes, 1))
+            columns.append(small_dft(values, 1))
+        for n in range(chunks):
+            values = [c_const(columns[a][n], a * n, inner, 1) for a in range(slots)]
+            values = small_dft(values, 1)
+            for k in range(slots):
+                outputs[c][n * slots + k, index, 0, 0] = values[k][0]
+                outputs[c][n * slots + k, index, 1, 0] = values[k][1]
+
+
+def group_matrix(orient):
+    index = np.arange(WIDTH)
+    small = np.exp(orient * 2j * np.pi * (np.outer(index, index) % WIDTH) / WIDTH)
+    whole = np.kron(np.eye(GROUPS), small)
+    return np.stack(split_bf16(np.block([[whole.real, whole.imag], [-whole.imag, whole.real]])))
+
+
+def row_filter(blocks, plan, turns, green, slots):
+    sources = blocks[0].shape[0]
+    modes = sources * GROUPS
+    forward = jnp.asarray(group_matrix(-1))
+    inverse = jnp.asarray(group_matrix(1))
+    specs = [
+        pl.BlockSpec((sources, len(which), 2, 1, 8, LANES), lambda i: (0, 0, 0, i, 0, 0))
+        for which in plan
+    ]
+    return pl.pallas_call(
+        functools.partial(row_filter_kernel, plan, slots),
+        grid=(4,),
+        out_shape=[jax.ShapeDtypeStruct(block.shape, jnp.float32) for block in blocks],
+        in_specs=[
+            whole_spec(forward.shape),
+            whole_spec(inverse.shape),
+            whole_spec(turns.shape),
+            pl.BlockSpec((modes, 8, LANES), lambda i: (0, i, 0)),
+        ]
+        + specs,
+        out_specs=specs,
+        scratch_shapes=[
+            pltpu.VMEM((GROUPS, sources, 2, 8, LANES), jnp.float32),
+            pltpu.VMEM((modes, 8, 2 * LANES), jnp.float32),
+        ],
+        compiler_params=params(),
+        cost_estimate=pl.CostEstimate(
+            flops=96 * LANES * LANES * modes * 32,
+            bytes_accessed=20 * modes * 32 * LANES,
+            transcendentals=0,
+        ),
+        name="row_filter",
+    )(forward, inverse, turns, green, *blocks)
+
+
+def four_plane(density, plane_wave):
+    narrow, wide = lax.axis_size("narrow"), lax.axis_size("wide")
+    device, place = lax.axis_index("narrow"), lax.axis_index("wide")
+    z_local, x_local = density.shape[1:]
+    total_z, total_x = z_local * narrow, x_local * wide
+    rows = z_local // GROUPS
+    modes = narrow * wide * GROUPS
+    partners = np.arange(4)
+
+    own = np.arange(4)
+    slots = np.stack([0 * own, 2 + 0 * own, 1 + 2 * (own % 2), 3 - 2 * (own % 2)], axis=1)
+    sign_low, sign_high = 1.0 - 2.0 * (own % 2), 1.0 - 2.0 * (own // 2)
+    phase = np.stack(
+        [
+            np.ones(4),
+            sign_low,
+            sign_high * np.where(own % 2 == 0, 1, 1j),
+            sign_high * np.where(own % 2 == 0, 1, -1j),
+        ],
+        axis=1,
+    )
+    group = np.repeat(np.arange(GROUPS), WIDTH)
+    depth = group[None, :] * rows + np.arange(rows)[:, None]
+    angle = 2.0 * np.pi * (slots[:, :, None, None] * depth % total_z) / total_z
+    head = phase[:, :, None, None] * np.exp(-1j * angle)
+    head = pick(np.stack([head.real, head.imag], axis=2).astype(np.float32), device)
+    slots = pick(slots.astype(np.int32), device)
+    turns = turn(group[None, :] * np.arange(rows)[:, None], GROUPS * rows)
+    turns = jnp.asarray(np.moveaxis(turns, 2, 0))
+    four = np.exp(-2j * np.pi * (np.outer(partners, partners) % 4) / 4)
+    mixing = np.round(np.kron(four, np.eye(WIDTH)))
+    ahead = np.block([[mixing.real, mixing.imag], [-mixing.imag, mixing.real]])
+    back = np.block([[mixing.real, -mixing.imag], [mixing.imag, mixing.real]])
+    tables = (jnp.asarray(ahead.astype(jnp.bfloat16)), jnp.asarray(dft_matrix(rows, -1, True)), turns)
+    tables_back = (jnp.asarray(back.astype(jnp.bfloat16)), jnp.asarray(dft_matrix(rows, 1, True)), turns)
+    places = device ^ jnp.asarray(partners.astype(np.int32))
+    cell = np.tile(np.arange(WIDTH), GROUPS)
+    x_turns = turn(np.arange(modes)[:, None] * cell[None, :], total_x)
+    x_turns = jnp.asarray(np.moveaxis(x_turns, 2, 0))
+    residue = np.arange(4)[:, None, None] + 16 * np.arange(8)[:, None] + 4 * group
+    wave_z = jnp.asarray(residue.reshape(32, LANES).astype(np.int32))
+    wave_z = wave_z + 16 * 8 * (device * wide + place)
+    wave_x = np.arange(modes)[:, None, None] + modes * cell
+    signed_x = jnp.asarray(np.where(wave_x < total_x // 2, wave_x, wave_x - total_x).astype(np.int32))
+    green = green_of(plane_wave, wave_z[None], signed_x, total_z, total_x)
+
+    source = density.reshape(2, GROUPS, rows, x_local)
+
+    def send(pieces):
+        return [pieces[0]] + [swap(pieces[k], "narrow", k) for k in range(1, 4)]
+
+    def trade_all(blocks):
+        return lax.all_to_all(blocks, ("narrow", "wide"), 0, 0, tiled=True)
+
+    arrived, got = [], None
+    for which in PLAN:
+        pieces = cut_columns(source if got is None else source, places, which)
+        got = send(pieces if got is None else after(pieces, got))
+        arrived.append(trade_all(lines_forward(got, slots, head, tables)))
+
+    filtered = row_filter(arrived, PLAN, x_turns, green, wide)
+
+    back = [None] * len(PLAN)
+    for c in reversed(range(len(PLAN))):
+        pieces = lines_inverse(trade_all(filtered[c]), slots, head, tables_back)
+        back[c] = send(pieces)
+    return place_columns(back, PLAN, places).reshape(density.shape)
 
 
 def plane(density, plane_wave):
@@ -575,7 +1027,9 @@
 
 
 def shards(density, plane_wave):
-    planes = [plane(density[:, y], plane_wave[y]) for y in range(density.shape[1])]
+    sizes = lax.axis_size("narrow"), lax.axis_size("wide")
+    one = four_plane if fits(*sizes, *density.shape[2:]) else plane
+    planes = [one(density[:, y], plane_wave[y]) for y in range(density.shape[1])]
     return jnp.stack(planes, axis=1)
 
 

time: 356 us -> 307 us (0.86)
  starting transfers between devices: 63.1 us -> 27.3 us
  blocking collectives: 29 us -> 52.5 us
  local copies, waits for them, and re-layouts: 23.8 us -> 4.25 us
  Pallas kernels: 66.3 us -> 48.9 us
    all_to_all x7 -> x3, waiting for transfers between devices: 37 us -> 109 us  [trade_all(): return lax.all_to_all(blocks, ('narrow', 'wide'), 0, 0, tiled=True)]
    ppermute x32 -> x12, waiting for transfers between devices: 132 us -> 61.1 us  [swap(): return lax.ppermute(value, axis, pairs)]
    all_to_all x1, blocking collectives: 29 us -> 52.5 us  [trade_all(): return lax.all_to_all(blocks, ('narrow', 'wide'), 0, 0, tiled=True)]
    ppermute x32 -> x12, starting transfers between devices: 33.6 us -> 15 us  [swap(): return lax.ppermute(value, axis, pairs)]
    pallas_call x21 -> x8, Pallas kernels: 66.3 us -> 48.9 us  [the longest x1 12.1 us: row_filter(): pl.pallas_call(functools.partial(row_filter_kernel, plan, slots), grid=(4...]
    all_to_all x7 -> x3, starting transfers between devices: 29.4 us -> 12.3 us  [trade_all(): return lax.all_to_all(blocks, ('narrow', 'wide'), 0, 0, tiled=True)]
    unnamed x84 -> x36, local copies, waits for them, and re-layouts: 16.3 us -> 2.15 us
  transfers between devices with their start and end apart: 39 -> 15, of which waited for: 34 -> 10; matrix products, arithmetic and copies ran while one was open for 2% -> 1% of each run, Pallas kernels for 12% -> 9%
where the time goes in v3:
time: 307 us; the launch traced here: 306 us
  waiting for transfers between devices  171 us (56%)
  blocking collectives  52.5 us (17%)
  Pallas kernels  48.9 us (16%)
  starting transfers between devices  27.3 us (9%)
  local copies, waits for them, and re-layouts  4.25 us (1%)
    all_to_all x3, waiting for transfers between devices, trade_all(): return lax.all_to_all(blocks, ('narrow', 'wide'), 0, 0, tiled=True)  109 us
    ppermute x12, waiting for transfers between devices, swap(): return lax.ppermute(value, axis, pairs)  61.1 us
    all_to_all x1, blocking collectives, trade_all(): return lax.all_to_all(blocks, ('narrow', 'wide'), 0, 0, tiled=True)  52.5 us
    ppermute x12, starting transfers between devices, swap(): return lax.ppermute(value, axis, pairs)  15 us
    all_to_all x3, starting transfers between devices, trade_all(): return lax.all_to_all(blocks, ('narrow', 'wide'), 0, 0, tiled=True)  12.3 us
    pallas_call x1, Pallas kernels, row_filter(): pl.pallas_call(functools.partial(row_filter_kernel, plan, slots), grid=(4...  12.1 us
    pallas_call x2, Pallas kernels, lines_forward(): pl.pallas_call(functools.partial(lines_forward_kernel, rows), grid=(count...  11.6 us
    pallas_call x2, Pallas kernels, lines_inverse(): pl.pallas_call(functools.partial(lines_inverse_kernel, rows), grid=(count...  11.2 us
  transfers between devices with their start and end apart: 15, of which 10 were waited for; matrix products, arithmetic and copies ran while one was open for 1% of the time, Pallas kernels for 9%

profile of v3, /device:TPU:0, one launch (start us, length us, event | category | flops | bytes accessed | tf_op | source)
XLA Modules:
  0.0 306.4 jit_solution(16058256141228821827)
XLA Ops:
  0.0 4.6 %cut.2 = (f32[2,2,256,128]{3,2,1,0:T(8,128)S(1)}, f32[2,2,256,128]{3,2,1,0:T(8,128)}, f32[2,2,256,128]{3,2,1,0:T(8,128)}, f32[2,2,256,128]{3,2,1,0:T(8,128)}) custom-call(s32[4]{0:T(128)S(1)} %iota_xor_fusion.place_ref, f32[2,4,256,512]{3,2,1,0:T(8,128)} %bitcast.9), custom_call_target="tpu_custom_call" | custom-call | flops 2097152 | bytes 5242880 | tf_op jit(solution)/shard_map/cut/pallas_call | solution.py:537
  4.6 2.9 collective-permute-start
  7.5 1.5 collective-permute-start.1
  9.0 0.0 collective-permute-start.2
  9.0 0.0 copy-done
  9.0 4.6 %cut.3 = (f32[2,2,256,128]{3,2,1,0:T(8,128)S(1)}, f32[2,2,256,128]{3,2,1,0:T(8,128)}, f32[2,2,256,128]{3,2,1,0:T(8,128)}, f32[2,2,256,128]{3,2,1,0:T(8,128)}) custom-call(s32[4]{0:T(128)S(1)} %iota_xor_fusion.place_ref, f32[2,4,256,512]{3,2,1,0:T(8,128)} %bitcast.10), custom_call_target="tpu_custom_call" | custom-call | flops 2097152 | bytes 5242880 | tf_op jit(solution)/shard_map/cut/pallas_call | solution.py:537
  13.6 0.0 copy-start.15
  13.6 0.8 dynamic-slice_bitcast_fusion.1.slot_ref
  14.4 1.3 dynamic-slice_bitcast_fusion.head_ref
  15.8 4.7 %collective-permute-done.refs_1_ = f32[2,2,256,128]{3,2,1,0:T(8,128)S(1)} collective-permute-done((f32[2,2,256,128]{3,2,1,0:T(8,128)}, f32[2,2,256,128]{3,2,1,0:T(8,128)S(1)}, u32[]{:S(2)}, u32[]{:S(2)}) %collective-permute-start) | collective-permute-done | bytes 524320 | tf_op jit(solution)/shard_map/ppermute | solution.py:405
  20.5 11.9 %collective-permute-done.1.refs_2_ = f32[2,2,256,128]{3,2,1,0:T(8,128)S(1)} collective-permute-done((f32[2,2,256,128]{3,2,1,0:T(8,128)}, f32[2,2,256,128]{3,2,1,0:T(8,128)S(1)}, u32[]{:S(2)}, u32[]{:S(2)}) %collective-permute-start.1) | collective-permute-done | bytes 524320 | tf_op jit(solution)/shard_map/ppermute | solution.py:405
  32.3 0.0 collective-permute-done.2.refs_3_
  32.3 1.3 collective-permute-start.3
  33.7 0.7 collective-permute-start.4
  34.4 1.4 collective-permute-start.5
  35.8 0.0 copy-done.6
  35.8 0.0 copy-done.8
  35.8 0.0 copy-done.10
  35.8 0.0 copy-done.15
  35.8 5.7 %lines_forward.2 = f32[32,2,2,4,8,128]{5,4,3,2,1,0:T(8,128)} custom-call(s32[4]{0:T(128)S(1)} %dynamic-slice_bitcast_fusion.1.slot_ref, bf16[256,256]{1,0:T(8,128)(2,1)S(1)} %copy-done.15, bf16[512,512]{1,0:T(8,128)(2,1)S(1)} %copy-done.8, bf16[512,512]{1,0:T(8,128)(2,1)S(1)} %copy-done.6, f32[4,2,256,128]{3,2,1,0:T(8,128)S(1)} %dynamic-slice_bitcast_fusion.head_ref, ...), custom_call_target="tpu_custom_call" | custom-call | flops 50331648000 | bytes 4194304 | tf_op jit(solution)/shard_map/lines_forward/pallas_call | solution.py:644
  41.5 5.0 %all-to-all-start = ((f32[32,2,2,4,8,128]{5,4,3,2,1,0:T(8,128)}), f32[32,2,2,4,8,128]{5,4,3,2,1,0:T(8,128)}, u32[]{:S(2)}, u32[]{:S(2)}) async-start(f32[32,2,2,4,8,128]{5,4,3,2,1,0:T(8,128)} %lines_forward.2), calls=%async_computation | async-start | bytes 4194304 | tf_op jit(solution)/shard_map/all_to_all | solution.py:904
  46.6 0.9 collective-permute-done.3.refs_1_
  47.5 20.8 %collective-permute-done.4.refs_2_ = f32[2,2,256,128]{3,2,1,0:T(8,128)} collective-permute-done((f32[2,2,256,128]{3,2,1,0:T(8,128)}, f32[2,2,256,128]{3,2,1,0:T(8,128)}, u32[]{:S(2)}, u32[]{:S(2)}) %collective-permute-start.4) | collective-permute-done | bytes 524320 | tf_op jit(solution)/shard_map/ppermute | solution.py:405
  68.4 0.5 collective-permute-done.5.refs_3_
  68.9 0.0 copy-done.7
  68.9 0.0 copy-done.9
  68.9 6.0 %lines_forward.3 = f32[32,2,2,4,8,128]{5,4,3,2,1,0:T(8,128)} custom-call(s32[4]{0:T(128)S(1)} %dynamic-slice_bitcast_fusion.1.slot_ref, bf16[256,256]{1,0:T(8,128)(2,1)S(1)} %copy-done.15, bf16[512,512]{1,0:T(8,128)(2,1)S(1)} %copy-done.9, bf16[512,512]{1,0:T(8,128)(2,1)S(1)} %copy-done.7, f32[4,2,256,128]{3,2,1,0:T(8,128)S(1)} %dynamic-slice_bitcast_fusion.head_ref, ...), custom_call_target="tpu_custom_call" | custom-call | flops 50331648000 | bytes 4194304 | tf_op jit(solution)/shard_map/lines_forward/pallas_call | solution.py:644
  74.9 21.8 %all-to-all-done.refs_0_ = f32[32,2,2,4,8,128]{5,4,3,2,1,0:T(8,128)} async-done(((f32[32,2,2,4,8,128]{5,4,3,2,1,0:T(8,128)}), f32[32,2,2,4,8,128]{5,4,3,2,1,0:T(8,128)}, u32[]{:S(2)}, u32[]{:S(2)}) %all-to-all-start) | async-done | bytes 2097184 | tf_op jit(solution)/shard_map/all_to_all | solution.py:904
  96.7 3.5 %all-to-all-start.1 = ((f32[32,2,2,4,8,128]{5,4,3,2,1,0:T(8,128)}), f32[32,2,2,4,8,128]{5,4,3,2,1,0:T(8,128)}, u32[]{:S(2)}, u32[]{:S(2)}) async-start(f32[32,2,2,4,8,128]{5,4,3,2,1,0:T(8,128)} %lines_forward.3), calls=%async_computation.1 | async-start | bytes 4194304 | tf_op jit(solution)/shard_map/all_to_all | solution.py:904
  100.1 0.0 copy-start.11
  100.2 0.0 copy-start.12
  100.2 0.0 copy-start.14
  100.9 0.0 copy-done.17
  100.9 0.0 copy-done.16
  100.9 2.0 add_multiply_fusion.green_ref
  102.9 47.3 %all-to-all-done.1.refs_1_ = f32[32,2,2,4,8,128]{5,4,3,2,1,0:T(8,128)} async-done(((f32[32,2,2,4,8,128]{5,4,3,2,1,0:T(8,128)}), f32[32,2,2,4,8,128]{5,4,3,2,1,0:T(8,128)}, u32[]{:S(2)}, u32[]{:S(2)}) %all-to-all-start.1) | async-done | bytes 2097184 | tf_op jit(solution)/shard_map/all_to_all | solution.py:904
  150.2 0.0 copy-done.11
  150.2 0.0 copy-done.12
  150.2 0.0 copy-done.14
  150.2 12.1 %row_filter.1 = (f32[32,2,2,4,8,128]{5,4,3,2,1,0:T(8,128)}, f32[32,2,2,4,8,128]{5,4,3,2,1,0:T(8,128)S(1)}) custom-call(bf16[2,256,256]{2,1,0:T(8,128)(2,1)S(1)} %copy-done.12, bf16[2,256,256]{2,1,0:T(8,128)(2,1)S(1)} %copy-done.11, f32[2,128,128]{2,1,0:T(8,128)S(1)} %copy-done.14, f32[128,32,128]{2,1,0:T(8,128)} %add_multiply_fusion.green_ref, ...), custom_call_target="tpu_custom_call" | custom-call | flops 6442450944 | bytes 10485760 | tf_op jit(solution)/shard_map/row_filter/pallas_call | solution.py:826
  162.3 52.5 %all_to_all.20.in_ref = f32[32,2,2,4,8,128]{5,4,3,2,1,0:T(8,128)} all-to-all(f32[32,2,2,4,8,128]{5,4,3,2,1,0:T(8,128)S(1)} %get-tuple-element.44), channel_id=1, replica_groups=mesh['wide'=8,'narrow'=4] {'narrow','wide'}, dimensions={0} | all-to-all | bytes 4194304 | tf_op jit(solution)/shard_map/all_to_all | solution.py:904
  214.8 3.8 %all-to-all-start.2 = ((f32[32,2,2,4,8,128]{5,4,3,2,1,0:T(8,128)}), f32[32,2,2,4,8,128]{5,4,3,2,1,0:T(8,128)}, u32[]{:S(2)}, u32[]{:S(2)}) async-start(f32[32,2,2,4,8,128]{5,4,3,2,1,0:T(8,128)} %get-tuple-element.39), calls=%async_computation.2 | async-start | bytes 4194304 | tf_op jit(solution)/shard_map/all_to_all | solution.py:904
  218.6 0.0 copy-done.2
  218.6 0.0 copy-done.4
  218.6 0.0 copy-done.13
  218.6 6.0 %lines_inverse.3 = (f32[2,2,256,128]{3,2,1,0:T(8,128)S(1)}, f32[2,2,256,128]{3,2,1,0:T(8,128)}, f32[2,2,256,128]{3,2,1,0:T(8,128)}, f32[2,2,256,128]{3,2,1,0:T(8,128)}) custom-call(s32[4]{0:T(128)S(1)} %dynamic-slice_bitcast_fusion.1.slot_ref, bf16[256,256]{1,0:T(8,128)(2,1)S(1)} %copy-done.13, bf16[512,512]{1,0:T(8,128)(2,1)S(1)} %copy-done.4, ...), custom_call_target="tpu_custom_call" | custom-call | flops 50331648000 | bytes 4194304 | tf_op jit(solution)/shard_map/lines_inverse/pallas_call | solution.py:709
  224.6 1.4 collective-permute-start.9
  226.0 1.5 collective-permute-start.10
  227.5 0.6 collective-permute-start.11
  228.1 40.4 %all-to-all-done.2.in_ref = f32[32,2,2,4,8,128]{5,4,3,2,1,0:T(8,128)} async-done(((f32[32,2,2,4,8,128]{5,4,3,2,1,0:T(8,128)}), f32[32,2,2,4,8,128]{5,4,3,2,1,0:T(8,128)}, u32[]{:S(2)}, u32[]{:S(2)}) %all-to-all-start.2) | async-done | bytes 2097184 | tf_op jit(solution)/shard_map/all_to_all | solution.py:904
  268.5 1.0 copy-done.3
  269.5 1.0 copy-done.5
  270.6 5.1 %lines_inverse.2 = (f32[2,2,256,128]{3,2,1,0:T(8,128)S(1)}, f32[2,2,256,128]{3,2,1,0:T(8,128)S(1)}, f32[2,2,256,128]{3,2,1,0:T(8,128)S(1)}, f32[2,2,256,128]{3,2,1,0:T(8,128)S(1)}) custom-call(s32[4]{0:T(128)S(1)} %dynamic-slice_bitcast_fusion.1.slot_ref, bf16[256,256]{1,0:T(8,128)(2,1)S(1)} %copy-done.13, bf16[512,512]{1,0:T(8,128)(2,1)S(1)} %copy-done.5, ...), custom_call_target="tpu_custom_call" | custom-call | flops 50331648000 | bytes 4194304 | tf_op jit(solution)/shard_map/lines_inverse/pallas_call | solution.py:709
  275.7 0.1 collective-permute-start.6
  275.8 1.2 collective-permute-start.7
  277.0 0.0 collective-permute-done.9.refs_5_
  277.0 2.3 collective-permute-start.8
  279.3 0.0 collective-permute-done.10.refs_6_
  279.3 0.0 collective-permute-done.11.refs_7_
  279.3 11.3 %collective-permute-done.6.refs_1_ = f32[2,2,256,128]{3,2,1,0:T(8,128)S(1)} collective-permute-done((f32[2,2,256,128]{3,2,1,0:T(8,128)S(1)}, f32[2,2,256,128]{3,2,1,0:T(8,128)S(1)}, u32[]{:S(2)}, u32[]{:S(2)}) %collective-permute-start.6) | collective-permute-done | bytes 524320 | tf_op jit(solution)/shard_map/ppermute | solution.py:405
  290.6 10.9 %collective-permute-done.7.refs_2_ = f32[2,2,256,128]{3,2,1,0:T(8,128)S(1)} collective-permute-done((f32[2,2,256,128]{3,2,1,0:T(8,128)S(1)}, f32[2,2,256,128]{3,2,1,0:T(8,128)S(1)}, u32[]{:S(2)}, u32[]{:S(2)}) %collective-permute-start.7) | collective-permute-done | bytes 524320 | tf_op jit(solution)/shard_map/ppermute | solution.py:405
  301.5 0.0 collective-permute-done.8.refs_3_
  301.5 0.0 copy-done.1
  301.5 4.9 %place.1 = f32[2,4,256,512]{3,2,1,0:T(8,128)} custom-call(s32[4]{0:T(128)S(1)} %copy-done.1, f32[2,2,256,128]{3,2,1,0:T(8,128)S(1)} %get-tuple-element.40.refs_0_, f32[2,2,256,128]{3,2,1,0:T(8,128)S(1)} %collective-permute-done.6.refs_1_, f32[2,2,256,128]{3,2,1,0:T(8,128)S(1)} %collective-permute-done.7.refs_2_, ...), custom_call_target="tpu_custom_call" | custom-call | flops 2097152 | bytes 4194304 | tf_op jit(solution)/shard_map/place/pallas_call | solution.py:577
  (16 shorter events, 0.0 us)
Async XLA Ops:
  0.0 9.0 %copy-start = (s32[4]{0:T(128)}, s32[4]{0:T(128)S(1)}, u32[]{:S(2)}) copy-start(s32[4]{0:T(128)S(1)} %iota_xor_fusion.place_ref) | copy-start | bytes 52
  4.6 15.9 %collective-permute-start = (f32[2,2,256,128]{3,2,1,0:T(8,128)}, f32[2,2,256,128]{3,2,1,0:T(8,128)S(1)}, u32[]{:S(2)}, u32[]{:S(2)}) collective-permute-start(f32[2,2,256,128]{3,2,1,0:T(8,128)} %get-tuple-element.28), channel_id=1, source_target_pairs={{0,1},{1,0},{2,3},{3,2},{4,5},{5,4},{6,7},{7,6},{8,9},{9,8},{10,11... | collective-permute-start | bytes 1572872 | tf_op jit(solution)/shard_map/ppermute | solution.py:405
  7.5 24.8 %collective-permute-start.1 = (f32[2,2,256,128]{3,2,1,0:T(8,128)}, f32[2,2,256,128]{3,2,1,0:T(8,128)S(1)}, u32[]{:S(2)}, u32[]{:S(2)}) collective-permute-start(f32[2,2,256,128]{3,2,1,0:T(8,128)} %get-tuple-element.29), channel_id=1, source_target_pairs={{0,2},{1,3},{2,0},{3,1},{4,6},{5,7},{6,4},{7,5},{8,10},{9,11},{10,... | collective-permute-start | bytes 1572872 | tf_op jit(solution)/shard_map/ppermute | solution.py:405
  9.0 23.3 %collective-permute-start.2 = (f32[2,2,256,128]{3,2,1,0:T(8,128)}, f32[2,2,256,128]{3,2,1,0:T(8,128)}, u32[]{:S(2)}, u32[]{:S(2)}) collective-permute-start(f32[2,2,256,128]{3,2,1,0:T(8,128)} %get-tuple-element.30), channel_id=1, source_target_pairs={{0,3},{1,2},{2,1},{3,0},{4,7},{5,6},{6,5},{7,4},{8,11},{9,10},{10,... | collective-permute-start | bytes 1572872 | tf_op jit(solution)/shard_map/ppermute | solution.py:405
  13.6 22.2 %copy-start.6 = (bf16[512,512]{1,0:T(8,128)(2,1)S(1)}, bf16[512,512]{1,0:T(8,128)(2,1)}, u32[]{:S(2)}) copy-start(bf16[512,512]{1,0:T(8,128)(2,1)} %constant.84.low_ref) | copy-start | bytes 1572868
  13.6 22.2 %copy-start.8 = (bf16[512,512]{1,0:T(8,128)(2,1)S(1)}, bf16[512,512]{1,0:T(8,128)(2,1)}, u32[]{:S(2)}) copy-start(bf16[512,512]{1,0:T(8,128)(2,1)} %constant.82.high_ref) | copy-start | bytes 1572868
  13.6 22.2 %copy-start.10 = (f32[2,256,128]{2,1,0:T(8,128)S(1)}, f32[2,256,128]{2,1,0:T(8,128)}, u32[]{:S(2)}) copy-start(f32[2,256,128]{2,1,0:T(8,128)} %constant.65.clone.turn_ref) | copy-start | bytes 786436
  13.6 22.2 %copy-start.15 = (bf16[256,256]{1,0:T(8,128)(2,1)S(1)}, bf16[256,256]{1,0:T(8,128)(2,1)}, u32[]{:S(2)}) copy-start(bf16[256,256]{1,0:T(8,128)(2,1)} %constant.66.clone.mix_ref) | copy-start | bytes 393220
  32.3 15.2 %collective-permute-start.3 = (f32[2,2,256,128]{3,2,1,0:T(8,128)}, f32[2,2,256,128]{3,2,1,0:T(8,128)}, u32[]{:S(2)}, u32[]{:S(2)}) collective-permute-start(f32[2,2,256,128]{3,2,1,0:T(8,128)} %get-tuple-element.36), channel_id=1, source_target_pairs={{0,1},{1,0},{2,3},{3,2},{4,5},{5,4},{6,7},{7,6},{8,9},{9,8},{10,11... | collective-permute-start | bytes 1572872 | tf_op jit(solution)/shard_map/ppermute | solution.py:405
  33.7 34.7 %collective-permute-start.4 = (f32[2,2,256,128]{3,2,1,0:T(8,128)}, f32[2,2,256,128]{3,2,1,0:T(8,128)}, u32[]{:S(2)}, u32[]{:S(2)}) collective-permute-start(f32[2,2,256,128]{3,2,1,0:T(8,128)} %get-tuple-element.37), channel_id=1, source_target_pairs={{0,2},{1,3},{2,0},{3,1},{4,6},{5,7},{6,4},{7,5},{8,10},{9,11},{10,... | collective-permute-start | bytes 1572872 | tf_op jit(solution)/shard_map/ppermute | solution.py:405
  34.4 34.5 %collective-permute-start.5 = (f32[2,2,256,128]{3,2,1,0:T(8,128)}, f32[2,2,256,128]{3,2,1,0:T(8,128)}, u32[]{:S(2)}, u32[]{:S(2)}) collective-permute-start(f32[2,2,256,128]{3,2,1,0:T(8,128)} %get-tuple-element.38), channel_id=1, source_target_pairs={{0,3},{1,2},{2,1},{3,0},{4,7},{5,6},{6,5},{7,4},{8,11},{9,10},{10,... | collective-permute-start | bytes 1572872 | tf_op jit(solution)/shard_map/ppermute | solution.py:405
  41.5 27.4 %copy-start.7 = (bf16[512,512]{1,0:T(8,128)(2,1)S(1)}, bf16[512,512]{1,0:T(8,128)(2,1)}, u32[]{:S(2)}) copy-start(bf16[512,512]{1,0:T(8,128)(2,1)} %constant.84.low_ref) | copy-start | bytes 1572868
  41.5 27.4 %copy-start.9 = (bf16[512,512]{1,0:T(8,128)(2,1)S(1)}, bf16[512,512]{1,0:T(8,128)(2,1)}, u32[]{:S(2)}) copy-start(bf16[512,512]{1,0:T(8,128)(2,1)} %constant.82.high_ref) | copy-start | bytes 1572868
  41.5 55.1 %all-to-all-start = ((f32[32,2,2,4,8,128]{5,4,3,2,1,0:T(8,128)}), f32[32,2,2,4,8,128]{5,4,3,2,1,0:T(8,128)}, u32[]{:S(2)}, u32[]{:S(2)}) async-start(f32[32,2,2,4,8,128]{5,4,3,2,1,0:T(8,128)} %lines_forward.2), calls=%async_computation | async-start | bytes 4194304 | tf_op jit(solution)/shard_map/all_to_all | solution.py:904
  74.8 26.0 %copy-start.17 = (s32[32,128]{1,0:T(8,128)S(1)}, s32[32,128]{1,0:T(8,128)}, u32[]{:S(2)}) copy-start(s32[32,128]{1,0:T(8,128)} %constant.71.clone) | copy-start | bytes 49156
  74.9 26.1 %copy-start.16 = (s32[128,128]{1,0:T(8,128)S(1)}, s32[128,128]{1,0:T(8,128)}, u32[]{:S(2)}) copy-start(s32[128,128]{1,0:T(8,128)} %constant.80) | copy-start | bytes 196612
  96.7 53.6 %all-to-all-start.1 = ((f32[32,2,2,4,8,128]{5,4,3,2,1,0:T(8,128)}), f32[32,2,2,4,8,128]{5,4,3,2,1,0:T(8,128)}, u32[]{:S(2)}, u32[]{:S(2)}) async-start(f32[32,2,2,4,8,128]{5,4,3,2,1,0:T(8,128)} %lines_forward.3), calls=%async_computation.1 | async-start | bytes 4194304 | tf_op jit(solution)/shard_map/all_to_all | solution.py:904
  100.1 50.1 %copy-start.11 = (bf16[2,256,256]{2,1,0:T(8,128)(2,1)S(1)}, bf16[2,256,256]{2,1,0:T(8,128)(2,1)}, u32[]{:S(2)}) copy-start(bf16[2,256,256]{2,1,0:T(8,128)(2,1)} %constant.74.clone.inverse_ref) | copy-start | bytes 786436
  100.2 50.1 %copy-start.12 = (bf16[2,256,256]{2,1,0:T(8,128)(2,1)S(1)}, bf16[2,256,256]{2,1,0:T(8,128)(2,1)}, u32[]{:S(2)}) copy-start(bf16[2,256,256]{2,1,0:T(8,128)(2,1)} %constant.73.clone.forward_ref) | copy-start | bytes 786436
  100.2 50.1 %copy-start.14 = (f32[2,128,128]{2,1,0:T(8,128)S(1)}, f32[2,128,128]{2,1,0:T(8,128)}, u32[]{:S(2)}) copy-start(f32[2,128,128]{2,1,0:T(8,128)} %constant.70.clone.turn_ref) | copy-start | bytes 393220
  214.8 3.8 %copy-start.2 = (bf16[512,512]{1,0:T(8,128)(2,1)S(1)}, bf16[512,512]{1,0:T(8,128)(2,1)}, u32[]{:S(2)}) copy-start(bf16[512,512]{1,0:T(8,128)(2,1)} %constant.78.low_ref) | copy-start | bytes 1572868
  214.8 3.8 %copy-start.4 = (bf16[512,512]{1,0:T(8,128)(2,1)S(1)}, bf16[512,512]{1,0:T(8,128)(2,1)}, u32[]{:S(2)}) copy-start(bf16[512,512]{1,0:T(8,128)(2,1)} %constant.76.high_ref) | copy-start | bytes 1572868
  214.8 3.8 %copy-start.13 = (bf16[256,256]{1,0:T(8,128)(2,1)S(1)}, bf16[256,256]{1,0:T(8,128)(2,1)}, u32[]{:S(2)}) copy-start(bf16[256,256]{1,0:T(8,128)(2,1)} %constant.68.clone.mix_ref) | copy-start | bytes 393220
  214.8 53.7 %all-to-all-start.2 = ((f32[32,2,2,4,8,128]{5,4,3,2,1,0:T(8,128)}), f32[32,2,2,4,8,128]{5,4,3,2,1,0:T(8,128)}, u32[]{:S(2)}, u32[]{:S(2)}) async-start(f32[32,2,2,4,8,128]{5,4,3,2,1,0:T(8,128)} %get-tuple-element.39), calls=%async_computation.2 | async-start | bytes 4194304 | tf_op jit(solution)/shard_map/all_to_all | solution.py:904
  224.6 52.3 %collective-permute-start.9 = (f32[2,2,256,128]{3,2,1,0:T(8,128)}, f32[2,2,256,128]{3,2,1,0:T(8,128)S(1)}, u32[]{:S(2)}, u32[]{:S(2)}) collective-permute-start(f32[2,2,256,128]{3,2,1,0:T(8,128)} %get-tuple-element.46), channel_id=1, source_target_pairs={{0,1},{1,0},{2,3},{3,2},{4,5},{5,4},{6,7},{7,6},{8,9},{9,8},{10,11... | collective-permute-start | bytes 1572872 | tf_op jit(solution)/shard_map/ppermute | solution.py:405
  226.0 53.2 %collective-permute-start.10 = (f32[2,2,256,128]{3,2,1,0:T(8,128)}, f32[2,2,256,128]{3,2,1,0:T(8,128)S(1)}, u32[]{:S(2)}, u32[]{:S(2)}) collective-permute-start(f32[2,2,256,128]{3,2,1,0:T(8,128)} %get-tuple-element.47), channel_id=1, source_target_pairs={{0,2},{1,3},{2,0},{3,1},{4,6},{5,7},{6,4},{7,5},{8,10},{9,11},{10,... | collective-permute-start | bytes 1572872 | tf_op jit(solution)/shard_map/ppermute | solution.py:405
  227.5 74.0 %copy-start.1 = (s32[4]{0:T(128)S(1)}, s32[4]{0:T(128)}, u32[]{:S(2)}) copy-start(s32[4]{0:T(128)} %copy-done) | copy-start | bytes 52
  227.5 51.7 %collective-permute-start.11 = (f32[2,2,256,128]{3,2,1,0:T(8,128)}, f32[2,2,256,128]{3,2,1,0:T(8,128)S(1)}, u32[]{:S(2)}, u32[]{:S(2)}) collective-permute-start(f32[2,2,256,128]{3,2,1,0:T(8,128)} %get-tuple-element.48), channel_id=1, source_target_pairs={{0,3},{1,2},{2,1},{3,0},{4,7},{5,6},{6,5},{7,4},{8,11},{9,10},{10,... | collective-permute-start | bytes 1572872 | tf_op jit(solution)/shard_map/ppermute | solution.py:405
  268.5 1.0 copy-start.3
  269.5 1.0 copy-start.5
  275.7 14.9 %collective-permute-start.6 = (f32[2,2,256,128]{3,2,1,0:T(8,128)S(1)}, f32[2,2,256,128]{3,2,1,0:T(8,128)S(1)}, u32[]{:S(2)}, u32[]{:S(2)}) collective-permute-start(f32[2,2,256,128]{3,2,1,0:T(8,128)S(1)} %get-tuple-element.41), channel_id=1, source_target_pairs={{0,1},{1,0},{2,3},{3,2},{4,5},{5,4},{6,7},{7,6},{8,9},{9,8},{10,11... | collective-permute-start | bytes 1572872 | tf_op jit(solution)/shard_map/ppermute | solution.py:405
  275.8 25.7 %collective-permute-start.7 = (f32[2,2,256,128]{3,2,1,0:T(8,128)S(1)}, f32[2,2,256,128]{3,2,1,0:T(8,128)S(1)}, u32[]{:S(2)}, u32[]{:S(2)}) collective-permute-start(f32[2,2,256,128]{3,2,1,0:T(8,128)S(1)} %get-tuple-element.42), channel_id=1, source_target_pairs={{0,2},{1,3},{2,0},{3,1},{4,6},{5,7},{6,4},{7,5},{8,10},{9,11},{10,... | collective-permute-start | bytes 1572872 | tf_op jit(solution)/shard_map/ppermute | solution.py:405
  277.0 24.5 %collective-permute-start.8 = (f32[2,2,256,128]{3,2,1,0:T(8,128)S(1)}, f32[2,2,256,128]{3,2,1,0:T(8,128)S(1)}, u32[]{:S(2)}, u32[]{:S(2)}) collective-permute-start(f32[2,2,256,128]{3,2,1,0:T(8,128)S(1)} %get-tuple-element.43), channel_id=1, source_target_pairs={{0,3},{1,2},{2,1},{3,0},{4,7},{5,6},{6,5},{7,4},{8,11},{9,10},{10,... | collective-permute-start | bytes 1572872 | tf_op jit(solution)/shard_map/ppermute | solution.py:405

commit v4 on v3

--- a/solution.py
+++ b/solution.py
@@ -14,8 +14,10 @@
 LANES = 128
 MIX_WEIGHT = 480
 LINE_WEIGHT = 3000
+BACK_WEIGHT = 3000
+ADD_STEP = 128
 MIDDLE_UNROLL = 4
-PLAN = ((0, 1), (2, 3))
+PLAN = ((0,), (1,), (2, 3))
 VMEM_LIMIT = 48 * 1024 * 1024
 FIRSTS = (1, 2)
 
@@ -516,81 +518,142 @@
     return result
 
 
-def cut_kernel(which, place_ref, in_ref, *out_refs):
-    for k in range(GROUPS):
-        lanes = pl.ds(pl.multiple_of(place_ref[k] * LANES, LANES), LANES)
-        for part in range(2):
-            tiles = [in_ref[part, g, :, lanes] for g in range(GROUPS)]
-            if len(which) == 1:
-                out_refs[k][0, part] = pick_lanes(tiles, which[0])
-            else:
-                tiles = swap_lanes(tiles)
-                for index, q in enumerate(which):
-                    out_refs[k][index, part] = tiles[q]
-
-
-def cut_columns(density, places, which):
-    rows, columns = density.shape[2:]
+def cut_kernel(which, in_ref, out_ref):
+    for part in range(2):
+        tiles = [in_ref[part, g] for g in range(GROUPS)]
+        if len(which) == 1:
+            out_ref[0, part] = pick_lanes(tiles, which[0])
+        else:
+            tiles = swap_lanes(tiles)
+            for index, q in enumerate(which):
+                out_ref[index, part] = tiles[q]
+
+
+def cut_columns(density, which, partner):
+    rows = density.shape[2]
     step = min(rows, 128)
-    block = pl.BlockSpec((len(which), 2, step, LANES), lambda i: (0, 0, i, 0))
-    shape = jax.ShapeDtypeStruct((len(which), 2, rows, LANES), jnp.float32)
     return pl.pallas_call(
         functools.partial(cut_kernel, which),
         grid=(rows // step,),
-        out_shape=[shape] * GROUPS,
         in_specs=[
-            pl.BlockSpec(memory_space=pltpu.SMEM),
-            pl.BlockSpec((2, GROUPS, step, columns), lambda i: (0, 0, i, 0)),
+            pl.BlockSpec(
+                (2, GROUPS, step, LANES), lambda i: (0, 0, i, lax.axis_index("narrow") ^ partner)
+            )
         ],
-        out_specs=[block] * GROUPS,
+        out_specs=pl.BlockSpec((len(which), 2, step, LANES), lambda i: (0, 0, i, 0)),
+        out_shape=jax.ShapeDtypeStruct((len(which), 2, rows, LANES), jnp.float32),
         compiler_params=params(),
         cost_estimate=pl.CostEstimate(
-            flops=8 * rows * columns * len(which),
-            bytes_accessed=40 * rows * columns,
+            flops=8 * rows * LANES * len(which),
+            bytes_accessed=40 * rows * LANES,
             transcendentals=0,
         ),
         name="cut",
-    )(places, density)
-
-
-def place_kernel(chunks, order, place_ref, *refs):
+    )(density)
+
+
+def place_kernel(order, *refs):
     inputs, out_ref = refs[:-1], refs[-1]
+    device = lax.axis_index("narrow")
     for k in range(GROUPS):
-        lanes = pl.ds(pl.multiple_of(place_ref[k] * LANES, LANES), LANES)
+        lanes = pl.ds(pl.multiple_of((device ^ k) * LANES, LANES), LANES)
         for part in range(2):
-            tiles = [inputs[c * GROUPS + k][index, part] for c, index in order]
-            tiles = swap_lanes(tiles)
+            tiles = [
+                jnp.zeros(out_ref.shape[2:3] + (LANES,), jnp.float32)
+                if spot is None
+                else inputs[spot[0] * GROUPS + k][spot[1], part]
+                for spot in order
+            ]
+            for g, value in enumerate(swap_lanes(tiles)):
+                out_ref[part, g, :, lanes] = value
+
+
+def add_kernel(which, *refs):
+    inputs, so_far_ref, out_ref = refs[:4], refs[4], refs[5]
+    device = lax.axis_index("narrow")
+    group = lax.broadcasted_iota(jnp.int32, (out_ref.shape[2], LANES), 1) // WIDTH
+    for k in range(GROUPS):
+        lanes = pl.ds(pl.multiple_of((device ^ k) * LANES, LANES), LANES)
+        for part in range(2):
+            tile = inputs[k][0, part]
             for g in range(GROUPS):
-                out_ref[part, g, :, lanes] = tiles[g]
-
-
-def place_columns(chunks, plan, places):
-    rows = chunks[0][0].shape[2]
-    step = min(rows, 128)
-    where = {q: (c, index) for c, which in enumerate(plan) for index, q in enumerate(which)}
-    order = [where[q] for q in range(GROUPS)]
-    specs, operands = [], []
+                distance = (which - g) * WIDTH % LANES
+                moved = pltpu.roll(tile, distance, 1) if distance else tile
+                value = jnp.where(group == which, moved, so_far_ref[part, g, :, lanes])
+                out_ref[part, g, :, lanes] = value
+
+
+def place_columns(chunks, plan):
+    specs, operands, order = [], [], [None] * GROUPS
     for which, chunk in zip(plan, chunks):
+        if chunk is None:
+            continue
+        rows = chunk[0].shape[2]
+        step = min(rows, 128)
+        for index, q in enumerate(which):
+            order[q] = (len(operands) // GROUPS, index)
         specs += [pl.BlockSpec((len(which), 2, step, LANES), lambda i: (0, 0, i, 0))] * GROUPS
         operands += list(chunk)
     shape = (2, GROUPS, rows, GROUPS * LANES)
     return pl.pallas_call(
-        functools.partial(place_kernel, len(plan), order),
+        functools.partial(place_kernel, order),
         grid=(rows // step,),
         out_shape=jax.ShapeDtypeStruct(shape, jnp.float32),
-        in_specs=[pl.BlockSpec(memory_space=pltpu.SMEM)] + specs,
+        in_specs=specs,
         out_specs=pl.BlockSpec((2, GROUPS, step, GROUPS * LANES), lambda i: (0, 0, i, 0)),
         compiler_params=params(),
         cost_estimate=pl.CostEstimate(
             flops=64 * rows * LANES, bytes_accessed=128 * rows * LANES, transcendentals=0
         ),
         name="place",
-    )(places, *operands)
-
-
-def lines_forward_kernel(rows, slot_ref, mix_ref, high_ref, low_ref, head_ref, turn_ref, *refs):
-    inputs, out_ref, first, second = refs[:4], refs[4], refs[5], refs[6]
+    )(*operands)
+
+
+def add_columns(chunk, which, so_far):
+    rows = chunk[0].shape[2]
+    step = min(rows, ADD_STEP)
+    block = pl.BlockSpec((2, GROUPS, step, GROUPS * LANES), lambda i: (0, 0, i, 0))
+    return pl.pallas_call(
+        functools.partial(add_kernel, which),
+        grid=(rows // step,),
+        out_shape=jax.ShapeDtypeStruct(so_far.shape, jnp.float32),
+        in_specs=[pl.BlockSpec((1, 2, step, LANES), lambda i: (0, 0, i, 0))] * GROUPS + [block],
+        out_specs=block,
+        input_output_aliases={GROUPS: 0},
+        compiler_params=params(),
+        cost_estimate=pl.CostEstimate(
+            flops=64 * rows * LANES, bytes_accessed=128 * rows * LANES, transcendentals=0
+        ),
+        name="add",
+    )(*chunk, so_far)
+
+
+def fetch(sources, held, semaphores):
+    copies = [
+        pltpu.make_async_copy(source, there, semaphores.at[i])
+        for i, (source, there) in enumerate(zip(sources, held))
+    ]
+
+    @pl.when(pl.program_id(0) == 0)
+    def start():
+        for copy in copies:
+            copy.start()
+
+    def wait(*which):
+        @pl.when(pl.program_id(0) == 0)
+        def finish_copies():
+            for i in which:
+                copies[i].wait()
+
+    return wait
+
+
+def lines_forward_kernel(rows, slot_ref, *refs):
+    sources, inputs = refs[:4], refs[4:8]
+    out_ref, first, second, head_ref, mix_ref, matrix_ref, turn_ref, semaphores = refs[8:]
     tile = 8
+    wait = fetch(sources, (head_ref, mix_ref, matrix_ref, turn_ref), semaphores)
+    wait(0)
 
     def step(index, carry):
         place = pl.ds(pl.multiple_of(index * tile, tile), tile)
@@ -612,6 +675,7 @@
         return carry
 
     lax.fori_loop(0, rows // tile, step, 0)
+    wait(1, 2, 3)
     dot = functools.partial(jnp.dot, preferred_element_type=jnp.float32)
     for k in range(4):
         value = first[k]
@@ -625,33 +689,39 @@
         second[rows:, k * LANES : (k + 1) * LANES] = imag_part
     for side in range(2):
         lanes = slice(2 * side * LANES, 2 * (side + 1) * LANES)
-        value = dot3(high_ref[...], low_ref[...], second[:, lanes], True)
+        value = dot3(matrix_ref[0], matrix_ref[1], second[:, lanes], True)
         for k in range(2):
             for part in range(2):
                 piece = value[part * rows : (part + 1) * rows, k * LANES : (k + 1) * LANES]
                 out_ref[:, 0, part, 2 * side + k] = piece.reshape(rows // tile, tile, LANES)
 
 
-def line_specs(rows, tables):
-    return [pl.BlockSpec(memory_space=pltpu.SMEM)] + [whole_spec(table.shape) for table in tables]
-
-
-def lines_forward(pieces, slots, head, orient_tables):
+def line_specs():
+    return [pl.BlockSpec(memory_space=pltpu.SMEM)] + [pl.BlockSpec(memory_space=pl.ANY)] * 4
+
+
+def line_scratch(rows, tables):
+    return (
+        [
+            pltpu.VMEM((4, rows, 2 * LANES), jnp.float32),
+            pltpu.VMEM((2 * rows, 4 * LANES), jnp.float32),
+        ]
+        + [pltpu.VMEM(table.shape, table.dtype) for table in tables]
+        + [pltpu.SemaphoreType.DMA((len(tables),))]
+    )
+
+
+def lines_forward(pieces, slots, head, tables):
     count, _, rows, _ = pieces[0].shape
-    mixing, matrix, turns = orient_tables
-    tables = [mixing, matrix[0], matrix[1], head, turns]
     places = rows // 8
     return pl.pallas_call(
         functools.partial(lines_forward_kernel, rows),
         grid=(count,),
         out_shape=jax.ShapeDtypeStruct((places, count, 2, 4, 8, LANES), jnp.float32),
-        in_specs=line_specs(rows, tables)
+        in_specs=line_specs()
         + [pl.BlockSpec((1, 2, rows, LANES), lambda i: (i, 0, 0, 0))] * 4,
         out_specs=pl.BlockSpec((places, 1, 2, 4, 8, LANES), lambda i: (0, i, 0, 0, 0, 0)),
-        scratch_shapes=[
-            pltpu.VMEM((4, rows, 2 * LANES), jnp.float32),
-            pltpu.VMEM((2 * rows, 4 * LANES), jnp.float32),
-        ],
+        scratch_shapes=line_scratch(rows, (head, *tables)),
         compiler_params=params(),
         cost_estimate=pl.CostEstimate(
             flops=LINE_WEIGHT * rows * rows * LANES * count,
@@ -659,20 +729,24 @@
             transcendentals=0,
         ),
         name="lines_forward",
-    )(slots, *tables, *pieces)
-
-
-def lines_inverse_kernel(rows, slot_ref, mix_ref, high_ref, low_ref, head_ref, turn_ref, in_ref, *refs):
-    outputs, first, second = refs[:4], refs[4], refs[5]
+    )(slots, head, *tables, *pieces)
+
+
+def lines_inverse_kernel(rows, slot_ref, *refs):
+    sources, in_ref, outputs = refs[:4], refs[4], refs[5:9]
+    first, second, head_ref, mix_ref, matrix_ref, turn_ref, semaphores = refs[9:]
     tile = 8
+    wait = fetch(sources, (head_ref, mix_ref, matrix_ref, turn_ref), semaphores)
     for k in range(4):
         for part in range(2):
             piece = in_ref[:, 0, part, k].reshape(rows, LANES)
             second[part * rows : (part + 1) * rows, k * LANES : (k + 1) * LANES] = piece
     dot = functools.partial(jnp.dot, preferred_element_type=jnp.float32)
+    wait(2)
     for side in range(2):
         lanes = slice(2 * side * LANES, 2 * (side + 1) * LANES)
-        second[:, lanes] = dot3(high_ref[...], low_ref[...], second[:, lanes], True)
+        second[:, lanes] = dot3(matrix_ref[0], matrix_ref[1], second[:, lanes], True)
+    wait(0, 1, 3)
     for k in range(4):
         lanes = slice(k * LANES, (k + 1) * LANES)
         real_part, imag_part = c_mul(
@@ -701,30 +775,25 @@
     lax.fori_loop(0, rows // tile, step, 0)
 
 
-def lines_inverse(blocks, slots, head, orient_tables):
+def lines_inverse(blocks, slots, head, tables):
     places, count = blocks.shape[:2]
     rows = places * 8
-    mixing, matrix, turns = orient_tables
-    tables = [mixing, matrix[0], matrix[1], head, turns]
     return pl.pallas_call(
         functools.partial(lines_inverse_kernel, rows),
         grid=(count,),
         out_shape=[jax.ShapeDtypeStruct((count, 2, rows, LANES), jnp.float32)] * 4,
-        in_specs=line_specs(rows, tables)
+        in_specs=line_specs()
         + [pl.BlockSpec((places, 1, 2, 4, 8, LANES), lambda i: (0, i, 0, 0, 0, 0))],
         out_specs=[pl.BlockSpec((1, 2, rows, LANES), lambda i: (i, 0, 0, 0))] * 4,
-        scratch_shapes=[
-            pltpu.VMEM((4, rows, 2 * LANES), jnp.float32),
-            pltpu.VMEM((2 * rows, 4 * LANES), jnp.float32),
-        ],
+        scratch_shapes=line_scratch(rows, (head, *tables)),
         compiler_params=params(),
         cost_estimate=pl.CostEstimate(
-            flops=LINE_WEIGHT * rows * rows * LANES * count,
+            flops=BACK_WEIGHT * rows * rows * LANES * count,
             bytes_accessed=64 * rows * LANES * count,
             transcendentals=0,
         ),
         name="lines_inverse",
-    )(slots, *tables, blocks)
+    )(slots, head, *tables, blocks)
 
 
 def row_filter_kernel(plan, slots, forward_ref, inverse_ref, turn_ref, green_ref, *refs):
@@ -876,15 +945,21 @@
     head = phase[:, :, None, None] * np.exp(-1j * angle)
     head = pick(np.stack([head.real, head.imag], axis=2).astype(np.float32), device)
     slots = pick(slots.astype(np.int32), device)
-    turns = turn(group[None, :] * np.arange(rows)[:, None], GROUPS * rows)
-    turns = jnp.asarray(np.moveaxis(turns, 2, 0))
+    turns = np.moveaxis(turn(group[None, :] * np.arange(rows)[:, None], GROUPS * rows), 2, 0)
     four = np.exp(-2j * np.pi * (np.outer(partners, partners) % 4) / 4)
     mixing = np.round(np.kron(four, np.eye(WIDTH)))
     ahead = np.block([[mixing.real, mixing.imag], [-mixing.imag, mixing.real]])
-    back = np.block([[mixing.real, -mixing.imag], [mixing.imag, mixing.real]])
-    tables = (jnp.asarray(ahead.astype(jnp.bfloat16)), jnp.asarray(dft_matrix(rows, -1, True)), turns)
-    tables_back = (jnp.asarray(back.astype(jnp.bfloat16)), jnp.asarray(dft_matrix(rows, 1, True)), turns)
-    places = device ^ jnp.asarray(partners.astype(np.int32))
+    backward = np.block([[mixing.real, -mixing.imag], [mixing.imag, mixing.real]])
+    tables = (
+        jnp.asarray(ahead.astype(jnp.bfloat16)),
+        jnp.asarray(dft_matrix(rows, -1, True)),
+        jnp.asarray(turns),
+    )
+    tables_back = (
+        jnp.asarray(backward.astype(jnp.bfloat16)),
+        jnp.asarray(dft_matrix(rows, 1, True)),
+        jnp.asarray(turns),
+    )
     cell = np.tile(np.arange(WIDTH), GROUPS)
     x_turns = turn(np.arange(modes)[:, None] * cell[None, :], total_x)
     x_turns = jnp.asarray(np.moveaxis(x_turns, 2, 0))
@@ -898,24 +973,34 @@
     source = density.reshape(2, GROUPS, rows, x_local)
 
     def send(pieces):
-        return [pieces[0]] + [swap(pieces[k], "narrow", k) for k in range(1, 4)]
+        moved = {k: swap(pieces[k], "narrow", k) for k in (3, 1, 2)}
+        return [pieces[0], moved[1], moved[2], moved[3]]
 
     def trade_all(blocks):
         return lax.all_to_all(blocks, ("narrow", "wide"), 0, 0, tiled=True)
 
-    arrived, got = [], None
-    for which in PLAN:
-        pieces = cut_columns(source if got is None else source, places, which)
+    arrived, got, made = [], None, []
+    for c, which in enumerate(PLAN):
+        wanted = after(source, made[c - 2]) if c >= 2 else source
+        pieces = [cut_columns(wanted, which, k) for k in range(4)]
         got = send(pieces if got is None else after(pieces, got))
-        arrived.append(trade_all(lines_forward(got, slots, head, tables)))
+        made.append(lines_forward(got, slots, head, tables))
+        arrived.append(trade_all(made[c]))
 
     filtered = row_filter(arrived, PLAN, x_turns, green, wide)
 
-    back = [None] * len(PLAN)
+    back, blocks, made = [None] * len(PLAN), None, []
     for c in reversed(range(len(PLAN))):
-        pieces = lines_inverse(trade_all(filtered[c]), slots, head, tables_back)
-        back[c] = send(pieces)
-    return place_columns(back, PLAN, places).reshape(density.shape)
+        wanted = filtered[c] if blocks is None else after(filtered[c], blocks)
+        if len(made) >= 2:
+            wanted = after(wanted, made[-2])
+        blocks = trade_all(wanted)
+        made.append(lines_inverse(blocks, slots, head, tables_back))
+        back[c] = send(made[-1] if c + 1 == len(PLAN) else after(made[-1], back[c + 1]))
+    if len(PLAN[0]) > 1:
+        return place_columns(back, PLAN).reshape(density.shape)
+    so_far = place_columns([None] + back[1:], PLAN)
+    return add_columns(back[0], PLAN[0][0], so_far).reshape(density.shape)
 
 
 def plane(density, plane_wave):

time: 307 us -> 300 us (0.977)
  waiting for transfers between devices: 171 us -> 124 us
  local copies, waits for them, and re-layouts: 4.25 us -> 19.7 us
  starting transfers between devices: 27.3 us -> 38.9 us
  Pallas kernels: 48.9 us -> 58.3 us
    all_to_all x3 -> x5, waiting for transfers between devices: 109 us -> 85.6 us  [trade_all(): return lax.all_to_all(blocks, ('narrow', 'wide'), 0, 0, tiled=True)]
    ppermute x12 -> x18, waiting for transfers between devices: 61.1 us -> 38 us  [swap(): return lax.ppermute(value, axis, pairs)]
    unnamed x36 -> x46, local copies, waits for them, and re-layouts: 2.15 us -> 17.7 us
    ppermute x12 -> x18, starting transfers between devices: 15 us -> 22.2 us  [swap(): return lax.ppermute(value, axis, pairs)]
    pallas_call x1 -> x2, Pallas kernels: 4.9 us -> 9.31 us  [the longest x1 5.14 us: place_columns(): pl.pallas_call(functools.partial(place_kernel, order), grid=(rows // step...]
    all_to_all x3 -> x5, starting transfers between devices: 12.3 us -> 16.7 us  [trade_all(): return lax.all_to_all(blocks, ('narrow', 'wide'), 0, 0, tiled=True)]
    pallas_call x2 -> x3, Pallas kernels: 11.2 us -> 13.3 us  [lines_inverse(): pl.pallas_call(functools.partial(lines_inverse_kernel, rows), grid=(count...]
    pallas_call x2 -> x3, Pallas kernels: 11.6 us -> 13.8 us  [lines_forward(): pl.pallas_call(functools.partial(lines_forward_kernel, rows), grid=(count...]
  transfers between devices with their start and end apart: 15 -> 23, of which waited for: 10 -> 11; matrix products, arithmetic and copies ran while one was open for 1% -> 2% of each run, Pallas kernels for 9% -> 14%
where the time goes in v4:
time: 300 us; the launch traced here: 299 us
  waiting for transfers between devices  124 us (41%)
  Pallas kernels  58.3 us (19%)
  blocking collectives  53.5 us (18%)
  starting transfers between devices  38.9 us (13%)
  local copies, waits for them, and re-layouts  19.7 us (7%)
  other arithmetic  3.57 us (1%)
    all_to_all x5, waiting for transfers between devices, trade_all(): return lax.all_to_all(blocks, ('narrow', 'wide'), 0, 0, tiled=True)  85.6 us
    all_to_all x1, blocking collectives, trade_all(): return lax.all_to_all(blocks, ('narrow', 'wide'), 0, 0, tiled=True)  53.5 us
    ppermute x18, waiting for transfers between devices, swap(): return lax.ppermute(value, axis, pairs)  38 us
    ppermute x18, starting transfers between devices, swap(): return lax.ppermute(value, axis, pairs)  22.2 us
    unnamed x46, local copies, waits for them, and re-layouts  17.7 us
    all_to_all x5, starting transfers between devices, trade_all(): return lax.all_to_all(blocks, ('narrow', 'wide'), 0, 0, tiled=True)  16.7 us
    pallas_call x3, Pallas kernels, lines_forward(): pl.pallas_call(functools.partial(lines_forward_kernel, rows), grid=(count...  13.8 us
    pallas_call x3, Pallas kernels, lines_inverse(): pl.pallas_call(functools.partial(lines_inverse_kernel, rows), grid=(count...  13.3 us
  transfers between devices with their start and end apart: 23, of which 11 were waited for; matrix products, arithmetic and copies ran while one was open for 2% of the time, Pallas kernels for 14%

profile of v4, /device:TPU:0, one launch (start us, length us, event | category | flops | bytes accessed | tf_op | source)
XLA Modules:
  0.0 298.7 jit_solution(93240461897062924)
XLA Ops:
  0.0 2.2 copy-done
  2.7 3.0 %collective-permute-start = (f32[1,2,256,128]{3,2,1,0:T(8,128)S(1)}, f32[1,2,256,128]{3,2,1,0:T(8,128)S(1)}, u32[]{:S(2)}, u32[]{:S(2)}) collective-permute-start(f32[1,2,256,128]{3,2,1,0:T(8,128)S(1)} %cut.13), channel_id=1, source_target_pairs={{0,1},{1,0},{2,3},{3,2},{4,5},{5,4},{6,7},{7,6},{8,9},{9,8},{10,11... | collective-permute-start | bytes 786440 | tf_op jit(solution)/shard_map/ppermute | solution.py:407
  6.3 1.6 collective-permute-start.1
  9.7 0.6 cut.18
  10.2 0.6 cut.17
  11.4 0.7 dynamic-slice_bitcast_fusion.1.slot_ref
  12.1 1.3 dynamic-slice_bitcast_fusion.refs_0_
  13.4 6.4 %collective-permute-done.1.refs_6_ = f32[1,2,256,128]{3,2,1,0:T(8,128)} collective-permute-done((f32[1,2,256,128]{3,2,1,0:T(8,128)S(1)}, f32[1,2,256,128]{3,2,1,0:T(8,128)}, u32[]{:S(2)}, u32[]{:S(2)}) %collective-permute-start.1) | collective-permute-done | bytes 262176 | tf_op jit(solution)/shard_map/ppermute | solution.py:407
  19.9 0.6 collective-permute-start.3
  20.5 1.4 collective-permute-start.4
  21.9 1.4 collective-permute-start.5
  23.3 1.2 copy-done.11
  24.6 0.9 copy-done.14
  25.5 4.2 %lines_forward.3 = f32[32,1,2,4,8,128]{5,4,3,2,1,0:T(8,128)} custom-call(s32[4]{0:T(128)S(1)} %dynamic-slice_bitcast_fusion.1.slot_ref, f32[4,2,256,128]{3,2,1,0:T(8,128)S(1)} %dynamic-slice_bitcast_fusion.refs_0_, bf16[256,256]{1,0:T(8,128)(2,1)S(1)} %copy-done.22, bf16[2,512,512]{2,1,0:T(8,128)(2,1)S(1)} %copy-done.11, f32[2,256,128]{2,1,0:T(8,128)S(1)} %copy-done.14, ...), custom_call_target="tpu_custom_call" | custom-call | flops 25165824000 | bytes 2097152 | tf_op jit(solution)/shard_map/lines_forward/pallas_call | solution.py:717
  29.7 4.9 %all-to-all-start = ((f32[32,1,2,4,8,128]{5,4,3,2,1,0:T(8,128)}), f32[32,1,2,4,8,128]{5,4,3,2,1,0:T(8,128)S(1)}, u32[]{:S(2)}, u32[]{:S(2)}) async-start(f32[32,1,2,4,8,128]{5,4,3,2,1,0:T(8,128)} %lines_forward.3), calls=%async_computation | async-start | bytes 2097152 | tf_op jit(solution)/shard_map/all_to_all | solution.py:980
  34.7 2.2 copy-done.1
  36.9 1.5 cut.23
  38.4 1.5 cut.22
  39.9 1.5 cut.21
  41.4 0.8 cut.20.refs_4_
  42.2 0.8 copy-done.6
  43.0 1.8 collective-permute-start.6
  44.8 1.5 collective-permute-start.7
  46.5 3.3 %lines_forward.4 = f32[32,1,2,4,8,128]{5,4,3,2,1,0:T(8,128)S(1)} custom-call(s32[4]{0:T(128)S(1)} %dynamic-slice_bitcast_fusion.1.slot_ref, f32[4,2,256,128]{3,2,1,0:T(8,128)S(1)} %dynamic-slice_bitcast_fusion.refs_0_, bf16[256,256]{1,0:T(8,128)(2,1)S(1)} %copy-done.22, bf16[2,512,512]{2,1,0:T(8,128)(2,1)S(1)} %copy-done.12, f32[2,256,128]{2,1,0:T(8,128)S(1)} %copy-done.15, ...), custom_call_target="tpu_custom_call" | custom-call | flops 25165824000 | bytes 2097152 | tf_op jit(solution)/shard_map/lines_forward/pallas_call | solution.py:717
  49.9 1.0 copy-done.3
  50.9 11.4 %all-to-all-done.refs_0_ = f32[32,1,2,4,8,128]{5,4,3,2,1,0:T(8,128)S(1)} async-done(((f32[32,1,2,4,8,128]{5,4,3,2,1,0:T(8,128)}), f32[32,1,2,4,8,128]{5,4,3,2,1,0:T(8,128)S(1)}, u32[]{:S(2)}, u32[]{:S(2)}) %all-to-all-start) | async-done | bytes 1048608 | tf_op jit(solution)/shard_map/all_to_all | solution.py:980
  62.3 2.6 all-to-all-start.1
  64.9 15.8 %collective-permute-done.8.refs_7_ = f32[2,2,256,128]{3,2,1,0:T(8,128)} collective-permute-done((f32[2,2,256,128]{3,2,1,0:T(8,128)}, f32[2,2,256,128]{3,2,1,0:T(8,128)}, u32[]{:S(2)}, u32[]{:S(2)}) %collective-permute-start.8) | collective-permute-done | bytes 524320 | tf_op jit(solution)/shard_map/ppermute | solution.py:407
  80.7 1.0 copy-done.7
  81.7 1.2 copy-done.13
  83.0 6.3 %lines_forward.5 = f32[32,2,2,4,8,128]{5,4,3,2,1,0:T(8,128)} custom-call(s32[4]{0:T(128)S(1)} %dynamic-slice_bitcast_fusion.1.slot_ref, f32[4,2,256,128]{3,2,1,0:T(8,128)S(1)} %dynamic-slice_bitcast_fusion.refs_0_, bf16[256,256]{1,0:T(8,128)(2,1)S(1)} %copy-done.22, bf16[2,512,512]{2,1,0:T(8,128)(2,1)S(1)} %copy-done.13, f32[2,256,128]{2,1,0:T(8,128)S(1)} %copy-done.15, ...), custom_call_target="tpu_custom_call" | custom-call | flops 50331648000 | bytes 4194304 | tf_op jit(solution)/shard_map/lines_forward/pallas_call | solution.py:717
  89.2 3.3 %all-to-all-done.1.refs_1_ = f32[32,1,2,4,8,128]{5,4,3,2,1,0:T(8,128)S(1)} async-done(((f32[32,1,2,4,8,128]{5,4,3,2,1,0:T(8,128)}), f32[32,1,2,4,8,128]{5,4,3,2,1,0:T(8,128)S(1)}, u32[]{:S(2)}, u32[]{:S(2)}) %all-to-all-start.1) | async-done | bytes 1048608 | tf_op jit(solution)/shard_map/all_to_all | solution.py:980
  92.5 3.5 %all-to-all-start.2 = ((f32[32,2,2,4,8,128]{5,4,3,2,1,0:T(8,128)}), f32[32,2,2,4,8,128]{5,4,3,2,1,0:T(8,128)}, u32[]{:S(2)}, u32[]{:S(2)}) async-start(f32[32,2,2,4,8,128]{5,4,3,2,1,0:T(8,128)} %lines_forward.5), calls=%async_computation.2 | async-start | bytes 4194304 | tf_op jit(solution)/shard_map/all_to_all | solution.py:980
  96.7 0.7 fusion.1
  97.4 2.8 add_multiply_fusion.green_ref
  100.3 45.8 %all-to-all-done.2.refs_2_ = f32[32,2,2,4,8,128]{5,4,3,2,1,0:T(8,128)} async-done(((f32[32,2,2,4,8,128]{5,4,3,2,1,0:T(8,128)}), f32[32,2,2,4,8,128]{5,4,3,2,1,0:T(8,128)}, u32[]{:S(2)}, u32[]{:S(2)}) %all-to-all-start.2) | async-done | bytes 2097184 | tf_op jit(solution)/shard_map/all_to_all | solution.py:980
  146.1 0.9 copy-done.18
  147.0 0.9 copy-done.19
  148.0 12.1 %row_filter.1 = (f32[32,1,2,4,8,128]{5,4,3,2,1,0:T(8,128)}, f32[32,1,2,4,8,128]{5,4,3,2,1,0:T(8,128)S(1)}, f32[32,2,2,4,8,128]{5,4,3,2,1,0:T(8,128)}) custom-call(bf16[2,256,256]{2,1,0:T(8,128)(2,1)S(1)} %copy-done.19, bf16[2,256,256]{2,1,0:T(8,128)(2,1)S(1)} %copy-done.18, f32[2,128,128]{2,1,0:T(8,128)S(1)} %copy-done.21, ...), custom_call_target="tpu_custom_call" | custom-call | flops 6442450944 | bytes 10485760 | tf_op jit(solution)/shard_map/row_filter/pallas_call | solution.py:895
  160.1 53.5 %all_to_all.30.refs_4_ = f32[32,2,2,4,8,128]{5,4,3,2,1,0:T(8,128)} all-to-all(f32[32,2,2,4,8,128]{5,4,3,2,1,0:T(8,128)} %get-tuple-element.51), channel_id=1, replica_groups=mesh['wide'=8,'narrow'=4] {'narrow','wide'}, dimensions={0} | all-to-all | bytes 4194304 | tf_op jit(solution)/shard_map/all_to_all | solution.py:980
  213.6 3.0 all-to-all-start.4
  216.6 6.6 %lines_inverse.3 = (f32[2,2,256,128]{3,2,1,0:T(8,128)S(1)}, f32[2,2,256,128]{3,2,1,0:T(8,128)}, f32[2,2,256,128]{3,2,1,0:T(8,128)}, f32[2,2,256,128]{3,2,1,0:T(8,128)}) custom-call(s32[4]{0:T(128)S(1)} %dynamic-slice_bitcast_fusion.1.slot_ref, f32[4,2,256,128]{3,2,1,0:T(8,128)S(1)} %dynamic-slice_bitcast_fusion.refs_0_, bf16[256,256]{1,0:T(8,128)(2,1)S(1)} %copy-done.20, ...), custom_call_target="tpu_custom_call" | custom-call | flops 50331648000 | bytes 4194304 | tf_op jit(solution)/shard_map/lines_inverse/pallas_call | solution.py:781
  223.3 0.8 copy-done.4
  224.1 1.5 collective-permute-start.9
  225.6 1.5 collective-permute-start.10
  227.6 16.4 %all-to-all-done.4.refs_4_ = f32[32,1,2,4,8,128]{5,4,3,2,1,0:T(8,128)S(1)} async-done(((f32[32,1,2,4,8,128]{5,4,3,2,1,0:T(8,128)}), f32[32,1,2,4,8,128]{5,4,3,2,1,0:T(8,128)S(1)}, u32[]{:S(2)}, u32[]{:S(2)}) %all-to-all-start.4) | async-done | bytes 1048608 | tf_op jit(solution)/shard_map/all_to_all | solution.py:980
  244.0 2.6 all-to-all-start.5
  246.7 1.2 copy-done.9
  247.9 0.9 copy-done.16
  248.9 3.8 %lines_inverse.5 = (f32[1,2,256,128]{3,2,1,0:T(8,128)S(1)}, f32[1,2,256,128]{3,2,1,0:T(8,128)}, f32[1,2,256,128]{3,2,1,0:T(8,128)}, f32[1,2,256,128]{3,2,1,0:T(8,128)}) custom-call(s32[4]{0:T(128)S(1)} %dynamic-slice_bitcast_fusion.1.slot_ref, f32[4,2,256,128]{3,2,1,0:T(8,128)S(1)} %dynamic-slice_bitcast_fusion.refs_0_, bf16[256,256]{1,0:T(8,128)(2,1)S(1)} %copy-done.20, ...), custom_call_target="tpu_custom_call" | custom-call | flops 25165824000 | bytes 2097152 | tf_op jit(solution)/shard_map/lines_inverse/pallas_call | solution.py:781
  252.7 1.6 collective-permute-done.10.refs_6_
  254.2 7.9 %collective-permute-done.11.refs_7_ = f32[2,2,256,128]{3,2,1,0:T(8,128)} collective-permute-done((f32[2,2,256,128]{3,2,1,0:T(8,128)}, f32[2,2,256,128]{3,2,1,0:T(8,128)}, u32[]{:S(2)}, u32[]{:S(2)}) %collective-permute-start.11) | collective-permute-done | bytes 524320 | tf_op jit(solution)/shard_map/ppermute | solution.py:407
  262.1 1.6 collective-permute-start.12
  264.2 1.4 collective-permute-start.14
  265.6 8.7 %all-to-all-done.5.refs_4_ = f32[32,1,2,4,8,128]{5,4,3,2,1,0:T(8,128)S(1)} async-done(((f32[32,1,2,4,8,128]{5,4,3,2,1,0:T(8,128)}), f32[32,1,2,4,8,128]{5,4,3,2,1,0:T(8,128)S(1)}, u32[]{:S(2)}, u32[]{:S(2)}) %all-to-all-start.5) | async-done | bytes 1048608 | tf_op jit(solution)/shard_map/all_to_all | solution.py:980
  274.3 1.2 copy-done.10
  275.5 0.9 copy-done.17
  276.5 2.9 lines_inverse.4
  279.4 1.6 collective-permute-start.15
  281.5 1.4 collective-permute-start.17
  283.0 5.1 %place.1.refs_4_ = f32[2,4,256,512]{3,2,1,0:T(8,128)} custom-call(f32[1,2,256,128]{3,2,1,0:T(8,128)S(1)} %get-tuple-element.67.refs_0_, f32[1,2,256,128]{3,2,1,0:T(8,128)S(1)} %collective-permute-done.12.refs_1_, f32[1,2,256,128]{3,2,1,0:T(8,128)S(1)} %collective-permute-done.13.refs_2_, f32[1,2,256,128]{3,2,1,0:T(8,128)} %collective-permute-done.14.refs_3_, ...), custom_call_target="tpu_custom_call" | custom-call | flops 2097152 | bytes 4194304 | tf_op jit(solution)/shard_map/place/pallas_call | solution.py:598
  288.1 0.6 collective-permute-done.15.refs_1_
  288.7 5.8 %collective-permute-done.16.refs_2_ = f32[1,2,256,128]{3,2,1,0:T(8,128)S(1)} collective-permute-done((f32[1,2,256,128]{3,2,1,0:T(8,128)S(1)}, f32[1,2,256,128]{3,2,1,0:T(8,128)S(1)}, u32[]{:S(2)}, u32[]{:S(2)}) %collective-permute-start.16) | collective-permute-done | bytes 262176 | tf_op jit(solution)/shard_map/ppermute | solution.py:407
  294.5 4.2 %add.73 = f32[2,4,256,512]{3,2,1,0:T(8,128)} custom-call(f32[1,2,256,128]{3,2,1,0:T(8,128)S(1)} %get-tuple-element.71.refs_0_, f32[1,2,256,128]{3,2,1,0:T(8,128)S(1)} %collective-permute-done.15.refs_1_, f32[1,2,256,128]{3,2,1,0:T(8,128)S(1)} %collective-permute-done.16.refs_2_, ...), custom_call_target="tpu_custom_call", output_to_operand_aliasing={{}: (4, {})} | custom-call | flops 2097152 | bytes 4194304 | tf_op jit(solution)/shard_map/add/pallas_call | solution.py:616
  (54 shorter events, 5.3 us)
Async XLA Ops:
  0.0 2.2 copy-start
  2.7 10.7 %collective-permute-start = (f32[1,2,256,128]{3,2,1,0:T(8,128)S(1)}, f32[1,2,256,128]{3,2,1,0:T(8,128)S(1)}, u32[]{:S(2)}, u32[]{:S(2)}) collective-permute-start(f32[1,2,256,128]{3,2,1,0:T(8,128)S(1)} %cut.13), channel_id=1, source_target_pairs={{0,1},{1,0},{2,3},{3,2},{4,5},{5,4},{6,7},{7,6},{8,9},{9,8},{10,11... | collective-permute-start | bytes 786440 | tf_op jit(solution)/shard_map/ppermute | solution.py:407
  6.3 13.6 %collective-permute-start.1 = (f32[1,2,256,128]{3,2,1,0:T(8,128)S(1)}, f32[1,2,256,128]{3,2,1,0:T(8,128)}, u32[]{:S(2)}, u32[]{:S(2)}) collective-permute-start(f32[1,2,256,128]{3,2,1,0:T(8,128)S(1)} %cut.14), channel_id=1, source_target_pairs={{0,2},{1,3},{2,0},{3,1},{4,6},{5,7},{6,4},{7,5},{8,10},{9,11},{10,... | collective-permute-start | bytes 786440 | tf_op jit(solution)/shard_map/ppermute | solution.py:407
  8.4 11.4 %collective-permute-start.2 = (f32[1,2,256,128]{3,2,1,0:T(8,128)S(1)}, f32[1,2,256,128]{3,2,1,0:T(8,128)}, u32[]{:S(2)}, u32[]{:S(2)}) collective-permute-start(f32[1,2,256,128]{3,2,1,0:T(8,128)S(1)} %cut.15), channel_id=1, source_target_pairs={{0,3},{1,2},{2,1},{3,0},{4,7},{5,6},{6,5},{7,4},{8,11},{9,10},{10,... | collective-permute-start | bytes 786440 | tf_op jit(solution)/shard_map/ppermute | solution.py:407
  11.4 12.0 %copy-start.22 = (bf16[256,256]{1,0:T(8,128)(2,1)S(1)}, bf16[256,256]{1,0:T(8,128)(2,1)}, u32[]{:S(2)}) copy-start(bf16[256,256]{1,0:T(8,128)(2,1)} %constant.63.clone.refs_1_) | copy-start | bytes 393220
  19.9 23.1 %collective-permute-start.3 = (f32[1,2,256,128]{3,2,1,0:T(8,128)S(1)}, f32[1,2,256,128]{3,2,1,0:T(8,128)}, u32[]{:S(2)}, u32[]{:S(2)}) collective-permute-start(f32[1,2,256,128]{3,2,1,0:T(8,128)S(1)} %cut.17), channel_id=1, source_target_pairs={{0,1},{1,0},{2,3},{3,2},{4,5},{5,4},{6,7},{7,6},{8,9},{9,8},{10,11... | collective-permute-start | bytes 786440 | tf_op jit(solution)/shard_map/ppermute | solution.py:407
  20.5 22.5 %collective-permute-start.4 = (f32[1,2,256,128]{3,2,1,0:T(8,128)S(1)}, f32[1,2,256,128]{3,2,1,0:T(8,128)}, u32[]{:S(2)}, u32[]{:S(2)}) collective-permute-start(f32[1,2,256,128]{3,2,1,0:T(8,128)S(1)} %cut.18), channel_id=1, source_target_pairs={{0,2},{1,3},{2,0},{3,1},{4,6},{5,7},{6,4},{7,5},{8,10},{9,11},{10,... | collective-permute-start | bytes 786440 | tf_op jit(solution)/shard_map/ppermute | solution.py:407
  21.9 21.1 %collective-permute-start.5 = (f32[1,2,256,128]{3,2,1,0:T(8,128)S(1)}, f32[1,2,256,128]{3,2,1,0:T(8,128)}, u32[]{:S(2)}, u32[]{:S(2)}) collective-permute-start(f32[1,2,256,128]{3,2,1,0:T(8,128)S(1)} %cut.19), channel_id=1, source_target_pairs={{0,3},{1,2},{2,1},{3,0},{4,7},{5,6},{6,5},{7,4},{8,11},{9,10},{10,... | collective-permute-start | bytes 786440 | tf_op jit(solution)/shard_map/ppermute | solution.py:407
  23.3 1.2 copy-start.11
  24.6 0.9 copy-start.14
  29.7 32.5 %all-to-all-start = ((f32[32,1,2,4,8,128]{5,4,3,2,1,0:T(8,128)}), f32[32,1,2,4,8,128]{5,4,3,2,1,0:T(8,128)S(1)}, u32[]{:S(2)}, u32[]{:S(2)}) async-start(f32[32,1,2,4,8,128]{5,4,3,2,1,0:T(8,128)} %lines_forward.3), calls=%async_computation | async-start | bytes 2097152 | tf_op jit(solution)/shard_map/all_to_all | solution.py:980
  34.7 2.2 copy-start.1
  41.4 5.2 %copy-start.12 = (bf16[2,512,512]{2,1,0:T(8,128)(2,1)S(1)}, bf16[2,512,512]{2,1,0:T(8,128)(2,1)}, u32[]{:S(2)}) copy-start(bf16[2,512,512]{2,1,0:T(8,128)(2,1)} %constant.64.clone.refs_2_) | copy-start | bytes 3145732
  41.4 5.2 %copy-start.15 = (f32[2,256,128]{2,1,0:T(8,128)S(1)}, f32[2,256,128]{2,1,0:T(8,128)}, u32[]{:S(2)}) copy-start(f32[2,256,128]{2,1,0:T(8,128)} %constant.65.clone.refs_3_) | copy-start | bytes 786436
  42.2 0.8 copy-start.6
  43.0 21.9 %collective-permute-start.6 = (f32[2,2,256,128]{3,2,1,0:T(8,128)}, f32[2,2,256,128]{3,2,1,0:T(8,128)}, u32[]{:S(2)}, u32[]{:S(2)}) collective-permute-start(f32[2,2,256,128]{3,2,1,0:T(8,128)} %cut.21), channel_id=1, source_target_pairs={{0,1},{1,0},{2,3},{3,2},{4,5},{5,4},{6,7},{7,6},{8,9},{9,8},{10,11... | collective-permute-start | bytes 1572872 | tf_op jit(solution)/shard_map/ppermute | solution.py:407
  44.8 20.1 %collective-permute-start.7 = (f32[2,2,256,128]{3,2,1,0:T(8,128)}, f32[2,2,256,128]{3,2,1,0:T(8,128)}, u32[]{:S(2)}, u32[]{:S(2)}) collective-permute-start(f32[2,2,256,128]{3,2,1,0:T(8,128)} %cut.22), channel_id=1, source_target_pairs={{0,2},{1,3},{2,0},{3,1},{4,6},{5,7},{6,4},{7,5},{8,10},{9,11},{10,... | collective-permute-start | bytes 1572872 | tf_op jit(solution)/shard_map/ppermute | solution.py:407
  46.3 34.4 %collective-permute-start.8 = (f32[2,2,256,128]{3,2,1,0:T(8,128)}, f32[2,2,256,128]{3,2,1,0:T(8,128)}, u32[]{:S(2)}, u32[]{:S(2)}) collective-permute-start(f32[2,2,256,128]{3,2,1,0:T(8,128)} %cut.23), channel_id=1, source_target_pairs={{0,3},{1,2},{2,1},{3,0},{4,7},{5,6},{6,5},{7,4},{8,11},{9,10},{10,... | collective-permute-start | bytes 1572872 | tf_op jit(solution)/shard_map/ppermute | solution.py:407
  49.9 1.0 copy-start.3
  62.3 30.2 %all-to-all-start.1 = ((f32[32,1,2,4,8,128]{5,4,3,2,1,0:T(8,128)}), f32[32,1,2,4,8,128]{5,4,3,2,1,0:T(8,128)S(1)}, u32[]{:S(2)}, u32[]{:S(2)}) async-start(f32[32,1,2,4,8,128]{5,4,3,2,1,0:T(8,128)} %copy-done.3), calls=%async_computation.1 | async-start | bytes 2097152 | tf_op jit(solution)/shard_map/all_to_all | solution.py:980
  80.7 1.0 copy-start.7
  81.7 1.2 copy-start.13
  92.5 53.6 %all-to-all-start.2 = ((f32[32,2,2,4,8,128]{5,4,3,2,1,0:T(8,128)}), f32[32,2,2,4,8,128]{5,4,3,2,1,0:T(8,128)}, u32[]{:S(2)}, u32[]{:S(2)}) async-start(f32[32,2,2,4,8,128]{5,4,3,2,1,0:T(8,128)} %lines_forward.5), calls=%async_computation.2 | async-start | bytes 4194304 | tf_op jit(solution)/shard_map/all_to_all | solution.py:980
  96.0 50.1 %copy-start.21 = (f32[2,128,128]{2,1,0:T(8,128)S(1)}, f32[2,128,128]{2,1,0:T(8,128)}, u32[]{:S(2)}) copy-start(f32[2,128,128]{2,1,0:T(8,128)} %constant.68.clone.turn_ref) | copy-start | bytes 393220
  146.1 1.0 copy-start.18
  147.0 0.9 copy-start.19
  160.1 53.5 %copy-start.2 = (f32[32,1,2,4,8,128]{5,4,3,2,1,0:T(8,128)}, f32[32,1,2,4,8,128]{5,4,3,2,1,0:T(8,128)S(1)}, u32[]{:S(2)}) copy-start(f32[32,1,2,4,8,128]{5,4,3,2,1,0:T(8,128)S(1)} %get-tuple-element.52) | copy-start | bytes 3145732
  213.6 3.0 copy-start.8
  213.6 3.0 copy-start.20
  213.6 30.4 %all-to-all-start.4 = ((f32[32,1,2,4,8,128]{5,4,3,2,1,0:T(8,128)}), f32[32,1,2,4,8,128]{5,4,3,2,1,0:T(8,128)S(1)}, u32[]{:S(2)}, u32[]{:S(2)}) async-start(f32[32,1,2,4,8,128]{5,4,3,2,1,0:T(8,128)} %copy-done.2), calls=%async_computation.4 | async-start | bytes 2097152 | tf_op jit(solution)/shard_map/all_to_all | solution.py:980
  223.3 0.8 copy-start.4
  224.1 28.6 %collective-permute-start.9 = (f32[2,2,256,128]{3,2,1,0:T(8,128)}, f32[2,2,256,128]{3,2,1,0:T(8,128)}, u32[]{:S(2)}, u32[]{:S(2)}) collective-permute-start(f32[2,2,256,128]{3,2,1,0:T(8,128)} %get-tuple-element.55), channel_id=1, source_target_pairs={{0,1},{1,0},{2,3},{3,2},{4,5},{5,4},{6,7},{7,6},{8,9},{9,8},{10,11... | collective-permute-start | bytes 1572872 | tf_op jit(solution)/shard_map/ppermute | solution.py:407
  225.6 28.7 %collective-permute-start.10 = (f32[2,2,256,128]{3,2,1,0:T(8,128)}, f32[2,2,256,128]{3,2,1,0:T(8,128)}, u32[]{:S(2)}, u32[]{:S(2)}) collective-permute-start(f32[2,2,256,128]{3,2,1,0:T(8,128)} %get-tuple-element.56), channel_id=1, source_target_pairs={{0,2},{1,3},{2,0},{3,1},{4,6},{5,7},{6,4},{7,5},{8,10},{9,11},{10,... | collective-permute-start | bytes 1572872 | tf_op jit(solution)/shard_map/ppermute | solution.py:407
  227.1 35.1 %collective-permute-start.11 = (f32[2,2,256,128]{3,2,1,0:T(8,128)}, f32[2,2,256,128]{3,2,1,0:T(8,128)}, u32[]{:S(2)}, u32[]{:S(2)}) collective-permute-start(f32[2,2,256,128]{3,2,1,0:T(8,128)} %get-tuple-element.57), channel_id=1, source_target_pairs={{0,3},{1,2},{2,1},{3,0},{4,7},{5,6},{6,5},{7,4},{8,11},{9,10},{10,... | collective-permute-start | bytes 1572872 | tf_op jit(solution)/shard_map/ppermute | solution.py:407
  244.0 30.3 %all-to-all-start.5 = ((f32[32,1,2,4,8,128]{5,4,3,2,1,0:T(8,128)}), f32[32,1,2,4,8,128]{5,4,3,2,1,0:T(8,128)S(1)}, u32[]{:S(2)}, u32[]{:S(2)}) async-start(f32[32,1,2,4,8,128]{5,4,3,2,1,0:T(8,128)} %get-tuple-element.58), calls=%async_computation.5 | async-start | bytes 2097152 | tf_op jit(solution)/shard_map/all_to_all | solution.py:980
  246.7 1.2 copy-start.9
  247.9 0.9 copy-start.16
  262.1 20.9 %copy-start.5 = (f32[2,2,256,128]{3,2,1,0:T(8,128)S(1)}, f32[2,2,256,128]{3,2,1,0:T(8,128)}, u32[]{:S(2)}) copy-start(f32[2,2,256,128]{3,2,1,0:T(8,128)} %copy-done.4) | copy-start | bytes 1572868
  262.1 17.3 %collective-permute-start.12 = (f32[1,2,256,128]{3,2,1,0:T(8,128)}, f32[1,2,256,128]{3,2,1,0:T(8,128)S(1)}, u32[]{:S(2)}, u32[]{:S(2)}) collective-permute-start(f32[1,2,256,128]{3,2,1,0:T(8,128)} %get-tuple-element.68), channel_id=1, source_target_pairs={{0,1},{1,0},{2,3},{3,2},{4,5},{5,4},{6,7},{7,6},{8,9},{9,8},{10,11... | collective-permute-start | bytes 786440 | tf_op jit(solution)/shard_map/ppermute | solution.py:407
  263.7 15.7 %collective-permute-start.13 = (f32[1,2,256,128]{3,2,1,0:T(8,128)}, f32[1,2,256,128]{3,2,1,0:T(8,128)S(1)}, u32[]{:S(2)}, u32[]{:S(2)}) collective-permute-start(f32[1,2,256,128]{3,2,1,0:T(8,128)} %get-tuple-element.69), channel_id=1, source_target_pairs={{0,2},{1,3},{2,0},{3,1},{4,6},{5,7},{6,4},{7,5},{8,10},{9,11},{10,... | collective-permute-start | bytes 786440 | tf_op jit(solution)/shard_map/ppermute | solution.py:407
  264.2 15.2 %collective-permute-start.14 = (f32[1,2,256,128]{3,2,1,0:T(8,128)}, f32[1,2,256,128]{3,2,1,0:T(8,128)}, u32[]{:S(2)}, u32[]{:S(2)}) collective-permute-start(f32[1,2,256,128]{3,2,1,0:T(8,128)} %get-tuple-element.70), channel_id=1, source_target_pairs={{0,3},{1,2},{2,1},{3,0},{4,7},{5,6},{6,5},{7,4},{8,11},{9,10},{10,... | collective-permute-start | bytes 786440 | tf_op jit(solution)/shard_map/ppermute | solution.py:407
  274.3 1.2 copy-start.10
  275.5 0.9 copy-start.17
  279.4 9.3 %collective-permute-start.15 = (f32[1,2,256,128]{3,2,1,0:T(8,128)S(1)}, f32[1,2,256,128]{3,2,1,0:T(8,128)S(1)}, u32[]{:S(2)}, u32[]{:S(2)}) collective-permute-start(f32[1,2,256,128]{3,2,1,0:T(8,128)S(1)} %get-tuple-element.72), channel_id=1, source_target_pairs={{0,1},{1,0},{2,3},{3,2},{4,5},{5,4},{6,7},{7,6},{8,9},{9,8},{10,11... | collective-permute-start | bytes 786440 | tf_op jit(solution)/shard_map/ppermute | solution.py:407
  281.0 13.5 %collective-permute-start.16 = (f32[1,2,256,128]{3,2,1,0:T(8,128)S(1)}, f32[1,2,256,128]{3,2,1,0:T(8,128)S(1)}, u32[]{:S(2)}, u32[]{:S(2)}) collective-permute-start(f32[1,2,256,128]{3,2,1,0:T(8,128)S(1)} %get-tuple-element.73), channel_id=1, source_target_pairs={{0,2},{1,3},{2,0},{3,1},{4,6},{5,7},{6,4},{7,5},{8,10},{9,11},{10,... | collective-permute-start | bytes 786440 | tf_op jit(solution)/shard_map/ppermute | solution.py:407
  281.5 13.0 %collective-permute-start.17 = (f32[1,2,256,128]{3,2,1,0:T(8,128)S(1)}, f32[1,2,256,128]{3,2,1,0:T(8,128)S(1)}, u32[]{:S(2)}, u32[]{:S(2)}) collective-permute-start(f32[1,2,256,128]{3,2,1,0:T(8,128)S(1)} %get-tuple-element.74), channel_id=1, source_target_pairs={{0,3},{1,2},{2,1},{3,0},{4,7},{5,6},{6,5},{7,4},{8,11},{9,10},{10,... | collective-permute-start | bytes 786440 | tf_op jit(solution)/shard_map/ppermute | solution.py:407

commit v5 on v4

--- a/solution.py
+++ b/solution.py
@@ -950,11 +950,15 @@
     mixing = np.round(np.kron(four, np.eye(WIDTH)))
     ahead = np.block([[mixing.real, mixing.imag], [-mixing.imag, mixing.real]])
     backward = np.block([[mixing.real, -mixing.imag], [mixing.imag, mixing.real]])
-    tables = (
-        jnp.asarray(ahead.astype(jnp.bfloat16)),
-        jnp.asarray(dft_matrix(rows, -1, True)),
-        jnp.asarray(turns),
-    )
+    way = lax.optimization_barrier(jnp.arange(2, dtype=jnp.int32))
+    tables = [
+        pick(np.stack([one, two]), way[0])
+        for one, two in (
+            (ahead.astype(jnp.bfloat16), backward.astype(jnp.bfloat16)),
+            (dft_matrix(rows, -1, True), dft_matrix(rows, 1, True)),
+            (turns, turns),
+        )
+    ]
     tables_back = (
         jnp.asarray(backward.astype(jnp.bfloat16)),
         jnp.asarray(dft_matrix(rows, 1, True)),

time: 300 us -> 297 us (0.990)
  waiting for transfers between devices: 124 us -> 121 us
    ppermute x18, waiting for transfers between devices: 38 us -> 31.8 us  [swap(): return lax.ppermute(value, axis, pairs)]
    all_to_all x5, waiting for transfers between devices: 85.6 us -> 89.2 us  [trade_all(): return lax.all_to_all(blocks, ('narrow', 'wide'), 0, 0, tiled=True)]
    unnamed x46 -> x54, local copies, waits for them, and re-layouts: 17.7 us -> 16.8 us
  transfers between devices with their start and end apart: 23 -> 23, of which waited for: 11 -> 11; matrix products, arithmetic and copies ran while one was open for 2% -> 1% of each run, Pallas kernels for 14% -> 14%
where the time goes in v5:
time: 297 us; the launch traced here: 296 us
  waiting for transfers between devices  121 us (41%)
  Pallas kernels  59.1 us (20%)
  blocking collectives  53.5 us (18%)
  starting transfers between devices  40.1 us (14%)
  local copies, waits for them, and re-layouts  18.9 us (6%)
    all_to_all x5, waiting for transfers between devices, trade_all(): return lax.all_to_all(blocks, ('narrow', 'wide'), 0, 0, tiled=True)  89.2 us
    all_to_all x1, blocking collectives, trade_all(): return lax.all_to_all(blocks, ('narrow', 'wide'), 0, 0, tiled=True)  53.5 us
    ppermute x18, waiting for transfers between devices, swap(): return lax.ppermute(value, axis, pairs)  31.8 us
    ppermute x18, starting transfers between devices, swap(): return lax.ppermute(value, axis, pairs)  22.2 us
    all_to_all x5, starting transfers between devices, trade_all(): return lax.all_to_all(blocks, ('narrow', 'wide'), 0, 0, tiled=True)  17.8 us
    unnamed x54, local copies, waits for them, and re-layouts  16.8 us
    pallas_call x3, Pallas kernels, lines_inverse(): pl.pallas_call(functools.partial(lines_inverse_kernel, rows), grid=(count...  13.4 us
    pallas_call x3, Pallas kernels, lines_forward(): pl.pallas_call(functools.partial(lines_forward_kernel, rows), grid=(count...  12.8 us
  transfers between devices with their start and end apart: 23, of which 11 were waited for; matrix products, arithmetic and copies ran while one was open for 1% of the time, Pallas kernels for 14%

profile of v5, /device:TPU:0, one launch (start us, length us, event | category | flops | bytes accessed | tf_op | source)
XLA Modules:
  0.0 295.8 jit_solution(13856916443444930976)
XLA Ops:
  0.0 2.2 copy-done
  2.2 0.5 cut.13
  2.7 3.0 %collective-permute-start = (f32[1,2,256,128]{3,2,1,0:T(8,128)S(1)}, f32[1,2,256,128]{3,2,1,0:T(8,128)}, u32[]{:S(2)}, u32[]{:S(2)}) collective-permute-start(f32[1,2,256,128]{3,2,1,0:T(8,128)S(1)} %cut.13), channel_id=1, source_target_pairs={{0,1},{1,0},{2,3},{3,2},{4,5},{5,4},{6,7},{7,6},{8,9},{9,8},{10,11... | collective-permute-start | bytes 786440 | tf_op jit(solution)/shard_map/ppermute | solution.py:407
  5.7 0.5 cut.14
  6.3 1.6 collective-permute-start.1
  8.7 1.3 dynamic-slice_bitcast_fusion.1.refs_0_
  10.0 0.7 fusion.2.slot_ref
  10.7 2.2 copy-done.1
  13.4 1.2 cut.19
  14.6 1.2 cut.18
  15.8 1.2 cut.17
  18.0 0.7 copy-done.22
  18.8 1.0 collective-permute-done.1.refs_6_
  19.9 1.0 collective-permute-start.3
  20.9 1.5 collective-permute-start.4
  22.4 1.0 collective-permute-start.5
  23.4 3.3 %lines_forward.3 = f32[32,1,2,4,8,128]{5,4,3,2,1,0:T(8,128)S(1)} custom-call(s32[4]{0:T(128)S(1)} %fusion.2.slot_ref, f32[4,2,256,128]{3,2,1,0:T(8,128)S(1)} %dynamic-slice_bitcast_fusion.1.refs_0_, bf16[256,256]{1,0:T(8,128)(2,1)S(1)} %dynamic-slice_bitcast_fusion.3.refs_1_, bf16[2,512,512]{2,1,0:T(8,128)(2,1)S(1)} %dynamic-slice_bitcast_fusion.refs_2_, ...), custom_call_target="tpu_custom_call" | custom-call | flops 25165824000 | bytes 2097152 | tf_op jit(solution)/shard_map/lines_forward/pallas_call | solution.py:717
  26.7 1.0 copy-done.3
  27.6 5.3 %all-to-all-start = ((f32[32,1,2,4,8,128]{5,4,3,2,1,0:T(8,128)}), f32[32,1,2,4,8,128]{5,4,3,2,1,0:T(8,128)S(1)}, u32[]{:S(2)}, u32[]{:S(2)}) async-start(f32[32,1,2,4,8,128]{5,4,3,2,1,0:T(8,128)} %copy-done.3), calls=%async_computation | async-start | bytes 2097152 | tf_op jit(solution)/shard_map/all_to_all | solution.py:984
  33.0 2.2 copy-done.2
  35.2 1.5 cut.23
  36.7 1.5 cut.22
  38.2 1.5 cut.21
  39.7 0.8 cut.20.refs_4_
  40.5 0.8 copy-done.7
  41.3 1.8 collective-permute-start.6
  43.1 1.5 collective-permute-start.7
  44.9 3.3 %lines_forward.4 = f32[32,1,2,4,8,128]{5,4,3,2,1,0:T(8,128)S(1)} custom-call(s32[4]{0:T(128)S(1)} %fusion.2.slot_ref, f32[4,2,256,128]{3,2,1,0:T(8,128)S(1)} %dynamic-slice_bitcast_fusion.1.refs_0_, bf16[256,256]{1,0:T(8,128)(2,1)S(1)} %dynamic-slice_bitcast_fusion.3.refs_1_, bf16[2,512,512]{2,1,0:T(8,128)(2,1)S(1)} %dynamic-slice_bitcast_fusion.refs_2_, ...), custom_call_target="tpu_custom_call" | custom-call | flops 25165824000 | bytes 2097152 | tf_op jit(solution)/shard_map/lines_forward/pallas_call | solution.py:717
  48.2 1.0 copy-done.4
  49.2 11.4 %all-to-all-done.refs_0_ = f32[32,1,2,4,8,128]{5,4,3,2,1,0:T(8,128)S(1)} async-done(((f32[32,1,2,4,8,128]{5,4,3,2,1,0:T(8,128)}), f32[32,1,2,4,8,128]{5,4,3,2,1,0:T(8,128)S(1)}, u32[]{:S(2)}, u32[]{:S(2)}) %all-to-all-start) | async-done | bytes 1048608 | tf_op jit(solution)/shard_map/all_to_all | solution.py:984
  60.6 3.4 %all-to-all-start.1 = ((f32[32,1,2,4,8,128]{5,4,3,2,1,0:T(8,128)}), f32[32,1,2,4,8,128]{5,4,3,2,1,0:T(8,128)}, u32[]{:S(2)}, u32[]{:S(2)}) async-start(f32[32,1,2,4,8,128]{5,4,3,2,1,0:T(8,128)} %copy-done.4), calls=%async_computation.1 | async-start | bytes 2097152 | tf_op jit(solution)/shard_map/all_to_all | solution.py:984
  64.0 15.0 %collective-permute-done.8.refs_7_ = f32[2,2,256,128]{3,2,1,0:T(8,128)} collective-permute-done((f32[2,2,256,128]{3,2,1,0:T(8,128)}, f32[2,2,256,128]{3,2,1,0:T(8,128)}, u32[]{:S(2)}, u32[]{:S(2)}) %collective-permute-start.8) | collective-permute-done | bytes 524320 | tf_op jit(solution)/shard_map/ppermute | solution.py:407
  79.0 1.0 copy-done.8
  80.0 6.2 %lines_forward.5 = f32[32,2,2,4,8,128]{5,4,3,2,1,0:T(8,128)} custom-call(s32[4]{0:T(128)S(1)} %fusion.2.slot_ref, f32[4,2,256,128]{3,2,1,0:T(8,128)S(1)} %dynamic-slice_bitcast_fusion.1.refs_0_, bf16[256,256]{1,0:T(8,128)(2,1)S(1)} %dynamic-slice_bitcast_fusion.3.refs_1_, bf16[2,512,512]{2,1,0:T(8,128)(2,1)S(1)} %dynamic-slice_bitcast_fusion.refs_2_, ...), custom_call_target="tpu_custom_call" | custom-call | flops 50331648000 | bytes 4194304 | tf_op jit(solution)/shard_map/lines_forward/pallas_call | solution.py:717
  86.3 5.3 %all-to-all-done.1.refs_1_ = f32[32,1,2,4,8,128]{5,4,3,2,1,0:T(8,128)} async-done(((f32[32,1,2,4,8,128]{5,4,3,2,1,0:T(8,128)}), f32[32,1,2,4,8,128]{5,4,3,2,1,0:T(8,128)}, u32[]{:S(2)}, u32[]{:S(2)}) %all-to-all-start.1) | async-done | bytes 1048608 | tf_op jit(solution)/shard_map/all_to_all | solution.py:984
  91.6 3.5 %all-to-all-start.2 = ((f32[32,2,2,4,8,128]{5,4,3,2,1,0:T(8,128)}), f32[32,2,2,4,8,128]{5,4,3,2,1,0:T(8,128)}, u32[]{:S(2)}, u32[]{:S(2)}) async-start(f32[32,2,2,4,8,128]{5,4,3,2,1,0:T(8,128)} %lines_forward.5), calls=%async_computation.2 | async-start | bytes 4194304 | tf_op jit(solution)/shard_map/all_to_all | solution.py:984
  95.8 2.0 add_multiply_fusion.green_ref
  97.8 47.3 %all-to-all-done.2.refs_2_ = f32[32,2,2,4,8,128]{5,4,3,2,1,0:T(8,128)} async-done(((f32[32,2,2,4,8,128]{5,4,3,2,1,0:T(8,128)}), f32[32,2,2,4,8,128]{5,4,3,2,1,0:T(8,128)}, u32[]{:S(2)}, u32[]{:S(2)}) %all-to-all-start.2) | async-done | bytes 2097184 | tf_op jit(solution)/shard_map/all_to_all | solution.py:984
  145.1 12.1 %row_filter.1 = (f32[32,1,2,4,8,128]{5,4,3,2,1,0:T(8,128)}, f32[32,1,2,4,8,128]{5,4,3,2,1,0:T(8,128)}, f32[32,2,2,4,8,128]{5,4,3,2,1,0:T(8,128)}) custom-call(bf16[2,256,256]{2,1,0:T(8,128)(2,1)S(1)} %copy-done.19, bf16[2,256,256]{2,1,0:T(8,128)(2,1)S(1)} %copy-done.18, f32[2,128,128]{2,1,0:T(8,128)S(1)} %copy-done.21, ...), custom_call_target="tpu_custom_call" | custom-call | flops 6442450944 | bytes 10485760 | tf_op jit(solution)/shard_map/row_filter/pallas_call | solution.py:895
  157.2 53.5 %all_to_all.30.refs_4_ = f32[32,2,2,4,8,128]{5,4,3,2,1,0:T(8,128)} all-to-all(f32[32,2,2,4,8,128]{5,4,3,2,1,0:T(8,128)} %get-tuple-element.51), channel_id=1, replica_groups=mesh['wide'=8,'narrow'=4] {'narrow','wide'}, dimensions={0} | all-to-all | bytes 4194304 | tf_op jit(solution)/shard_map/all_to_all | solution.py:984
  210.8 3.0 all-to-all-start.4
  213.8 6.6 %lines_inverse.3 = (f32[2,2,256,128]{3,2,1,0:T(8,128)S(1)}, f32[2,2,256,128]{3,2,1,0:T(8,128)}, f32[2,2,256,128]{3,2,1,0:T(8,128)}, f32[2,2,256,128]{3,2,1,0:T(8,128)}) custom-call(s32[4]{0:T(128)S(1)} %fusion.2.slot_ref, f32[4,2,256,128]{3,2,1,0:T(8,128)S(1)} %dynamic-slice_bitcast_fusion.1.refs_0_, bf16[256,256]{1,0:T(8,128)(2,1)S(1)} %copy-done.20, ...), custom_call_target="tpu_custom_call" | custom-call | flops 50331648000 | bytes 4194304 | tf_op jit(solution)/shard_map/lines_inverse/pallas_call | solution.py:781
  220.4 0.8 copy-done.5
  221.2 1.5 collective-permute-start.9
  222.7 1.5 collective-permute-start.10
  224.7 16.5 %all-to-all-done.4.refs_4_ = f32[32,1,2,4,8,128]{5,4,3,2,1,0:T(8,128)S(1)} async-done(((f32[32,1,2,4,8,128]{5,4,3,2,1,0:T(8,128)}), f32[32,1,2,4,8,128]{5,4,3,2,1,0:T(8,128)S(1)}, u32[]{:S(2)}, u32[]{:S(2)}) %all-to-all-start.4) | async-done | bytes 1048608 | tf_op jit(solution)/shard_map/all_to_all | solution.py:984
  241.1 2.6 all-to-all-start.5
  243.8 1.2 copy-done.13
  245.0 0.9 copy-done.16
  246.0 3.8 %lines_inverse.5 = (f32[1,2,256,128]{3,2,1,0:T(8,128)S(1)}, f32[1,2,256,128]{3,2,1,0:T(8,128)}, f32[1,2,256,128]{3,2,1,0:T(8,128)}, f32[1,2,256,128]{3,2,1,0:T(8,128)}) custom-call(s32[4]{0:T(128)S(1)} %fusion.2.slot_ref, f32[4,2,256,128]{3,2,1,0:T(8,128)S(1)} %dynamic-slice_bitcast_fusion.1.refs_0_, bf16[256,256]{1,0:T(8,128)(2,1)S(1)} %copy-done.20, ...), custom_call_target="tpu_custom_call" | custom-call | flops 25165824000 | bytes 2097152 | tf_op jit(solution)/shard_map/lines_inverse/pallas_call | solution.py:781
  249.8 1.6 collective-permute-done.10.refs_6_
  251.4 7.9 %collective-permute-done.11.refs_7_ = f32[2,2,256,128]{3,2,1,0:T(8,128)} collective-permute-done((f32[2,2,256,128]{3,2,1,0:T(8,128)}, f32[2,2,256,128]{3,2,1,0:T(8,128)}, u32[]{:S(2)}, u32[]{:S(2)}) %collective-permute-start.11) | collective-permute-done | bytes 524320 | tf_op jit(solution)/shard_map/ppermute | solution.py:407
  259.2 1.6 collective-permute-start.12
  261.3 1.4 collective-permute-start.14
  262.7 8.7 %all-to-all-done.5.refs_4_ = f32[32,1,2,4,8,128]{5,4,3,2,1,0:T(8,128)S(1)} async-done(((f32[32,1,2,4,8,128]{5,4,3,2,1,0:T(8,128)}), f32[32,1,2,4,8,128]{5,4,3,2,1,0:T(8,128)S(1)}, u32[]{:S(2)}, u32[]{:S(2)}) %all-to-all-start.5) | async-done | bytes 1048608 | tf_op jit(solution)/shard_map/all_to_all | solution.py:984
  271.4 1.2 copy-done.14
  272.7 0.9 copy-done.17
  273.6 2.9 lines_inverse.4
  276.6 1.6 collective-permute-start.15
  278.7 1.5 collective-permute-start.17
  280.1 5.1 %place.1.refs_4_ = f32[2,4,256,512]{3,2,1,0:T(8,128)} custom-call(f32[1,2,256,128]{3,2,1,0:T(8,128)S(1)} %get-tuple-element.67.refs_0_, f32[1,2,256,128]{3,2,1,0:T(8,128)S(1)} %collective-permute-done.12.refs_1_, f32[1,2,256,128]{3,2,1,0:T(8,128)S(1)} %collective-permute-done.13.refs_2_, f32[1,2,256,128]{3,2,1,0:T(8,128)} %collective-permute-done.14.refs_3_, ...), custom_call_target="tpu_custom_call" | custom-call | flops 2097152 | bytes 4194304 | tf_op jit(solution)/shard_map/place/pallas_call | solution.py:598
  285.3 0.6 collective-permute-done.15.refs_1_
  285.8 5.8 %collective-permute-done.16.refs_2_ = f32[1,2,256,128]{3,2,1,0:T(8,128)S(1)} collective-permute-done((f32[1,2,256,128]{3,2,1,0:T(8,128)S(1)}, f32[1,2,256,128]{3,2,1,0:T(8,128)S(1)}, u32[]{:S(2)}, u32[]{:S(2)}) %collective-permute-start.16) | collective-permute-done | bytes 262176 | tf_op jit(solution)/shard_map/ppermute | solution.py:407
  291.6 4.2 %add.82 = f32[2,4,256,512]{3,2,1,0:T(8,128)} custom-call(f32[1,2,256,128]{3,2,1,0:T(8,128)S(1)} %get-tuple-element.71.refs_0_, f32[1,2,256,128]{3,2,1,0:T(8,128)S(1)} %collective-permute-done.15.refs_1_, f32[1,2,256,128]{3,2,1,0:T(8,128)S(1)} %collective-permute-done.16.refs_2_, ...), custom_call_target="tpu_custom_call", output_to_operand_aliasing={{}: (4, {})} | custom-call | flops 2097152 | bytes 4194304 | tf_op jit(solution)/shard_map/add/pallas_call | solution.py:616
  (66 shorter events, 4.3 us)
Async XLA Ops:
  0.0 2.2 copy-start
  2.7 16.1 %collective-permute-start = (f32[1,2,256,128]{3,2,1,0:T(8,128)S(1)}, f32[1,2,256,128]{3,2,1,0:T(8,128)}, u32[]{:S(2)}, u32[]{:S(2)}) collective-permute-start(f32[1,2,256,128]{3,2,1,0:T(8,128)S(1)} %cut.13), channel_id=1, source_target_pairs={{0,1},{1,0},{2,3},{3,2},{4,5},{5,4},{6,7},{7,6},{8,9},{9,8},{10,11... | collective-permute-start | bytes 786440 | tf_op jit(solution)/shard_map/ppermute | solution.py:407
  6.3 2.4 copy-start.25
  6.3 13.6 %collective-permute-start.1 = (f32[1,2,256,128]{3,2,1,0:T(8,128)S(1)}, f32[1,2,256,128]{3,2,1,0:T(8,128)}, u32[]{:S(2)}, u32[]{:S(2)}) collective-permute-start(f32[1,2,256,128]{3,2,1,0:T(8,128)S(1)} %cut.14), channel_id=1, source_target_pairs={{0,2},{1,3},{2,0},{3,1},{4,6},{5,7},{6,4},{7,5},{8,10},{9,11},{10,... | collective-permute-start | bytes 786440 | tf_op jit(solution)/shard_map/ppermute | solution.py:407
  8.4 11.4 %collective-permute-start.2 = (f32[1,2,256,128]{3,2,1,0:T(8,128)S(1)}, f32[1,2,256,128]{3,2,1,0:T(8,128)}, u32[]{:S(2)}, u32[]{:S(2)}) collective-permute-start(f32[1,2,256,128]{3,2,1,0:T(8,128)S(1)} %cut.15), channel_id=1, source_target_pairs={{0,3},{1,2},{2,1},{3,0},{4,7},{5,6},{6,5},{7,4},{8,11},{9,10},{10,... | collective-permute-start | bytes 786440 | tf_op jit(solution)/shard_map/ppermute | solution.py:407
  10.7 2.2 copy-start.1
  17.0 1.0 copy-start.23
  17.0 1.8 copy-start.22
  18.7 4.6 %copy-start.9 = (f32[2,256,128]{2,1,0:T(8,128)}, f32[2,256,128]{2,1,0:T(8,128)S(1)}, u32[]{:S(2)}) copy-start(f32[2,256,128]{2,1,0:T(8,128)S(1)} %dynamic-slice_bitcast_fusion.2.refs_3_) | copy-start | bytes 786436
  19.9 21.4 %collective-permute-start.3 = (f32[1,2,256,128]{3,2,1,0:T(8,128)}, f32[1,2,256,128]{3,2,1,0:T(8,128)}, u32[]{:S(2)}, u32[]{:S(2)}) collective-permute-start(f32[1,2,256,128]{3,2,1,0:T(8,128)} %cut.17), channel_id=1, source_target_pairs={{0,1},{1,0},{2,3},{3,2},{4,5},{5,4},{6,7},{7,6},{8,9},{9,8},{10,11... | collective-permute-start | bytes 786440 | tf_op jit(solution)/shard_map/ppermute | solution.py:407
  20.9 20.4 %collective-permute-start.4 = (f32[1,2,256,128]{3,2,1,0:T(8,128)}, f32[1,2,256,128]{3,2,1,0:T(8,128)}, u32[]{:S(2)}, u32[]{:S(2)}) collective-permute-start(f32[1,2,256,128]{3,2,1,0:T(8,128)} %cut.18), channel_id=1, source_target_pairs={{0,2},{1,3},{2,0},{3,1},{4,6},{5,7},{6,4},{7,5},{8,10},{9,11},{10,... | collective-permute-start | bytes 786440 | tf_op jit(solution)/shard_map/ppermute | solution.py:407
  22.4 18.9 %collective-permute-start.5 = (f32[1,2,256,128]{3,2,1,0:T(8,128)}, f32[1,2,256,128]{3,2,1,0:T(8,128)}, u32[]{:S(2)}, u32[]{:S(2)}) collective-permute-start(f32[1,2,256,128]{3,2,1,0:T(8,128)} %cut.19), channel_id=1, source_target_pairs={{0,3},{1,2},{2,1},{3,0},{4,7},{5,6},{6,5},{7,4},{8,11},{9,10},{10,... | collective-permute-start | bytes 786440 | tf_op jit(solution)/shard_map/ppermute | solution.py:407
  26.7 1.0 copy-start.3
  27.6 32.9 %all-to-all-start = ((f32[32,1,2,4,8,128]{5,4,3,2,1,0:T(8,128)}), f32[32,1,2,4,8,128]{5,4,3,2,1,0:T(8,128)S(1)}, u32[]{:S(2)}, u32[]{:S(2)}) async-start(f32[32,1,2,4,8,128]{5,4,3,2,1,0:T(8,128)} %copy-done.3), calls=%async_computation | async-start | bytes 2097152 | tf_op jit(solution)/shard_map/all_to_all | solution.py:984
  33.0 2.2 copy-start.2
  39.7 5.2 %copy-start.10 = (f32[2,256,128]{2,1,0:T(8,128)S(1)}, f32[2,256,128]{2,1,0:T(8,128)}, u32[]{:S(2)}) copy-start(f32[2,256,128]{2,1,0:T(8,128)} %copy-done.9) | copy-start | bytes 786436
  40.5 0.8 copy-start.7
  41.3 22.7 %collective-permute-start.6 = (f32[2,2,256,128]{3,2,1,0:T(8,128)}, f32[2,2,256,128]{3,2,1,0:T(8,128)}, u32[]{:S(2)}, u32[]{:S(2)}) collective-permute-start(f32[2,2,256,128]{3,2,1,0:T(8,128)} %cut.21), channel_id=1, source_target_pairs={{0,1},{1,0},{2,3},{3,2},{4,5},{5,4},{6,7},{7,6},{8,9},{9,8},{10,11... | collective-permute-start | bytes 1572872 | tf_op jit(solution)/shard_map/ppermute | solution.py:407
  43.1 20.9 %collective-permute-start.7 = (f32[2,2,256,128]{3,2,1,0:T(8,128)}, f32[2,2,256,128]{3,2,1,0:T(8,128)}, u32[]{:S(2)}, u32[]{:S(2)}) collective-permute-start(f32[2,2,256,128]{3,2,1,0:T(8,128)} %cut.22), channel_id=1, source_target_pairs={{0,2},{1,3},{2,0},{3,1},{4,6},{5,7},{6,4},{7,5},{8,10},{9,11},{10,... | collective-permute-start | bytes 1572872 | tf_op jit(solution)/shard_map/ppermute | solution.py:407
  44.6 34.4 %collective-permute-start.8 = (f32[2,2,256,128]{3,2,1,0:T(8,128)}, f32[2,2,256,128]{3,2,1,0:T(8,128)}, u32[]{:S(2)}, u32[]{:S(2)}) collective-permute-start(f32[2,2,256,128]{3,2,1,0:T(8,128)} %cut.23), channel_id=1, source_target_pairs={{0,3},{1,2},{2,1},{3,0},{4,7},{5,6},{6,5},{7,4},{8,11},{9,10},{10,... | collective-permute-start | bytes 1572872 | tf_op jit(solution)/shard_map/ppermute | solution.py:407
  48.2 1.0 copy-start.4
  49.2 29.8 %copy-start.11 = (f32[2,256,128]{2,1,0:T(8,128)S(1)}, f32[2,256,128]{2,1,0:T(8,128)}, u32[]{:S(2)}) copy-start(f32[2,256,128]{2,1,0:T(8,128)} %copy-done.9) | copy-start | bytes 786436
  60.6 31.0 %all-to-all-start.1 = ((f32[32,1,2,4,8,128]{5,4,3,2,1,0:T(8,128)}), f32[32,1,2,4,8,128]{5,4,3,2,1,0:T(8,128)}, u32[]{:S(2)}, u32[]{:S(2)}) async-start(f32[32,1,2,4,8,128]{5,4,3,2,1,0:T(8,128)} %copy-done.4), calls=%async_computation.1 | async-start | bytes 2097152 | tf_op jit(solution)/shard_map/all_to_all | solution.py:984
  79.0 1.0 copy-start.8
  86.2 9.6 %copy-start.26 = (s32[32,128]{1,0:T(8,128)S(1)}, s32[32,128]{1,0:T(8,128)}, u32[]{:S(2)}) copy-start(s32[32,128]{1,0:T(8,128)} %constant.85.clone) | copy-start | bytes 49156
  86.2 9.6 %copy-start.24 = (s32[128,128]{1,0:T(8,128)S(1)}, s32[128,128]{1,0:T(8,128)}, u32[]{:S(2)}) copy-start(s32[128,128]{1,0:T(8,128)} %constant.90) | copy-start | bytes 196612
  91.6 53.6 %all-to-all-start.2 = ((f32[32,2,2,4,8,128]{5,4,3,2,1,0:T(8,128)}), f32[32,2,2,4,8,128]{5,4,3,2,1,0:T(8,128)}, u32[]{:S(2)}, u32[]{:S(2)}) async-start(f32[32,2,2,4,8,128]{5,4,3,2,1,0:T(8,128)} %lines_forward.5), calls=%async_computation.2 | async-start | bytes 4194304 | tf_op jit(solution)/shard_map/all_to_all | solution.py:984
  95.1 50.1 %copy-start.18 = (bf16[2,256,256]{2,1,0:T(8,128)(2,1)S(1)}, bf16[2,256,256]{2,1,0:T(8,128)(2,1)}, u32[]{:S(2)}) copy-start(bf16[2,256,256]{2,1,0:T(8,128)(2,1)} %constant.88.clone.inverse_ref) | copy-start | bytes 786436
  95.1 50.1 %copy-start.19 = (bf16[2,256,256]{2,1,0:T(8,128)(2,1)S(1)}, bf16[2,256,256]{2,1,0:T(8,128)(2,1)}, u32[]{:S(2)}) copy-start(bf16[2,256,256]{2,1,0:T(8,128)(2,1)} %constant.87.clone.forward_ref) | copy-start | bytes 786436
  95.1 50.1 %copy-start.21 = (f32[2,128,128]{2,1,0:T(8,128)S(1)}, f32[2,128,128]{2,1,0:T(8,128)}, u32[]{:S(2)}) copy-start(f32[2,128,128]{2,1,0:T(8,128)} %constant.84.clone.turn_ref) | copy-start | bytes 393220
  210.8 3.0 %copy-start.12 = (bf16[2,512,512]{2,1,0:T(8,128)(2,1)S(1)}, bf16[2,512,512]{2,1,0:T(8,128)(2,1)}, u32[]{:S(2)}) copy-start(bf16[2,512,512]{2,1,0:T(8,128)(2,1)} %constant.82.clone.refs_2_) | copy-start | bytes 3145732
  210.8 3.0 %copy-start.15 = (f32[2,256,128]{2,1,0:T(8,128)S(1)}, f32[2,256,128]{2,1,0:T(8,128)}, u32[]{:S(2)}) copy-start(f32[2,256,128]{2,1,0:T(8,128)} %constant.83.clone.refs_3_) | copy-start | bytes 786436
  210.8 3.0 %copy-start.20 = (bf16[256,256]{1,0:T(8,128)(2,1)S(1)}, bf16[256,256]{1,0:T(8,128)(2,1)}, u32[]{:S(2)}) copy-start(bf16[256,256]{1,0:T(8,128)(2,1)} %constant.81.clone.refs_1_) | copy-start | bytes 393220
  210.8 30.4 %all-to-all-start.4 = ((f32[32,1,2,4,8,128]{5,4,3,2,1,0:T(8,128)}), f32[32,1,2,4,8,128]{5,4,3,2,1,0:T(8,128)S(1)}, u32[]{:S(2)}, u32[]{:S(2)}) async-start(f32[32,1,2,4,8,128]{5,4,3,2,1,0:T(8,128)} %get-tuple-element.52), calls=%async_computation.4 | async-start | bytes 2097152 | tf_op jit(solution)/shard_map/all_to_all | solution.py:984
  220.4 0.8 copy-start.5
  221.2 28.6 %collective-permute-start.9 = (f32[2,2,256,128]{3,2,1,0:T(8,128)}, f32[2,2,256,128]{3,2,1,0:T(8,128)}, u32[]{:S(2)}, u32[]{:S(2)}) collective-permute-start(f32[2,2,256,128]{3,2,1,0:T(8,128)} %get-tuple-element.55), channel_id=1, source_target_pairs={{0,1},{1,0},{2,3},{3,2},{4,5},{5,4},{6,7},{7,6},{8,9},{9,8},{10,11... | collective-permute-start | bytes 1572872 | tf_op jit(solution)/shard_map/ppermute | solution.py:407
  222.7 28.7 %collective-permute-start.10 = (f32[2,2,256,128]{3,2,1,0:T(8,128)}, f32[2,2,256,128]{3,2,1,0:T(8,128)}, u32[]{:S(2)}, u32[]{:S(2)}) collective-permute-start(f32[2,2,256,128]{3,2,1,0:T(8,128)} %get-tuple-element.56), channel_id=1, source_target_pairs={{0,2},{1,3},{2,0},{3,1},{4,6},{5,7},{6,4},{7,5},{8,10},{9,11},{10,... | collective-permute-start | bytes 1572872 | tf_op jit(solution)/shard_map/ppermute | solution.py:407
  224.2 35.1 %collective-permute-start.11 = (f32[2,2,256,128]{3,2,1,0:T(8,128)}, f32[2,2,256,128]{3,2,1,0:T(8,128)}, u32[]{:S(2)}, u32[]{:S(2)}) collective-permute-start(f32[2,2,256,128]{3,2,1,0:T(8,128)} %get-tuple-element.57), channel_id=1, source_target_pairs={{0,3},{1,2},{2,1},{3,0},{4,7},{5,6},{6,5},{7,4},{8,11},{9,10},{10,... | collective-permute-start | bytes 1572872 | tf_op jit(solution)/shard_map/ppermute | solution.py:407
  241.1 30.3 %all-to-all-start.5 = ((f32[32,1,2,4,8,128]{5,4,3,2,1,0:T(8,128)}), f32[32,1,2,4,8,128]{5,4,3,2,1,0:T(8,128)S(1)}, u32[]{:S(2)}, u32[]{:S(2)}) async-start(f32[32,1,2,4,8,128]{5,4,3,2,1,0:T(8,128)} %get-tuple-element.58), calls=%async_computation.5 | async-start | bytes 2097152 | tf_op jit(solution)/shard_map/all_to_all | solution.py:984
  243.8 1.2 copy-start.13
  245.0 0.9 copy-start.16
  259.2 20.9 %copy-start.6 = (f32[2,2,256,128]{3,2,1,0:T(8,128)S(1)}, f32[2,2,256,128]{3,2,1,0:T(8,128)}, u32[]{:S(2)}) copy-start(f32[2,2,256,128]{3,2,1,0:T(8,128)} %copy-done.5) | copy-start | bytes 1572868
  259.2 17.3 %collective-permute-start.12 = (f32[1,2,256,128]{3,2,1,0:T(8,128)}, f32[1,2,256,128]{3,2,1,0:T(8,128)S(1)}, u32[]{:S(2)}, u32[]{:S(2)}) collective-permute-start(f32[1,2,256,128]{3,2,1,0:T(8,128)} %get-tuple-element.68), channel_id=1, source_target_pairs={{0,1},{1,0},{2,3},{3,2},{4,5},{5,4},{6,7},{7,6},{8,9},{9,8},{10,11... | collective-permute-start | bytes 786440 | tf_op jit(solution)/shard_map/ppermute | solution.py:407
  260.8 15.7 %collective-permute-start.13 = (f32[1,2,256,128]{3,2,1,0:T(8,128)}, f32[1,2,256,128]{3,2,1,0:T(8,128)S(1)}, u32[]{:S(2)}, u32[]{:S(2)}) collective-permute-start(f32[1,2,256,128]{3,2,1,0:T(8,128)} %get-tuple-element.69), channel_id=1, source_target_pairs={{0,2},{1,3},{2,0},{3,1},{4,6},{5,7},{6,4},{7,5},{8,10},{9,11},{10,... | collective-permute-start | bytes 786440 | tf_op jit(solution)/shard_map/ppermute | solution.py:407
  261.3 15.2 %collective-permute-start.14 = (f32[1,2,256,128]{3,2,1,0:T(8,128)}, f32[1,2,256,128]{3,2,1,0:T(8,128)}, u32[]{:S(2)}, u32[]{:S(2)}) collective-permute-start(f32[1,2,256,128]{3,2,1,0:T(8,128)} %get-tuple-element.70), channel_id=1, source_target_pairs={{0,3},{1,2},{2,1},{3,0},{4,7},{5,6},{6,5},{7,4},{8,11},{9,10},{10,... | collective-permute-start | bytes 786440 | tf_op jit(solution)/shard_map/ppermute | solution.py:407
  271.4 1.2 copy-start.14
  272.7 0.9 copy-start.17
  276.6 9.3 %collective-permute-start.15 = (f32[1,2,256,128]{3,2,1,0:T(8,128)S(1)}, f32[1,2,256,128]{3,2,1,0:T(8,128)S(1)}, u32[]{:S(2)}, u32[]{:S(2)}) collective-permute-start(f32[1,2,256,128]{3,2,1,0:T(8,128)S(1)} %get-tuple-element.72), channel_id=1, source_target_pairs={{0,1},{1,0},{2,3},{3,2},{4,5},{5,4},{6,7},{7,6},{8,9},{9,8},{10,11... | collective-permute-start | bytes 786440 | tf_op jit(solution)/shard_map/ppermute | solution.py:407
  278.1 13.5 %collective-permute-start.16 = (f32[1,2,256,128]{3,2,1,0:T(8,128)S(1)}, f32[1,2,256,128]{3,2,1,0:T(8,128)S(1)}, u32[]{:S(2)}, u32[]{:S(2)}) collective-permute-start(f32[1,2,256,128]{3,2,1,0:T(8,128)S(1)} %get-tuple-element.73), channel_id=1, source_target_pairs={{0,2},{1,3},{2,0},{3,1},{4,6},{5,7},{6,4},{7,5},{8,10},{9,11},{10,... | collective-permute-start | bytes 786440 | tf_op jit(solution)/shard_map/ppermute | solution.py:407
  278.7 13.0 %collective-permute-start.17 = (f32[1,2,256,128]{3,2,1,0:T(8,128)S(1)}, f32[1,2,256,128]{3,2,1,0:T(8,128)S(1)}, u32[]{:S(2)}, u32[]{:S(2)}) collective-permute-start(f32[1,2,256,128]{3,2,1,0:T(8,128)S(1)} %get-tuple-element.74), channel_id=1, source_target_pairs={{0,3},{1,2},{2,1},{3,0},{4,7},{5,6},{6,5},{7,4},{8,11},{9,10},{10,... | collective-permute-start | bytes 786440 | tf_op jit(solution)/shard_map/ppermute | solution.py:407

commit v6 on v5

--- a/solution.py
+++ b/solution.py
@@ -830,7 +830,7 @@
             held[where_to, :, :LANES], held[where_to, :, LANES:] = c_mul(values[e], twiddle)
         return carry
 
-    lax.fori_loop(0, inner, before, 0, unroll=8)
+    lax.fori_loop(0, inner, before, 0, unroll=16)
 
     group = 256 // rows
 
@@ -857,7 +857,7 @@
             x[q, mode, 0], x[q, mode, 1] = values[q]
         return carry
 
-    lax.fori_loop(0, inner, after_, 0, unroll=8)
+    lax.fori_loop(0, inner, after_, 0, unroll=16)
 
     for q in range(GROUPS):
         c, index = where[q]
@@ -977,7 +977,7 @@
     source = density.reshape(2, GROUPS, rows, x_local)
 
     def send(pieces):
-        moved = {k: swap(pieces[k], "narrow", k) for k in (3, 1, 2)}
+        moved = {k: swap(pieces[k], "narrow", k) for k in (1, 2, 3)}
         return [pieces[0], moved[1], moved[2], moved[3]]
 
     def trade_all(blocks):

time: 297 us -> 297 us (level)
  no operation moved by 1% of the time
where the time goes in v6:
time: 297 us; the launch traced here: 296 us
  waiting for transfers between devices  121 us (41%)
  Pallas kernels  59 us (20%)
  blocking collectives  53.5 us (18%)
  starting transfers between devices  40.1 us (14%)
  local copies, waits for them, and re-layouts  18.9 us (6%)
    all_to_all x5, waiting for transfers between devices, trade_all(): return lax.all_to_all(blocks, ('narrow', 'wide'), 0, 0, tiled=True)  89.2 us
    all_to_all x1, blocking collectives, trade_all(): return lax.all_to_all(blocks, ('narrow', 'wide'), 0, 0, tiled=True)  53.5 us
    ppermute x18, waiting for transfers between devices, swap(): return lax.ppermute(value, axis, pairs)  31.8 us
    ppermute x18, starting transfers between devices, swap(): return lax.ppermute(value, axis, pairs)  22.2 us
    all_to_all x5, starting transfers between devices, trade_all(): return lax.all_to_all(blocks, ('narrow', 'wide'), 0, 0, tiled=True)  17.8 us
    unnamed x54, local copies, waits for them, and re-layouts  16.8 us
    pallas_call x3, Pallas kernels, lines_inverse(): pl.pallas_call(functools.partial(lines_inverse_kernel, rows), grid=(count...  13.3 us
    pallas_call x3, Pallas kernels, lines_forward(): pl.pallas_call(functools.partial(lines_forward_kernel, rows), grid=(count...  12.8 us
  transfers between devices with their start and end apart: 23, of which 11 were waited for; matrix products, arithmetic and copies ran while one was open for 1% of the time, Pallas kernels for 14%

profile of v6, /device:TPU:0, one launch (start us, length us, event | category | flops | bytes accessed | tf_op | source)
XLA Modules:
  0.0 295.7 jit_solution(2642234916224981235)
XLA Ops:
  0.0 2.2 copy-done
  2.2 0.5 cut.13
  2.7 3.0 %collective-permute-start = (f32[1,2,256,128]{3,2,1,0:T(8,128)S(1)}, f32[1,2,256,128]{3,2,1,0:T(8,128)}, u32[]{:S(2)}, u32[]{:S(2)}) collective-permute-start(f32[1,2,256,128]{3,2,1,0:T(8,128)S(1)} %cut.13), channel_id=1, source_target_pairs={{0,1},{1,0},{2,3},{3,2},{4,5},{5,4},{6,7},{7,6},{8,9},{9,8},{10,11... | collective-permute-start | bytes 786440 | tf_op jit(solution)/shard_map/ppermute | solution.py:407
  5.7 0.5 cut.14
  6.3 1.6 collective-permute-start.1
  8.7 1.3 dynamic-slice_bitcast_fusion.1.refs_0_
  10.0 0.7 fusion.2.slot_ref
  10.7 2.2 copy-done.1
  13.4 1.2 cut.19
  14.6 1.2 cut.18
  15.8 1.2 cut.17
  18.0 0.7 copy-done.22
  18.8 1.0 collective-permute-done.1.refs_6_
  19.9 1.0 collective-permute-start.3
  20.9 1.5 collective-permute-start.4
  22.4 1.0 collective-permute-start.5
  23.4 3.3 %lines_forward.3 = f32[32,1,2,4,8,128]{5,4,3,2,1,0:T(8,128)S(1)} custom-call(s32[4]{0:T(128)S(1)} %fusion.2.slot_ref, f32[4,2,256,128]{3,2,1,0:T(8,128)S(1)} %dynamic-slice_bitcast_fusion.1.refs_0_, bf16[256,256]{1,0:T(8,128)(2,1)S(1)} %dynamic-slice_bitcast_fusion.3.refs_1_, bf16[2,512,512]{2,1,0:T(8,128)(2,1)S(1)} %dynamic-slice_bitcast_fusion.refs_2_, ...), custom_call_target="tpu_custom_call" | custom-call | flops 25165824000 | bytes 2097152 | tf_op jit(solution)/shard_map/lines_forward/pallas_call | solution.py:717
  26.7 1.0 copy-done.3
  27.6 5.3 %all-to-all-start = ((f32[32,1,2,4,8,128]{5,4,3,2,1,0:T(8,128)}), f32[32,1,2,4,8,128]{5,4,3,2,1,0:T(8,128)S(1)}, u32[]{:S(2)}, u32[]{:S(2)}) async-start(f32[32,1,2,4,8,128]{5,4,3,2,1,0:T(8,128)} %copy-done.3), calls=%async_computation | async-start | bytes 2097152 | tf_op jit(solution)/shard_map/all_to_all | solution.py:984
  33.0 2.2 copy-done.2
  35.2 1.5 cut.23
  36.7 1.5 cut.22
  38.2 1.5 cut.21
  39.7 0.8 cut.20.refs_4_
  40.5 0.8 copy-done.7
  41.3 1.8 collective-permute-start.6
  43.1 1.5 collective-permute-start.7
  44.9 3.3 %lines_forward.4 = f32[32,1,2,4,8,128]{5,4,3,2,1,0:T(8,128)S(1)} custom-call(s32[4]{0:T(128)S(1)} %fusion.2.slot_ref, f32[4,2,256,128]{3,2,1,0:T(8,128)S(1)} %dynamic-slice_bitcast_fusion.1.refs_0_, bf16[256,256]{1,0:T(8,128)(2,1)S(1)} %dynamic-slice_bitcast_fusion.3.refs_1_, bf16[2,512,512]{2,1,0:T(8,128)(2,1)S(1)} %dynamic-slice_bitcast_fusion.refs_2_, ...), custom_call_target="tpu_custom_call" | custom-call | flops 25165824000 | bytes 2097152 | tf_op jit(solution)/shard_map/lines_forward/pallas_call | solution.py:717
  48.2 1.0 copy-done.4
  49.2 11.4 %all-to-all-done.refs_0_ = f32[32,1,2,4,8,128]{5,4,3,2,1,0:T(8,128)S(1)} async-done(((f32[32,1,2,4,8,128]{5,4,3,2,1,0:T(8,128)}), f32[32,1,2,4,8,128]{5,4,3,2,1,0:T(8,128)S(1)}, u32[]{:S(2)}, u32[]{:S(2)}) %all-to-all-start) | async-done | bytes 1048608 | tf_op jit(solution)/shard_map/all_to_all | solution.py:984
  60.6 3.4 %all-to-all-start.1 = ((f32[32,1,2,4,8,128]{5,4,3,2,1,0:T(8,128)}), f32[32,1,2,4,8,128]{5,4,3,2,1,0:T(8,128)}, u32[]{:S(2)}, u32[]{:S(2)}) async-start(f32[32,1,2,4,8,128]{5,4,3,2,1,0:T(8,128)} %copy-done.4), calls=%async_computation.1 | async-start | bytes 2097152 | tf_op jit(solution)/shard_map/all_to_all | solution.py:984
  64.0 15.0 %collective-permute-done.8.refs_7_ = f32[2,2,256,128]{3,2,1,0:T(8,128)} collective-permute-done((f32[2,2,256,128]{3,2,1,0:T(8,128)}, f32[2,2,256,128]{3,2,1,0:T(8,128)}, u32[]{:S(2)}, u32[]{:S(2)}) %collective-permute-start.8) | collective-permute-done | bytes 524320 | tf_op jit(solution)/shard_map/ppermute | solution.py:407
  79.0 1.0 copy-done.8
  80.0 6.2 %lines_forward.5 = f32[32,2,2,4,8,128]{5,4,3,2,1,0:T(8,128)} custom-call(s32[4]{0:T(128)S(1)} %fusion.2.slot_ref, f32[4,2,256,128]{3,2,1,0:T(8,128)S(1)} %dynamic-slice_bitcast_fusion.1.refs_0_, bf16[256,256]{1,0:T(8,128)(2,1)S(1)} %dynamic-slice_bitcast_fusion.3.refs_1_, bf16[2,512,512]{2,1,0:T(8,128)(2,1)S(1)} %dynamic-slice_bitcast_fusion.refs_2_, ...), custom_call_target="tpu_custom_call" | custom-call | flops 50331648000 | bytes 4194304 | tf_op jit(solution)/shard_map/lines_forward/pallas_call | solution.py:717
  86.3 5.3 %all-to-all-done.1.refs_1_ = f32[32,1,2,4,8,128]{5,4,3,2,1,0:T(8,128)} async-done(((f32[32,1,2,4,8,128]{5,4,3,2,1,0:T(8,128)}), f32[32,1,2,4,8,128]{5,4,3,2,1,0:T(8,128)}, u32[]{:S(2)}, u32[]{:S(2)}) %all-to-all-start.1) | async-done | bytes 1048608 | tf_op jit(solution)/shard_map/all_to_all | solution.py:984
  91.6 3.5 %all-to-all-start.2 = ((f32[32,2,2,4,8,128]{5,4,3,2,1,0:T(8,128)}), f32[32,2,2,4,8,128]{5,4,3,2,1,0:T(8,128)}, u32[]{:S(2)}, u32[]{:S(2)}) async-start(f32[32,2,2,4,8,128]{5,4,3,2,1,0:T(8,128)} %lines_forward.5), calls=%async_computation.2 | async-start | bytes 4194304 | tf_op jit(solution)/shard_map/all_to_all | solution.py:984
  95.8 2.0 add_multiply_fusion.green_ref
  97.8 47.3 %all-to-all-done.2.refs_2_ = f32[32,2,2,4,8,128]{5,4,3,2,1,0:T(8,128)} async-done(((f32[32,2,2,4,8,128]{5,4,3,2,1,0:T(8,128)}), f32[32,2,2,4,8,128]{5,4,3,2,1,0:T(8,128)}, u32[]{:S(2)}, u32[]{:S(2)}) %all-to-all-start.2) | async-done | bytes 2097184 | tf_op jit(solution)/shard_map/all_to_all | solution.py:984
  145.1 12.0 %row_filter.1 = (f32[32,1,2,4,8,128]{5,4,3,2,1,0:T(8,128)}, f32[32,1,2,4,8,128]{5,4,3,2,1,0:T(8,128)}, f32[32,2,2,4,8,128]{5,4,3,2,1,0:T(8,128)}) custom-call(bf16[2,256,256]{2,1,0:T(8,128)(2,1)S(1)} %copy-done.19, bf16[2,256,256]{2,1,0:T(8,128)(2,1)S(1)} %copy-done.18, f32[2,128,128]{2,1,0:T(8,128)S(1)} %copy-done.21, ...), custom_call_target="tpu_custom_call" | custom-call | flops 6442450944 | bytes 10485760 | tf_op jit(solution)/shard_map/row_filter/pallas_call | solution.py:895
  157.1 53.5 %all_to_all.30.refs_4_ = f32[32,2,2,4,8,128]{5,4,3,2,1,0:T(8,128)} all-to-all(f32[32,2,2,4,8,128]{5,4,3,2,1,0:T(8,128)} %get-tuple-element.51), channel_id=1, replica_groups=mesh['wide'=8,'narrow'=4] {'narrow','wide'}, dimensions={0} | all-to-all | bytes 4194304 | tf_op jit(solution)/shard_map/all_to_all | solution.py:984
  210.7 3.0 all-to-all-start.4
  213.7 6.6 %lines_inverse.3 = (f32[2,2,256,128]{3,2,1,0:T(8,128)S(1)}, f32[2,2,256,128]{3,2,1,0:T(8,128)}, f32[2,2,256,128]{3,2,1,0:T(8,128)}, f32[2,2,256,128]{3,2,1,0:T(8,128)}) custom-call(s32[4]{0:T(128)S(1)} %fusion.2.slot_ref, f32[4,2,256,128]{3,2,1,0:T(8,128)S(1)} %dynamic-slice_bitcast_fusion.1.refs_0_, bf16[256,256]{1,0:T(8,128)(2,1)S(1)} %copy-done.20, ...), custom_call_target="tpu_custom_call" | custom-call | flops 50331648000 | bytes 4194304 | tf_op jit(solution)/shard_map/lines_inverse/pallas_call | solution.py:781
  220.3 0.8 copy-done.5
  221.1 1.5 collective-permute-start.9
  222.6 1.5 collective-permute-start.10
  224.6 16.5 %all-to-all-done.4.refs_4_ = f32[32,1,2,4,8,128]{5,4,3,2,1,0:T(8,128)S(1)} async-done(((f32[32,1,2,4,8,128]{5,4,3,2,1,0:T(8,128)}), f32[32,1,2,4,8,128]{5,4,3,2,1,0:T(8,128)S(1)}, u32[]{:S(2)}, u32[]{:S(2)}) %all-to-all-start.4) | async-done | bytes 1048608 | tf_op jit(solution)/shard_map/all_to_all | solution.py:984
  241.0 2.6 all-to-all-start.5
  243.7 1.2 copy-done.13
  244.9 0.9 copy-done.16
  245.9 3.8 %lines_inverse.5 = (f32[1,2,256,128]{3,2,1,0:T(8,128)S(1)}, f32[1,2,256,128]{3,2,1,0:T(8,128)}, f32[1,2,256,128]{3,2,1,0:T(8,128)}, f32[1,2,256,128]{3,2,1,0:T(8,128)}) custom-call(s32[4]{0:T(128)S(1)} %fusion.2.slot_ref, f32[4,2,256,128]{3,2,1,0:T(8,128)S(1)} %dynamic-slice_bitcast_fusion.1.refs_0_, bf16[256,256]{1,0:T(8,128)(2,1)S(1)} %copy-done.20, ...), custom_call_target="tpu_custom_call" | custom-call | flops 25165824000 | bytes 2097152 | tf_op jit(solution)/shard_map/lines_inverse/pallas_call | solution.py:781
  249.7 1.6 collective-permute-done.10.refs_6_
  251.3 7.9 %collective-permute-done.11.refs_7_ = f32[2,2,256,128]{3,2,1,0:T(8,128)} collective-permute-done((f32[2,2,256,128]{3,2,1,0:T(8,128)}, f32[2,2,256,128]{3,2,1,0:T(8,128)}, u32[]{:S(2)}, u32[]{:S(2)}) %collective-permute-start.11) | collective-permute-done | bytes 524320 | tf_op jit(solution)/shard_map/ppermute | solution.py:407
  259.1 1.6 collective-permute-start.12
  261.2 1.4 collective-permute-start.14
  262.6 8.7 %all-to-all-done.5.refs_4_ = f32[32,1,2,4,8,128]{5,4,3,2,1,0:T(8,128)S(1)} async-done(((f32[32,1,2,4,8,128]{5,4,3,2,1,0:T(8,128)}), f32[32,1,2,4,8,128]{5,4,3,2,1,0:T(8,128)S(1)}, u32[]{:S(2)}, u32[]{:S(2)}) %all-to-all-start.5) | async-done | bytes 1048608 | tf_op jit(solution)/shard_map/all_to_all | solution.py:984
  271.3 1.2 copy-done.14
  272.6 0.9 copy-done.17
  273.5 2.9 lines_inverse.4
  276.5 1.6 collective-permute-start.15
  278.6 1.5 collective-permute-start.17
  280.0 5.1 %place.1.refs_4_ = f32[2,4,256,512]{3,2,1,0:T(8,128)} custom-call(f32[1,2,256,128]{3,2,1,0:T(8,128)S(1)} %get-tuple-element.67.refs_0_, f32[1,2,256,128]{3,2,1,0:T(8,128)S(1)} %collective-permute-done.12.refs_1_, f32[1,2,256,128]{3,2,1,0:T(8,128)S(1)} %collective-permute-done.13.refs_2_, f32[1,2,256,128]{3,2,1,0:T(8,128)} %collective-permute-done.14.refs_3_, ...), custom_call_target="tpu_custom_call" | custom-call | flops 2097152 | bytes 4194304 | tf_op jit(solution)/shard_map/place/pallas_call | solution.py:598
  285.2 0.6 collective-permute-done.15.refs_1_
  285.7 5.8 %collective-permute-done.16.refs_2_ = f32[1,2,256,128]{3,2,1,0:T(8,128)S(1)} collective-permute-done((f32[1,2,256,128]{3,2,1,0:T(8,128)S(1)}, f32[1,2,256,128]{3,2,1,0:T(8,128)S(1)}, u32[]{:S(2)}, u32[]{:S(2)}) %collective-permute-start.16) | collective-permute-done | bytes 262176 | tf_op jit(solution)/shard_map/ppermute | solution.py:407
  291.5 4.2 %add.82 = f32[2,4,256,512]{3,2,1,0:T(8,128)} custom-call(f32[1,2,256,128]{3,2,1,0:T(8,128)S(1)} %get-tuple-element.71.refs_0_, f32[1,2,256,128]{3,2,1,0:T(8,128)S(1)} %collective-permute-done.15.refs_1_, f32[1,2,256,128]{3,2,1,0:T(8,128)S(1)} %collective-permute-done.16.refs_2_, ...), custom_call_target="tpu_custom_call", output_to_operand_aliasing={{}: (4, {})} | custom-call | flops 2097152 | bytes 4194304 | tf_op jit(solution)/shard_map/add/pallas_call | solution.py:616
  (66 shorter events, 4.3 us)
Async XLA Ops:
  0.0 2.2 copy-start
  2.7 16.1 %collective-permute-start = (f32[1,2,256,128]{3,2,1,0:T(8,128)S(1)}, f32[1,2,256,128]{3,2,1,0:T(8,128)}, u32[]{:S(2)}, u32[]{:S(2)}) collective-permute-start(f32[1,2,256,128]{3,2,1,0:T(8,128)S(1)} %cut.13), channel_id=1, source_target_pairs={{0,1},{1,0},{2,3},{3,2},{4,5},{5,4},{6,7},{7,6},{8,9},{9,8},{10,11... | collective-permute-start | bytes 786440 | tf_op jit(solution)/shard_map/ppermute | solution.py:407
  6.3 2.4 copy-start.25
  6.3 13.6 %collective-permute-start.1 = (f32[1,2,256,128]{3,2,1,0:T(8,128)S(1)}, f32[1,2,256,128]{3,2,1,0:T(8,128)}, u32[]{:S(2)}, u32[]{:S(2)}) collective-permute-start(f32[1,2,256,128]{3,2,1,0:T(8,128)S(1)} %cut.14), channel_id=1, source_target_pairs={{0,2},{1,3},{2,0},{3,1},{4,6},{5,7},{6,4},{7,5},{8,10},{9,11},{10,... | collective-permute-start | bytes 786440 | tf_op jit(solution)/shard_map/ppermute | solution.py:407
  8.4 11.4 %collective-permute-start.2 = (f32[1,2,256,128]{3,2,1,0:T(8,128)S(1)}, f32[1,2,256,128]{3,2,1,0:T(8,128)}, u32[]{:S(2)}, u32[]{:S(2)}) collective-permute-start(f32[1,2,256,128]{3,2,1,0:T(8,128)S(1)} %cut.15), channel_id=1, source_target_pairs={{0,3},{1,2},{2,1},{3,0},{4,7},{5,6},{6,5},{7,4},{8,11},{9,10},{10,... | collective-permute-start | bytes 786440 | tf_op jit(solution)/shard_map/ppermute | solution.py:407
  10.7 2.2 copy-start.1
  17.0 1.0 copy-start.23
  17.0 1.8 copy-start.22
  18.7 4.6 %copy-start.9 = (f32[2,256,128]{2,1,0:T(8,128)}, f32[2,256,128]{2,1,0:T(8,128)S(1)}, u32[]{:S(2)}) copy-start(f32[2,256,128]{2,1,0:T(8,128)S(1)} %dynamic-slice_bitcast_fusion.2.refs_3_) | copy-start | bytes 786436
  19.9 21.4 %collective-permute-start.3 = (f32[1,2,256,128]{3,2,1,0:T(8,128)}, f32[1,2,256,128]{3,2,1,0:T(8,128)}, u32[]{:S(2)}, u32[]{:S(2)}) collective-permute-start(f32[1,2,256,128]{3,2,1,0:T(8,128)} %cut.17), channel_id=1, source_target_pairs={{0,1},{1,0},{2,3},{3,2},{4,5},{5,4},{6,7},{7,6},{8,9},{9,8},{10,11... | collective-permute-start | bytes 786440 | tf_op jit(solution)/shard_map/ppermute | solution.py:407
  20.9 20.4 %collective-permute-start.4 = (f32[1,2,256,128]{3,2,1,0:T(8,128)}, f32[1,2,256,128]{3,2,1,0:T(8,128)}, u32[]{:S(2)}, u32[]{:S(2)}) collective-permute-start(f32[1,2,256,128]{3,2,1,0:T(8,128)} %cut.18), channel_id=1, source_target_pairs={{0,2},{1,3},{2,0},{3,1},{4,6},{5,7},{6,4},{7,5},{8,10},{9,11},{10,... | collective-permute-start | bytes 786440 | tf_op jit(solution)/shard_map/ppermute | solution.py:407
  22.4 18.9 %collective-permute-start.5 = (f32[1,2,256,128]{3,2,1,0:T(8,128)}, f32[1,2,256,128]{3,2,1,0:T(8,128)}, u32[]{:S(2)}, u32[]{:S(2)}) collective-permute-start(f32[1,2,256,128]{3,2,1,0:T(8,128)} %cut.19), channel_id=1, source_target_pairs={{0,3},{1,2},{2,1},{3,0},{4,7},{5,6},{6,5},{7,4},{8,11},{9,10},{10,... | collective-permute-start | bytes 786440 | tf_op jit(solution)/shard_map/ppermute | solution.py:407
  26.7 1.0 copy-start.3
  27.6 32.9 %all-to-all-start = ((f32[32,1,2,4,8,128]{5,4,3,2,1,0:T(8,128)}), f32[32,1,2,4,8,128]{5,4,3,2,1,0:T(8,128)S(1)}, u32[]{:S(2)}, u32[]{:S(2)}) async-start(f32[32,1,2,4,8,128]{5,4,3,2,1,0:T(8,128)} %copy-done.3), calls=%async_computation | async-start | bytes 2097152 | tf_op jit(solution)/shard_map/all_to_all | solution.py:984
  33.0 2.2 copy-start.2
  39.7 5.2 %copy-start.10 = (f32[2,256,128]{2,1,0:T(8,128)S(1)}, f32[2,256,128]{2,1,0:T(8,128)}, u32[]{:S(2)}) copy-start(f32[2,256,128]{2,1,0:T(8,128)} %copy-done.9) | copy-start | bytes 786436
  40.5 0.8 copy-start.7
  41.3 22.7 %collective-permute-start.6 = (f32[2,2,256,128]{3,2,1,0:T(8,128)}, f32[2,2,256,128]{3,2,1,0:T(8,128)}, u32[]{:S(2)}, u32[]{:S(2)}) collective-permute-start(f32[2,2,256,128]{3,2,1,0:T(8,128)} %cut.21), channel_id=1, source_target_pairs={{0,1},{1,0},{2,3},{3,2},{4,5},{5,4},{6,7},{7,6},{8,9},{9,8},{10,11... | collective-permute-start | bytes 1572872 | tf_op jit(solution)/shard_map/ppermute | solution.py:407
  43.1 20.9 %collective-permute-start.7 = (f32[2,2,256,128]{3,2,1,0:T(8,128)}, f32[2,2,256,128]{3,2,1,0:T(8,128)}, u32[]{:S(2)}, u32[]{:S(2)}) collective-permute-start(f32[2,2,256,128]{3,2,1,0:T(8,128)} %cut.22), channel_id=1, source_target_pairs={{0,2},{1,3},{2,0},{3,1},{4,6},{5,7},{6,4},{7,5},{8,10},{9,11},{10,... | collective-permute-start | bytes 1572872 | tf_op jit(solution)/shard_map/ppermute | solution.py:407
  44.6 34.4 %collective-permute-start.8 = (f32[2,2,256,128]{3,2,1,0:T(8,128)}, f32[2,2,256,128]{3,2,1,0:T(8,128)}, u32[]{:S(2)}, u32[]{:S(2)}) collective-permute-start(f32[2,2,256,128]{3,2,1,0:T(8,128)} %cut.23), channel_id=1, source_target_pairs={{0,3},{1,2},{2,1},{3,0},{4,7},{5,6},{6,5},{7,4},{8,11},{9,10},{10,... | collective-permute-start | bytes 1572872 | tf_op jit(solution)/shard_map/ppermute | solution.py:407
  48.2 1.0 copy-start.4
  49.2 29.8 %copy-start.11 = (f32[2,256,128]{2,1,0:T(8,128)S(1)}, f32[2,256,128]{2,1,0:T(8,128)}, u32[]{:S(2)}) copy-start(f32[2,256,128]{2,1,0:T(8,128)} %copy-done.9) | copy-start | bytes 786436
  60.6 31.0 %all-to-all-start.1 = ((f32[32,1,2,4,8,128]{5,4,3,2,1,0:T(8,128)}), f32[32,1,2,4,8,128]{5,4,3,2,1,0:T(8,128)}, u32[]{:S(2)}, u32[]{:S(2)}) async-start(f32[32,1,2,4,8,128]{5,4,3,2,1,0:T(8,128)} %copy-done.4), calls=%async_computation.1 | async-start | bytes 2097152 | tf_op jit(solution)/shard_map/all_to_all | solution.py:984
  79.0 1.0 copy-start.8
  86.2 9.6 %copy-start.26 = (s32[32,128]{1,0:T(8,128)S(1)}, s32[32,128]{1,0:T(8,128)}, u32[]{:S(2)}) copy-start(s32[32,128]{1,0:T(8,128)} %constant.85.clone) | copy-start | bytes 49156
  86.2 9.6 %copy-start.24 = (s32[128,128]{1,0:T(8,128)S(1)}, s32[128,128]{1,0:T(8,128)}, u32[]{:S(2)}) copy-start(s32[128,128]{1,0:T(8,128)} %constant.90) | copy-start | bytes 196612
  91.6 53.6 %all-to-all-start.2 = ((f32[32,2,2,4,8,128]{5,4,3,2,1,0:T(8,128)}), f32[32,2,2,4,8,128]{5,4,3,2,1,0:T(8,128)}, u32[]{:S(2)}, u32[]{:S(2)}) async-start(f32[32,2,2,4,8,128]{5,4,3,2,1,0:T(8,128)} %lines_forward.5), calls=%async_computation.2 | async-start | bytes 4194304 | tf_op jit(solution)/shard_map/all_to_all | solution.py:984
  95.1 50.1 %copy-start.18 = (bf16[2,256,256]{2,1,0:T(8,128)(2,1)S(1)}, bf16[2,256,256]{2,1,0:T(8,128)(2,1)}, u32[]{:S(2)}) copy-start(bf16[2,256,256]{2,1,0:T(8,128)(2,1)} %constant.88.clone.inverse_ref) | copy-start | bytes 786436
  95.1 50.1 %copy-start.19 = (bf16[2,256,256]{2,1,0:T(8,128)(2,1)S(1)}, bf16[2,256,256]{2,1,0:T(8,128)(2,1)}, u32[]{:S(2)}) copy-start(bf16[2,256,256]{2,1,0:T(8,128)(2,1)} %constant.87.clone.forward_ref) | copy-start | bytes 786436
  95.1 50.1 %copy-start.21 = (f32[2,128,128]{2,1,0:T(8,128)S(1)}, f32[2,128,128]{2,1,0:T(8,128)}, u32[]{:S(2)}) copy-start(f32[2,128,128]{2,1,0:T(8,128)} %constant.84.clone.turn_ref) | copy-start | bytes 393220
  210.7 3.0 %copy-start.12 = (bf16[2,512,512]{2,1,0:T(8,128)(2,1)S(1)}, bf16[2,512,512]{2,1,0:T(8,128)(2,1)}, u32[]{:S(2)}) copy-start(bf16[2,512,512]{2,1,0:T(8,128)(2,1)} %constant.82.clone.refs_2_) | copy-start | bytes 3145732
  210.7 3.0 %copy-start.15 = (f32[2,256,128]{2,1,0:T(8,128)S(1)}, f32[2,256,128]{2,1,0:T(8,128)}, u32[]{:S(2)}) copy-start(f32[2,256,128]{2,1,0:T(8,128)} %constant.83.clone.refs_3_) | copy-start | bytes 786436
  210.7 3.0 %copy-start.20 = (bf16[256,256]{1,0:T(8,128)(2,1)S(1)}, bf16[256,256]{1,0:T(8,128)(2,1)}, u32[]{:S(2)}) copy-start(bf16[256,256]{1,0:T(8,128)(2,1)} %constant.81.clone.refs_1_) | copy-start | bytes 393220
  210.7 30.4 %all-to-all-start.4 = ((f32[32,1,2,4,8,128]{5,4,3,2,1,0:T(8,128)}), f32[32,1,2,4,8,128]{5,4,3,2,1,0:T(8,128)S(1)}, u32[]{:S(2)}, u32[]{:S(2)}) async-start(f32[32,1,2,4,8,128]{5,4,3,2,1,0:T(8,128)} %get-tuple-element.52), calls=%async_computation.4 | async-start | bytes 2097152 | tf_op jit(solution)/shard_map/all_to_all | solution.py:984
  220.3 0.8 copy-start.5
  221.1 28.6 %collective-permute-start.9 = (f32[2,2,256,128]{3,2,1,0:T(8,128)}, f32[2,2,256,128]{3,2,1,0:T(8,128)}, u32[]{:S(2)}, u32[]{:S(2)}) collective-permute-start(f32[2,2,256,128]{3,2,1,0:T(8,128)} %get-tuple-element.55), channel_id=1, source_target_pairs={{0,1},{1,0},{2,3},{3,2},{4,5},{5,4},{6,7},{7,6},{8,9},{9,8},{10,11... | collective-permute-start | bytes 1572872 | tf_op jit(solution)/shard_map/ppermute | solution.py:407
  222.6 28.7 %collective-permute-start.10 = (f32[2,2,256,128]{3,2,1,0:T(8,128)}, f32[2,2,256,128]{3,2,1,0:T(8,128)}, u32[]{:S(2)}, u32[]{:S(2)}) collective-permute-start(f32[2,2,256,128]{3,2,1,0:T(8,128)} %get-tuple-element.56), channel_id=1, source_target_pairs={{0,2},{1,3},{2,0},{3,1},{4,6},{5,7},{6,4},{7,5},{8,10},{9,11},{10,... | collective-permute-start | bytes 1572872 | tf_op jit(solution)/shard_map/ppermute | solution.py:407
  224.1 35.1 %collective-permute-start.11 = (f32[2,2,256,128]{3,2,1,0:T(8,128)}, f32[2,2,256,128]{3,2,1,0:T(8,128)}, u32[]{:S(2)}, u32[]{:S(2)}) collective-permute-start(f32[2,2,256,128]{3,2,1,0:T(8,128)} %get-tuple-element.57), channel_id=1, source_target_pairs={{0,3},{1,2},{2,1},{3,0},{4,7},{5,6},{6,5},{7,4},{8,11},{9,10},{10,... | collective-permute-start | bytes 1572872 | tf_op jit(solution)/shard_map/ppermute | solution.py:407
  241.0 30.3 %all-to-all-start.5 = ((f32[32,1,2,4,8,128]{5,4,3,2,1,0:T(8,128)}), f32[32,1,2,4,8,128]{5,4,3,2,1,0:T(8,128)S(1)}, u32[]{:S(2)}, u32[]{:S(2)}) async-start(f32[32,1,2,4,8,128]{5,4,3,2,1,0:T(8,128)} %get-tuple-element.58), calls=%async_computation.5 | async-start | bytes 2097152 | tf_op jit(solution)/shard_map/all_to_all | solution.py:984
  243.7 1.2 copy-start.13
  244.9 0.9 copy-start.16
  259.1 20.9 %copy-start.6 = (f32[2,2,256,128]{3,2,1,0:T(8,128)S(1)}, f32[2,2,256,128]{3,2,1,0:T(8,128)}, u32[]{:S(2)}) copy-start(f32[2,2,256,128]{3,2,1,0:T(8,128)} %copy-done.5) | copy-start | bytes 1572868
  259.1 17.3 %collective-permute-start.12 = (f32[1,2,256,128]{3,2,1,0:T(8,128)}, f32[1,2,256,128]{3,2,1,0:T(8,128)S(1)}, u32[]{:S(2)}, u32[]{:S(2)}) collective-permute-start(f32[1,2,256,128]{3,2,1,0:T(8,128)} %get-tuple-element.68), channel_id=1, source_target_pairs={{0,1},{1,0},{2,3},{3,2},{4,5},{5,4},{6,7},{7,6},{8,9},{9,8},{10,11... | collective-permute-start | bytes 786440 | tf_op jit(solution)/shard_map/ppermute | solution.py:407
  260.7 15.7 %collective-permute-start.13 = (f32[1,2,256,128]{3,2,1,0:T(8,128)}, f32[1,2,256,128]{3,2,1,0:T(8,128)S(1)}, u32[]{:S(2)}, u32[]{:S(2)}) collective-permute-start(f32[1,2,256,128]{3,2,1,0:T(8,128)} %get-tuple-element.69), channel_id=1, source_target_pairs={{0,2},{1,3},{2,0},{3,1},{4,6},{5,7},{6,4},{7,5},{8,10},{9,11},{10,... | collective-permute-start | bytes 786440 | tf_op jit(solution)/shard_map/ppermute | solution.py:407
  261.2 15.2 %collective-permute-start.14 = (f32[1,2,256,128]{3,2,1,0:T(8,128)}, f32[1,2,256,128]{3,2,1,0:T(8,128)}, u32[]{:S(2)}, u32[]{:S(2)}) collective-permute-start(f32[1,2,256,128]{3,2,1,0:T(8,128)} %get-tuple-element.70), channel_id=1, source_target_pairs={{0,3},{1,2},{2,1},{3,0},{4,7},{5,6},{6,5},{7,4},{8,11},{9,10},{10,... | collective-permute-start | bytes 786440 | tf_op jit(solution)/shard_map/ppermute | solution.py:407
  271.3 1.2 copy-start.14
  272.6 0.9 copy-start.17
  276.5 9.3 %collective-permute-start.15 = (f32[1,2,256,128]{3,2,1,0:T(8,128)S(1)}, f32[1,2,256,128]{3,2,1,0:T(8,128)S(1)}, u32[]{:S(2)}, u32[]{:S(2)}) collective-permute-start(f32[1,2,256,128]{3,2,1,0:T(8,128)S(1)} %get-tuple-element.72), channel_id=1, source_target_pairs={{0,1},{1,0},{2,3},{3,2},{4,5},{5,4},{6,7},{7,6},{8,9},{9,8},{10,11... | collective-permute-start | bytes 786440 | tf_op jit(solution)/shard_map/ppermute | solution.py:407
  278.0 13.5 %collective-permute-start.16 = (f32[1,2,256,128]{3,2,1,0:T(8,128)S(1)}, f32[1,2,256,128]{3,2,1,0:T(8,128)S(1)}, u32[]{:S(2)}, u32[]{:S(2)}) collective-permute-start(f32[1,2,256,128]{3,2,1,0:T(8,128)S(1)} %get-tuple-element.73), channel_id=1, source_target_pairs={{0,2},{1,3},{2,0},{3,1},{4,6},{5,7},{6,4},{7,5},{8,10},{9,11},{10,... | collective-permute-start | bytes 786440 | tf_op jit(solution)/shard_map/ppermute | solution.py:407
  278.6 13.0 %collective-permute-start.17 = (f32[1,2,256,128]{3,2,1,0:T(8,128)S(1)}, f32[1,2,256,128]{3,2,1,0:T(8,128)S(1)}, u32[]{:S(2)}, u32[]{:S(2)}) collective-permute-start(f32[1,2,256,128]{3,2,1,0:T(8,128)S(1)} %get-tuple-element.74), channel_id=1, source_target_pairs={{0,3},{1,2},{2,1},{3,0},{4,7},{5,6},{6,5},{7,4},{8,11},{9,10},{10,... | collective-permute-start | bytes 786440 | tf_op jit(solution)/shard_map/ppermute | solution.py:407
